TPU v7x, 32 devices: a whole 2x2x4 slice. The times are simulated.
32 devices in a mesh: expert: 8 (over z, x), tensor: 4 (over y, core).
Axes of the slice: x: 2, y: 2, z: 4, core: 2. Of those that a mesh axis runs over, the one named last changes fastest.
Arguments:
- tokens: bfloat16 [256, 4096], P('expert', 'tensor'), may hold values from -6 to 6
- cotangent: bfloat16 [256, 4096], P('expert', 'tensor'), may hold values from -6 to 6
- routing: int32 [256, 8], P('expert'), may hold values from 0 to 63, as said below
- gates: float32 [256, 8], P('expert'), may hold values from 0.1 to 0.4
- w_in: bfloat16 [64, 4096, 1536], P('expert', None, 'tensor'), may hold values from -0.09375 to 0.09375
- w_out: bfloat16 [64, 1536, 4096], P('expert', 'tensor'), may hold values from -0.15625 to 0.15625
Outputs:
- mixed: bfloat16 [256, 4096], P('expert', 'tensor')
- d_tokens: bfloat16 [256, 4096], P('expert', 'tensor')
- d_w_in: bfloat16 [64, 4096, 1536], P('expert', None, 'tensor')
- d_w_out: bfloat16 [64, 1536, 4096], P('expert', 'tensor')
Inputs may be any that keep to these rules, and one draw needn't show every extreme that they name: `routing`: each row names 8 different experts. In each aligned block of 32 rows (the tokens of one index of the expert axis) no expert is named by more than 8 rows, and one expert is named by exactly 8 rows of every block.
All inputs are finite; a program needn't handle non-finite values.
Results may differ from a plain program's by a relative error of at most 0.0058.
Values may be sent and summed in bfloat16 or wider, within the bound.
No kernel may reach another device: no remote copies, remote signals or barrier semaphores. Data moves between devices by JAX's collectives and lax.ppermute only.
A program may use at most 192 MiB of HBM per device.

v0:
```python
import jax
import jax.numpy as jnp
from jax import lax
from jax.sharding import PartitionSpec as P


def shards(tokens, cotangent, routing, gates, w_in, w_out):
    devices = lax.axis_size("expert")
    local_experts = w_in.shape[0]
    experts = devices * local_experts
    tok_rows = routing.shape[0]
    capacity = tok_rows // 4
    buffer_rows = experts * capacity
    highest = lax.Precision.HIGHEST
    matches = (routing[:, :, None] == jnp.arange(experts, dtype=jnp.int32)[None, None, :]).astype(
        jnp.int32
    )
    per_token = jnp.sum(matches, axis=1)
    earlier = jnp.cumsum(per_token, axis=0) - per_token
    destination = routing * capacity + jnp.take_along_axis(earlier, routing, axis=1)
    placed = (
        destination[:, :, None] == jnp.arange(buffer_rows, dtype=jnp.int32)[None, None, :]
    ).astype(jnp.float32)
    membership = jnp.sum(placed, axis=1)
    weighting = jnp.sum(placed * gates[:, :, None], axis=1)
    whole_tokens, whole_cot = (
        lax.all_gather(tokens, "tensor", axis=1, tiled=True),
        lax.all_gather(cotangent, "tensor", axis=1, tiled=True),
    )
    width = whole_tokens.shape[1]
    rows = jnp.einsum(
        "tr,td->rd",
        membership.astype(jnp.bfloat16),
        whole_tokens,
        preferred_element_type=jnp.float32,
    ).astype(jnp.bfloat16)
    scaled = jnp.einsum(
        "tr,td->rd", weighting, whole_cot.astype(jnp.float32), precision=highest
    ).astype(jnp.bfloat16)
    send_rows = rows.reshape(devices, local_experts, capacity, width)
    send_scaled = scaled.reshape(devices, local_experts, capacity, width)
    expert_rows, expert_scaled = (
        lax.all_to_all(send_rows, "expert", split_axis=0, concat_axis=0, tiled=True),
        lax.all_to_all(send_scaled, "expert", split_axis=0, concat_axis=0, tiled=True),
    )
    preact = jnp.einsum("nesd,edh->nesh", expert_rows, w_in, preferred_element_type=jnp.float32)
    sigmoid_val = jax.nn.sigmoid(preact)
    hidden = (preact * sigmoid_val).astype(jnp.bfloat16)
    out_part = jnp.einsum("nesh,ehd->nesd", hidden, w_out, preferred_element_type=jnp.float32)
    grad_hidden = jnp.einsum(
        "nesd,ehd->nesh", expert_scaled, w_out, preferred_element_type=jnp.float32
    )
    grad_preact = (grad_hidden * sigmoid_val * (1.0 + preact * (1.0 - sigmoid_val))).astype(
        jnp.bfloat16
    )
    d_w_out = jnp.einsum(
        "nesh,nesd->ehd", hidden, expert_scaled, preferred_element_type=jnp.float32
    ).astype(jnp.bfloat16)
    d_w_in = jnp.einsum(
        "nesd,nesh->edh", expert_rows, grad_preact, preferred_element_type=jnp.float32
    ).astype(jnp.bfloat16)
    grad_part = jnp.einsum("nesh,edh->nesd", grad_preact, w_in, preferred_element_type=jnp.float32)
    out_sums, grad_sums = (
        lax.psum_scatter(out_part, "tensor", scatter_dimension=3, tiled=True),
        lax.psum_scatter(grad_part, "tensor", scatter_dimension=3, tiled=True),
    )
    back_out, back_grad = (
        lax.all_to_all(out_sums, "expert", split_axis=0, concat_axis=0, tiled=True),
        lax.all_to_all(grad_sums, "expert", split_axis=0, concat_axis=0, tiled=True),
    )
    width_q = back_out.shape[3]
    mixed = jnp.einsum(
        "tr,rd->td", weighting, back_out.reshape(buffer_rows, width_q), precision=highest
    ).astype(jnp.bfloat16)
    d_tokens = jnp.einsum(
        "tr,rd->td", membership, back_grad.reshape(buffer_rows, width_q), precision=highest
    ).astype(jnp.bfloat16)
    return (mixed, d_tokens, d_w_in, d_w_out)


def solution(mesh):
    placed = (
        P("expert", "tensor"),
        P("expert", "tensor"),
        P("expert", None),
        P("expert", None),
        P("expert", None, "tensor"),
        P("expert", "tensor", None),
    )
    return jax.shard_map(
        shards,
        mesh=mesh,
        in_specs=placed,
        out_specs=(
            P("expert", "tensor"),
            P("expert", "tensor"),
            P("expert", None, "tensor"),
            P("expert", "tensor", None),
        ),
        check_vma=False,
    )
```

profile of v0, /device:TPU:0, one launch (start us, length us, event | category | flops | bytes accessed | tf_op | source)
XLA Modules:
  0.0 461.7 jit_solution(13349624298508323391)
XLA Ops:
  7.2 0.7 bitcast_or_fusion
  7.9 0.8 copy.49
  8.6 0.1 copy.50
  8.7 0.1 reshape.37
  8.8 0.8 copy.53
  9.6 0.1 convert_reduce_fusion.1
  9.7 0.1 reduce_window_sum.11
  9.7 0.0 copy-start.4
  9.7 0.0 copy-start.2
  9.8 1.9 gather_fusion
  11.7 0.1 reshape.40
  11.8 0.1 copy.51
  11.9 0.0 copy-done.4
  11.9 0.1 copy.52
  12.0 0.0 copy-done.2
  12.0 7.2 %all_gather.6 = bf16[32,4096]{1,0:T(8,128)(2,1)S(1)} all-gather(bf16[32,1024]{1,0:T(8,128)(2,1)S(1)} %copy-done.2), channel_id=1, replica_groups=mesh['expert'=8,'tensor'=4] {'tensor'}, dimensions={1}, use_global_device_ids=true | all-gather | bytes 327680 | tf_op jit(solution)/shard_map/all_gather | solution.py:27
  19.2 0.4 convert_reduce_fusion
  19.6 0.0 copy-start
  19.6 3.3 convolution_convert_fusion.1
  22.9 0.0 copy-done
  22.9 5.9 %all-to-all-start = ((bf16[8,8,8,4096]{3,2,1,0:T(8,128)(2,1)}), bf16[8,8,8,4096]{3,2,1,0:T(8,128)(2,1)}, u32[]{:S(2)}, u32[]{:S(2)}) async-start(bf16[8,8,8,4096]{3,2,1,0:T(8,128)(2,1)} %bitcast.65), calls=%async_computation | async-start | bytes 8388608 | tf_op jit(solution)/shard_map/all_to_all | solution.py:43
  28.8 0.0 copy-done.3
  28.8 5.8 %all_gather.7 = bf16[32,4096]{1,0:T(8,128)(2,1)S(1)} all-gather(bf16[32,1024]{1,0:T(8,128)(2,1)S(1)} %copy-done.3), channel_id=1, replica_groups=mesh['expert'=8,'tensor'=4] {'tensor'}, dimensions={1}, use_global_device_ids=true | all-gather | bytes 327680 | tf_op jit(solution)/shard_map/all_gather | solution.py:28
  34.6 5.0 %convolution_convert_fusion = bf16[512,4096]{1,0:T(8,128)(2,1)} fusion(f32[32,512]{1,0:T(8,128)S(1)} %get-tuple-element.5, bf16[32,4096]{1,0:T(8,128)(2,1)S(1)} %all_gather.7), kind=kOutput, calls=%fused_computation.13 | convolution fusion | flops 807403520 | bytes 4521984 | tf_op jit(solution)/shard_map/tr,td->rd/dot_general | solution.py:37
  39.6 83.0 %all-to-all-done = bf16[8,8,8,4096]{3,2,1,0:T(8,128)(2,1)} async-done(((bf16[8,8,8,4096]{3,2,1,0:T(8,128)(2,1)}), bf16[8,8,8,4096]{3,2,1,0:T(8,128)(2,1)}, u32[]{:S(2)}, u32[]{:S(2)}) %all-to-all-start) | async-done | bytes 4194336 | tf_op jit(solution)/shard_map/all_to_all | solution.py:43
  122.6 4.5 all-to-all-start.2
  127.2 0.2 reduce-scatter.5.cloned.1.call-start
  127.4 13.3 %fusion.22 = f32[8,8,8,384]{3,2,0,1:T(8,128)S(1)} fusion(bf16[8,4096,384]{2,1,0:T(8,128)(2,1)} %param.10, bf16[8,8,8,4096]{3,2,1,0:T(8,128)(2,1)} %all-to-all-done), kind=kOutput, calls=%fused_computation.19 | convolution fusion | flops 1610612736 | bytes 30146560 | tf_op jit(solution)/shard_map/nesd,edh->nesh/dot_general | solution.py:46
  140.7 79.3 %all-to-all-done.2 = bf16[8,8,8,4096]{3,2,1,0:T(8,128)(2,1)} async-done(((bf16[8,8,8,4096]{3,2,1,0:T(8,128)(2,1)}), bf16[8,8,8,4096]{3,2,1,0:T(8,128)(2,1)}, u32[]{:S(2)}, u32[]{:S(2)}) %all-to-all-start.2) | async-done | bytes 4194336 | tf_op jit(solution)/shard_map/all_to_all | solution.py:44
  220.0 13.6 %fusion.37 = bf16[8,8,8,384]{3,2,0,1:T(8,128)(2,1)S(1)} fusion(bf16[8,384,4096]{2,1,0:T(8,128)(2,1)} %param.11, bf16[8,8,8,4096]{3,2,1,0:T(8,128)(2,1)} %all-to-all-done.2, f32[8,8,8,384]{3,2,0,1:T(8,128)S(1)} %fusion.22), kind=kOutput, calls=%fused_computation.22 | convolution fusion | flops 1612382208 | bytes 30539776 | tf_op jit(solution)/shard_map/nesd,ehd->nesh/dot_general | solution.py:50
  233.6 14.7 %fusion.11 = f32[8,8,8,4096]{3,2,0,1:T(8,128)} fusion(bf16[8,8,8,384]{3,2,0,1:T(8,128)(2,1)S(1)} %fusion.37, bf16[8,4096,384]{2,1,0:T(8,128)(2,1)} %param.10), kind=kOutput, calls=%fused_computation.12 | convolution fusion | flops 1610612736 | bytes 33947648 | tf_op jit(solution)/shard_map/nesh,edh->nesd/dot_general | solution.py:62
  248.3 0.0 reduce-scatter.5.cloned.1.call-update
  248.3 0.3 reduce-scatter.3.cloned.1.call-start
  248.6 18.4 %fusion.8 = f32[8,8,8,4096]{3,2,0,1:T(8,128)} fusion(bf16[8,384,4096]{2,1,0:T(8,128)(2,1)} %param.11, f32[8,8,8,384]{3,2,0,1:T(8,128)S(1)} %fusion.22), kind=kOutput, calls=%fused_computation.11 | convolution fusion | flops 1611595776 | bytes 34340864 | tf_op jit(solution)/shard_map/nesh,ehd->nesd/dot_general | solution.py:49
  267.0 0.0 reduce-scatter.3.cloned.1.call-update
  267.1 52.2 %reduce-scatter.5.cloned.1.call-done = f32[8,8,8,1024]{3,2,0,1:T(8,128)} async-done(((f32[8,8,8,4096]{3,2,0,1:T(8,128)}), f32[8,8,8,1024]{3,2,0,1:T(8,128)}) %reduce-scatter.5.cloned.1.call-update) | async-done | bytes 2097168 | tf_op jit(solution)/shard_map/reduce_scatter | solution.py:65
  319.3 3.1 copy.57
  322.4 5.5 %all-to-all-start.3 = ((f32[8,8,8,1024]{3,2,1,0:T(8,128)}), f32[8,8,8,1024]{3,2,1,0:T(8,128)S(1)}, u32[]{:S(2)}, u32[]{:S(2)}) async-start(f32[8,8,8,1024]{3,2,1,0:T(8,128)} %copy.57), calls=%async_computation.5 | async-start | bytes 4194304 | tf_op jit(solution)/shard_map/all_to_all | solution.py:69
  327.9 15.5 %bitcast_convert_fusion.1 = bf16[8,4096,384]{2,1,0:T(8,128)(2,1)} fusion(bf16[8,8,8,4096]{3,2,1,0:T(8,128)(2,1)} %all-to-all-done, bf16[8,8,8,384]{3,2,0,1:T(8,128)(2,1)S(1)} %fusion.37), kind=kOutput, calls=%fused_computation.2 | convolution fusion | flops 1623195648 | bytes 29753344 | tf_op jit(solution)/shard_map/nesd,nesh->edh/dot_general | solution.py:59
  343.4 50.9 %reduce-scatter.3.cloned.1.call-done = f32[8,8,8,1024]{3,2,0,1:T(8,128)} async-done(((f32[8,8,8,4096]{3,2,0,1:T(8,128)}), f32[8,8,8,1024]{3,2,0,1:T(8,128)}) %reduce-scatter.3.cloned.1.call-update) | async-done | bytes 2097168 | tf_op jit(solution)/shard_map/reduce_scatter | solution.py:64
  394.3 3.2 copy.55
  397.5 0.0 all-to-all-done.3
  397.5 5.5 %all-to-all-start.1 = ((f32[8,8,8,1024]{3,2,1,0:T(8,128)}), f32[8,8,8,1024]{3,2,1,0:T(8,128)}, u32[]{:S(2)}, u32[]{:S(2)}) async-start(f32[8,8,8,1024]{3,2,1,0:T(8,128)} %copy.55), calls=%async_computation.2 | async-start | bytes 4194304 | tf_op jit(solution)/shard_map/all_to_all | solution.py:68
  403.0 13.8 %bitcast_convert_fusion = bf16[8,384,4096]{2,1,0:T(8,128)(2,1)} fusion(bf16[8,8,8,4096]{3,2,1,0:T(8,128)(2,1)} %all-to-all-done.2, f32[8,8,8,384]{3,2,0,1:T(8,128)S(1)} %fusion.22), kind=kOutput, calls=%fused_computation.1 | convolution fusion | flops 1624178688 | bytes 30146560 | tf_op jit(solution)/shard_map/nesh,nesd->ehd/dot_general | solution.py:56
  416.8 0.0 copy-done.1
  416.8 1.9 convolution_convert_fusion.2
  418.8 32.6 %all-to-all-done.1 = f32[8,8,8,1024]{3,2,1,0:T(8,128)} async-done(((f32[8,8,8,1024]{3,2,1,0:T(8,128)}), f32[8,8,8,1024]{3,2,1,0:T(8,128)}, u32[]{:S(2)}, u32[]{:S(2)}) %all-to-all-start.1) | async-done | bytes 2097184 | tf_op jit(solution)/shard_map/all_to_all | solution.py:68
  451.4 3.5 convolution_convert_fusion.3
  (4 shorter events, 0.0 us)
Async XLA Ops:
  9.7 2.1 copy-start.4
  9.7 2.2 copy-start.2
  19.6 3.3 copy-start
  22.9 6.0 %copy-start.3 = (bf16[32,1024]{1,0:T(8,128)(2,1)S(1)}, bf16[32,1024]{1,0:T(8,128)(2,1)}, u32[]{:S(2)}) copy-start(bf16[32,1024]{1,0:T(8,128)(2,1)} %param.7) | copy-start | bytes 196612
  22.9 99.7 %all-to-all-start = ((bf16[8,8,8,4096]{3,2,1,0:T(8,128)(2,1)}), bf16[8,8,8,4096]{3,2,1,0:T(8,128)(2,1)}, u32[]{:S(2)}, u32[]{:S(2)}) async-start(bf16[8,8,8,4096]{3,2,1,0:T(8,128)(2,1)} %bitcast.65), calls=%async_computation | async-start | bytes 8388608 | tf_op jit(solution)/shard_map/all_to_all | solution.py:43
  122.6 97.4 %all-to-all-start.2 = ((bf16[8,8,8,4096]{3,2,1,0:T(8,128)(2,1)}), bf16[8,8,8,4096]{3,2,1,0:T(8,128)(2,1)}, u32[]{:S(2)}, u32[]{:S(2)}) async-start(bf16[8,8,8,4096]{3,2,1,0:T(8,128)(2,1)} %bitcast.64), calls=%async_computation.3 | async-start | bytes 8388608 | tf_op jit(solution)/shard_map/all_to_all | solution.py:44
  127.2 192.1 %reduce-scatter.5.cloned.1.call-start = ((), (), s32[]{:S(2)}) async-start(), calls=%async_computation.7 | async-start | bytes 10485760 | tf_op jit(solution)/shard_map/reduce_scatter | solution.py:65
  248.3 146.0 %reduce-scatter.3.cloned.1.call-start = ((), (), s32[]{:S(2)}) async-start(), calls=%async_computation.6 | async-start | bytes 10485760 | tf_op jit(solution)/shard_map/reduce_scatter | solution.py:64
  322.4 75.1 %all-to-all-start.3 = ((f32[8,8,8,1024]{3,2,1,0:T(8,128)}), f32[8,8,8,1024]{3,2,1,0:T(8,128)S(1)}, u32[]{:S(2)}, u32[]{:S(2)}) async-start(f32[8,8,8,1024]{3,2,1,0:T(8,128)} %copy.57), calls=%async_computation.5 | async-start | bytes 4194304 | tf_op jit(solution)/shard_map/all_to_all | solution.py:69
  397.5 53.9 %all-to-all-start.1 = ((f32[8,8,8,1024]{3,2,1,0:T(8,128)}), f32[8,8,8,1024]{3,2,1,0:T(8,128)}, u32[]{:S(2)}, u32[]{:S(2)}) async-start(f32[8,8,8,1024]{3,2,1,0:T(8,128)} %copy.55), calls=%async_computation.2 | async-start | bytes 4194304 | tf_op jit(solution)/shard_map/all_to_all | solution.py:68
  403.0 13.8 %copy-start.1 = (f32[32,512]{1,0:T(8,128)S(1)}, f32[32,512]{1,0:T(8,128)}, u32[]{:S(2)}) copy-start(f32[32,512]{1,0:T(8,128)} %copy-done) | copy-start | bytes 196612
Sparse Core Ops, SparseCore 0:
  248.5 70.7 reduce-scatter.4
  322.6 71.6 reduce-scatter.2
where the time goes:
time: 462 us
  waiting for transfers between devices  298 us (65%)
  matrix products  103 us (22%)
  starting transfers between devices  22 us (5%)
  between operations  14.1 us (3%)
  blocking collectives  13 us (3%)
  local copies, waits for them, and re-layouts  10.2 us (2%)
    all_to_all x1, waiting for transfers between devices, shards(): lax.all_to_all(send_rows, 'expert', split_axis=0, concat_axis=0, tiled=True)  83 us
    all_to_all x1, waiting for transfers between devices, shards(): lax.all_to_all(send_scaled, 'expert', split_axis=0, concat_axis=0, tiled=...  79.3 us
    reduce_scatter x1, waiting for transfers between devices, shards(): lax.psum_scatter(grad_part, 'tensor', scatter_dimension=3, tiled=True)  52.2 us
    reduce_scatter x1, waiting for transfers between devices, shards(): lax.psum_scatter(out_part, 'tensor', scatter_dimension=3, tiled=True)  50.9 us
    all_to_all x1, waiting for transfers between devices, shards(): lax.all_to_all(out_sums, 'expert', split_axis=0, concat_axis=0, tiled=True)  32.6 us
    dot_general x1, matrix products, shards(): jnp.einsum('nesh,ehd->nesd', hidden, w_out, preferred_element_type=jnp.fl...  18.4 us
    dot_general x1, matrix products, shards(): jnp.einsum('nesd,nesh->edh', expert_rows, grad_preact, preferred_element_...  15.5 us
    dot_general x1, matrix products, shards(): jnp.einsum('nesh,edh->nesd', grad_preact, w_in, preferred_element_type=jn...  14.7 us
  transfers between devices with their start and end apart: 6, of which 5 were waited for; matrix products, arithmetic and copies ran while one was open for 16% of the time, Pallas kernels for 0%

commit v1 on v0

v1 whole, which is shorter than its diff:
```python
import functools

import jax
import jax.numpy as jnp
from jax import lax
from jax.experimental import pallas as pl
from jax.experimental.pallas import tpu as pltpu
from jax.sharding import PartitionSpec as P

MIB = 1024 * 1024
LIMIT = 40 * MIB
DIRECT = 8
F32 = jnp.float32
BF16 = jnp.bfloat16


def swap(value, axis, bits):
    size = lax.axis_size(axis)
    return lax.ppermute(value, axis, [(i, i ^ bits) for i in range(size)])


def gather_rows(value):
    size = lax.axis_size("expert")
    if size > DIRECT:
        return lax.all_gather(value, "expert", axis=0, tiled=True)
    return jnp.concatenate([value] + [swap(value, "expert", s) for s in range(1, size)], axis=0)


def scatter_rows(value, rows):
    size = lax.axis_size("expert")
    if size > DIRECT:
        return lax.psum_scatter(value.astype(F32), "expert", scatter_dimension=0, tiled=True)
    total = value[:rows].astype(F32)
    for s in range(1, size):
        total = total + swap(value[s * rows : (s + 1) * rows], "expert", s).astype(F32)
    return total


def gather_chunks(value):
    chunks = {0: value}
    bit = lax.axis_size("tensor") // 2
    while bit:
        chunks.update({s | bit: swap(c, "tensor", bit) for s, c in list(chunks.items())})
        bit //= 2
    return [chunks[s] for s in range(len(chunks))]


def scatter_chunks(even, odd):
    size = lax.axis_size("tensor")
    got = swap(odd, "tensor", 1)
    parts = [even[i].astype(F32) + got[i].astype(F32) for i in range(size // 2)]
    bit = 2
    while bit < size:
        kept = []
        for i in range(len(parts) // 2):
            sent = parts[2 * i + 1].astype(BF16)
            kept.append(parts[2 * i] + swap(sent, "tensor", bit).astype(F32))
        parts = kept
        bit *= 2
    return parts[0].astype(BF16)


def column(gates, index):
    lane = lax.broadcasted_iota(jnp.int32, gates.shape, 1)
    return jnp.sum(jnp.where(lane == index, gates, 0.0), axis=1, keepdims=True)


def place(me_ref, s, width):
    return pl.ds(pl.multiple_of((me_ref[0] ^ s) * width, width), width)


def dot(a, b, dims=((1,), (0,))):
    return lax.dot_general(a, b, (dims, ((), ())), preferred_element_type=F32)


def preact_kernel(n, me_ref, gates_ref, *refs):
    xs, (w_ref, act_ref, slope_ref) = refs[:n], refs[n:]
    width = xs[0].shape[1]
    pre = sum(dot(xs[s][...], w_ref[0, place(me_ref, s, width), :]) for s in range(n))
    sig = jax.nn.sigmoid(pre)
    gate = column(gates_ref[...], pl.program_id(0))
    act_ref[...] = (gate * (pre * sig)).astype(BF16)
    slope_ref[...] = gate * (sig * (1.0 + pre * (1.0 - sig)))


def slope_kernel(n, me_ref, slope_ref, *refs):
    ys, (w_ref, grad_ref) = refs[:n], refs[n:]
    width = ys[0].shape[1]
    grad = sum(
        dot(ys[s][...], w_ref[:, place(me_ref, s, width)], ((1,), (1,))) for s in range(n)
    )
    grad_ref[...] = (grad * slope_ref[...]).astype(BF16)


def mix_kernel(me_ref, act_ref, w_ref, out_ref):
    out_ref[0] = dot(act_ref[...], w_ref[...]).astype(BF16)


def back_kernel(me_ref, grad_ref, w_ref, out_ref):
    hid = w_ref.shape[2]
    total = sum(
        dot(grad_ref[:, e * hid : (e + 1) * hid], w_ref[e], ((1,), (1,)))
        for e in range(w_ref.shape[0])
    )
    out_ref[0] = total.astype(BF16)


def d_out_kernel(n, me_ref, act_ref, *refs):
    ys, out_ref = refs[:n], refs[n]
    width = ys[0].shape[1]
    act = act_ref[...].T
    for s in range(n):
        out_ref[:, place(me_ref, s, width)] = dot(act, ys[s][...]).astype(BF16)


def d_in_kernel(n, me_ref, grad_ref, *refs):
    xs, out_ref = refs[:n], refs[n]
    width = xs[0].shape[0]
    grad = grad_ref[...]
    for s in range(n):
        out_ref[0, place(me_ref, s, width), :] = dot(xs[s][...], grad).astype(BF16)


def call(kernel, name, grid, in_specs, out_specs, out_shape, args, flops):
    moved = sum(a.size * a.dtype.itemsize for a in args)
    moved += sum(o.size * o.dtype.itemsize for o in jax.tree.leaves(out_shape))
    return pl.pallas_call(
        kernel,
        grid_spec=pltpu.PrefetchScalarGridSpec(
            num_scalar_prefetch=1, grid=grid, in_specs=in_specs, out_specs=out_specs
        ),
        out_shape=out_shape,
        name=name,
        cost_estimate=pl.CostEstimate(flops=flops, bytes_accessed=moved, transcendentals=0),
        compiler_params=pltpu.CompilerParams(vmem_limit_bytes=LIMIT),
    )(*args)


def once(shape, index):
    return pl.BlockSpec(shape, index, pipeline_mode=pl.Buffered(1))


def shards(tokens, cotangent, routing, gates, w_in, w_out):
    n = lax.axis_size("tensor")
    local, width, hid = w_in.shape
    rows, quarter = tokens.shape
    me = lax.axis_index("tensor").astype(jnp.int32).reshape(1)

    routed = jnp.concatenate([routing.astype(F32), gates], axis=1)
    own_x = gather_rows(tokens)
    routed = gather_rows(routed)
    xs = gather_chunks(own_x)
    own_y = gather_rows(cotangent)
    ys = gather_chunks(own_y)
    total = own_x.shape[0]
    top = routing.shape[1]
    first = lax.axis_index("expert") * local
    experts = (first + jnp.arange(local, dtype=jnp.int32)).astype(F32)
    match = routed[:, :top, None] == experts[None, None, :]
    gate = jnp.sum(jnp.where(match, routed[:, top:, None], 0.0), axis=1)

    tile = min(total, 256)
    tiles = total // tile
    cols = min(512, quarter)
    per = quarter // cols
    flat_out = w_out.reshape(local * hid, width)
    flops = 2 * total * local * hid * width
    flat = jax.ShapeDtypeStruct((total, local * hid), BF16)

    x_specs = [once((tile, quarter), lambda e, t, me: (t, 0))] * n
    act, slope = call(
        functools.partial(preact_kernel, n),
        "preact",
        (local, tiles),
        [pl.BlockSpec((tile, local), lambda e, t, me: (t, 0))]
        + x_specs
        + [pl.BlockSpec((1, width, hid), lambda e, t, me: (e, 0, 0))],
        [pl.BlockSpec((tile, hid), lambda e, t, me: (t, e))] * 2,
        [flat, jax.ShapeDtypeStruct(flat.shape, F32)],
        (me, gate, *xs, w_in),
        flops,
    )

    def parts(kernel, name, left, weights, odd):
        is_out = weights.ndim == 2

        def w_index(i, j, t, me):
            block = (me[0] ^ (2 * i + odd)) * per + j
            return (0, block) if is_out else (0, block, 0)

        w_block = (local * hid, cols) if is_out else (local, cols, hid)
        return call(
            kernel,
            name,
            (n // 2, per, tiles),
            [
                pl.BlockSpec((tile, local * hid), lambda i, j, t, me: (t, 0)),
                pl.BlockSpec(w_block, w_index),
            ],
            pl.BlockSpec((1, tile, cols), lambda i, j, t, me: (i, t, j)),
            jax.ShapeDtypeStruct((n // 2, total, quarter), BF16),
            (me, left, weights),
            flops // 2,
        )

    mix_odd = parts(mix_kernel, "mix_odd", act, flat_out, 1)
    mix_even = parts(mix_kernel, "mix_even", act, flat_out, 0)
    mixed = scatter_rows(scatter_chunks(mix_even, mix_odd), rows).astype(BF16)

    grad = call(
        functools.partial(slope_kernel, n),
        "grad_preact",
        (local, tiles),
        [pl.BlockSpec((tile, hid), lambda e, t, me: (t, e))]
        + x_specs
        + [pl.BlockSpec((hid, width), lambda e, t, me: (e, 0))],
        pl.BlockSpec((tile, hid), lambda e, t, me: (t, e)),
        flat,
        (me, slope, *ys, flat_out),
        flops,
    )

    back_odd = parts(back_kernel, "back_odd", grad, w_in, 1)
    back_even = parts(back_kernel, "back_even", grad, w_in, 0)
    d_tokens = scatter_rows(scatter_chunks(back_even, back_odd), rows).astype(BF16)

    d_w_out = call(
        functools.partial(d_out_kernel, n),
        "d_w_out",
        (local,),
        [pl.BlockSpec((total, hid), lambda e, me: (0, e))]
        + [once((total, quarter), lambda e, me: (0, 0))] * n,
        pl.BlockSpec((hid, width), lambda e, me: (e, 0)),
        jax.ShapeDtypeStruct((local * hid, width), BF16),
        (me, act, *ys),
        flops,
    ).reshape(w_out.shape)
    d_w_in = call(
        functools.partial(d_in_kernel, n),
        "d_w_in",
        (local,),
        [pl.BlockSpec((total, hid), lambda e, me: (0, e))]
        + [once((quarter, total), lambda e, me: (0, 0))] * n,
        pl.BlockSpec((1, width, hid), lambda e, me: (e, 0, 0)),
        jax.ShapeDtypeStruct(w_in.shape, BF16),
        (me, grad, *[x.T for x in xs]),
        flops,
    )
    return mixed, d_tokens, d_w_in, d_w_out


def solution(mesh):
    rows = P("expert", "tensor")
    routes = P("expert", None)
    columns_in = P("expert", None, "tensor")
    rows_out = P("expert", "tensor", None)
    return jax.shard_map(
        shards,
        mesh=mesh,
        in_specs=(rows, rows, routes, routes, columns_in, rows_out),
        out_specs=(rows, rows, columns_in, rows_out),
        check_vma=False,
    )
```

time: 462 us -> 236 us (0.51)
  waiting for transfers between devices: 298 us -> 44.8 us
  matrix products: 103 us -> 0 us
  Pallas kernels: 0 us -> 85.5 us
  starting transfers between devices: 22 us -> 84.2 us
  between operations: 14.1 us -> 0.92 us
  blocking collectives: 13 us -> 0 us
  local copies, waits for them, and re-layouts: 10.2 us -> 16 us
    all_to_all x4 -> x0, waiting for transfers between devices: 195 us -> none  [the longest x1 83 us: shards(): lax.all_to_all(send_rows, 'expert', split_axis=0, concat_axis=0, tiled=True)]
    reduce_scatter x2 -> x0, waiting for transfers between devices: 103 us -> none  [the longest x1 52.2 us: shards(): lax.psum_scatter(grad_part, 'tensor', scatter_dimension=3, tiled=True)]
    dot_general x10 -> x0, matrix products: 103 us -> none  [the longest x1 18.4 us: shards(): jnp.einsum('nesh,ehd->nesd', hidden, w_out, preferred_element_type=jnp.fl...]
    pallas_call x0 -> x8, Pallas kernels: none -> 85.5 us  [call(): pl.pallas_call(kernel, grid_spec=pltpu.PrefetchScalarGridSpec(num_scalar_...]
    ppermute x0 -> x45, starting transfers between devices: none -> 84.2 us  [swap(): return lax.ppermute(value, axis, [(i, i ^ bits) for i in range(size)])]
    ppermute x0 -> x45, waiting for transfers between devices: none -> 44.8 us  [swap(): return lax.ppermute(value, axis, [(i, i ^ bits) for i in range(size)])]
    all_to_all x4 -> x0, starting transfers between devices: 21.5 us -> none  [the longest x1 5.95 us: shards(): lax.all_to_all(send_rows, 'expert', split_axis=0, concat_axis=0, tiled=True)]
    all_gather x2 -> x0, blocking collectives: 13 us -> none  [the longest x1 7.22 us: shards(): lax.all_gather(tokens, 'tensor', axis=1, tiled=True)]
  transfers between devices with their start and end apart: 6 -> 45, of which waited for: 5 -> 17; matrix products, arithmetic and copies ran while one was open for 16% -> 6% of each run, Pallas kernels for 0% -> 36%
where the time goes in v1:
time: 236 us; the launch traced here: 235 us
  Pallas kernels  85.5 us (36%)
  starting transfers between devices  84.2 us (36%)
  waiting for transfers between devices  44.8 us (19%)
  local copies, waits for them, and re-layouts  16 us (7%)
  other arithmetic  3.79 us (2%)
    pallas_call x8, Pallas kernels, call(): pl.pallas_call(kernel, grid_spec=pltpu.PrefetchScalarGridSpec(num_scalar_...  85.5 us
    ppermute x45, starting transfers between devices, swap(): return lax.ppermute(value, axis, [(i, i ^ bits) for i in range(size)])  84.2 us
    ppermute x45, waiting for transfers between devices, swap(): return lax.ppermute(value, axis, [(i, i ^ bits) for i in range(size)])  44.8 us
    unnamed x16, local copies, waits for them, and re-layouts  6.08 us
    ppermute x3, local copies, waits for them, and re-layouts, swap(): return lax.ppermute(value, axis, [(i, i ^ bits) for i in range(size)])  5.12 us
  transfers between devices with their start and end apart: 45, of which 17 were waited for; matrix products, arithmetic and copies ran while one was open for 6% of the time, Pallas kernels for 36%

profile of v1, /device:TPU:0, one launch (start us, length us, event | category | flops | bytes accessed | tf_op | source)
XLA Modules:
  0.0 235.2 jit_solution(4375701488077378278)
XLA Ops:
  1.6 6.0 %collective-permute-start.13 = (bf16[32,1024]{0,1:T(8,128)(2,1)S(1)}, bf16[32,1024]{0,1:T(8,128)(2,1)S(1)}, u32[]{:S(2)}, u32[]{:S(2)}) collective-permute-start(bf16[32,1024]{0,1:T(8,128)(2,1)S(1)} %copy.31), channel_id=1, source_target_pairs={{0,28},{4,24},{8,20},{12,16},{16,12},{20,8},{24,4},{28,0},{1,29},{... | collective-permute-start | bytes 196616 | tf_op jit(solution)/shard_map/ppermute | solution.py:19
  8.7 2.0 collective-permute-start.10
  10.7 2.3 collective-permute-start.9
  13.7 1.4 collective-permute-done.13
  15.0 24.5 %collective-permute-start.8 = (bf16[32,1024]{0,1:T(8,128)(2,1)S(1)}, bf16[32,1024]{0,1:T(8,128)(2,1)S(1)}, u32[]{:S(2)}, u32[]{:S(2)}) collective-permute-start(bf16[32,1024]{0,1:T(8,128)(2,1)S(1)} %copy.31), channel_id=1, source_target_pairs={{0,8},{4,12},{8,0},{12,4},{16,24},{20,28},{24,16},{28,20},{1,9},{5... | collective-permute-start | bytes 196616 | tf_op jit(solution)/shard_map/ppermute | solution.py:19
  39.5 1.4 collective-permute-start.7
  40.9 8.4 %collective-permute-done.11 = bf16[32,1024]{0,1:T(8,128)(2,1)S(1)} collective-permute-done((bf16[32,1024]{0,1:T(8,128)(2,1)S(1)}, bf16[32,1024]{0,1:T(8,128)(2,1)S(1)}, u32[]{:S(2)}, u32[]{:S(2)}) %collective-permute-start.11) | collective-permute-done | bytes 65568 | tf_op jit(solution)/shard_map/ppermute | solution.py:19
  51.6 2.4 %collective-permute-done.10 = bf16[32,1024]{0,1:T(8,128)(2,1)S(1)} collective-permute-done((bf16[32,1024]{0,1:T(8,128)(2,1)S(1)}, bf16[32,1024]{0,1:T(8,128)(2,1)S(1)}, u32[]{:S(2)}, u32[]{:S(2)}) %collective-permute-start.10) | collective-permute-done | bytes 65568 | tf_op jit(solution)/shard_map/ppermute | solution.py:19
  54.0 2.1 collective-permute-start.31
  56.1 2.9 %collective-permute-start.29 = (bf16[32,1024]{1,0:T(8,128)(2,1)}, bf16[32,1024]{1,0:T(8,128)(2,1)S(1)}, u32[]{:S(2)}, u32[]{:S(2)}) collective-permute-start(bf16[32,1024]{1,0:T(8,128)(2,1)} %param.7), channel_id=1, source_target_pairs={{0,16},{4,20},{8,24},{12,28},{16,0},{20,4},{24,8},{28,12},{1,17},{... | collective-permute-start | bytes 196616 | tf_op jit(solution)/shard_map/ppermute | solution.py:19
  59.3 3.5 %concatenate.14 = bf16[256,1024]{0,1:T(8,128)(2,1)S(1)} concatenate(bf16[32,1024]{0,1:T(8,128)(2,1)S(1)} %copy.31, bf16[32,1024]{0,1:T(8,128)(2,1)S(1)} %collective-permute-done.7, bf16[32,1024]{0,1:T(8,128)(2,1)S(1)} %collective-permute-done.8, bf16[32,1024]{0,1:T(8,128)(2,1)S(1)} %collective-permute-done.9, bf16[32,1024]{0,1:T(8,128)(2,1)S(1)} %collective-permute-done.10, ...), dimensions={0} | concatenate | bytes 1048576 | tf_op jit(solution)/shard_map/concatenate | solution.py:26
  62.8 2.7 %collective-permute-start.27 = (bf16[32,1024]{1,0:T(8,128)(2,1)}, bf16[32,1024]{1,0:T(8,128)(2,1)S(1)}, u32[]{:S(2)}, u32[]{:S(2)}) collective-permute-start(bf16[32,1024]{1,0:T(8,128)(2,1)} %param.7), channel_id=1, source_target_pairs={{0,8},{4,12},{8,0},{12,4},{16,24},{20,28},{24,16},{28,20},{1,9},{5... | collective-permute-start | bytes 196616 | tf_op jit(solution)/shard_map/ppermute | solution.py:19
  65.6 2.5 %collective-permute-done.27 = bf16[32,1024]{1,0:T(8,128)(2,1)S(1)} collective-permute-done((bf16[32,1024]{1,0:T(8,128)(2,1)}, bf16[32,1024]{1,0:T(8,128)(2,1)S(1)}, u32[]{:S(2)}, u32[]{:S(2)}) %collective-permute-start.27) | collective-permute-done | bytes 65568 | tf_op jit(solution)/shard_map/ppermute | solution.py:19
  68.0 1.7 collective-permute-start.32
  69.7 1.6 collective-permute-start.15
  71.4 3.8 %collective-permute-done.32 = bf16[32,1024]{1,0:T(8,128)(2,1)S(1)} collective-permute-done((bf16[32,1024]{1,0:T(8,128)(2,1)}, bf16[32,1024]{1,0:T(8,128)(2,1)S(1)}, u32[]{:S(2)}, u32[]{:S(2)}) %collective-permute-start.32) | collective-permute-done | bytes 65568 | tf_op jit(solution)/shard_map/ppermute | solution.py:19
  75.3 1.5 collective-permute-start.34
  76.8 7.8 %collective-permute-done.15 = bf16[256,1024]{0,1:T(8,128)(2,1)S(1)} collective-permute-done((bf16[256,1024]{0,1:T(8,128)(2,1)S(1)}, bf16[256,1024]{0,1:T(8,128)(2,1)S(1)}, u32[]{:S(2)}, u32[]{:S(2)}) %collective-permute-start.15) | collective-permute-done | bytes 524320 | tf_op jit(solution)/shard_map/ppermute | solution.py:19
  85.3 3.0 %collective-permute-start.6 = (f32[32,16]{0,1:T(8,128)S(1)}, f32[32,16]{0,1:T(8,128)S(1)}, u32[]{:S(2)}, u32[]{:S(2)}) collective-permute-start(f32[32,16]{0,1:T(8,128)S(1)} %pad_maximum_fusion), channel_id=1, source_target_pairs={{0,28},{4,24},{8,20},{12,16},{16,12},{20,8},{24,4},{28,0},{1,29},{... | collective-permute-start | bytes 6152 | tf_op jit(solution)/shard_map/ppermute | solution.py:19
  88.4 1.7 collective-permute-start.5
  90.0 1.7 collective-permute-done.6
  93.8 1.7 collective-permute-start.3
  95.5 1.7 collective-permute-done.4
  98.4 1.7 collective-permute-start.1
  100.1 1.7 collective-permute-done.2
  101.7 1.4 collective-permute-start
  103.1 2.2 collective-permute-done
  108.2 2.0 copy.34.refs_1_
  110.3 2.1 copy.36.refs_3_
  116.5 14.9 %preact.1 = (bf16[256,3072]{1,0:T(8,128)(2,1)S(1)}, f32[256,3072]{1,0:T(8,128)S(1)}) custom-call(s32[1]{0:T(128)} %bitcast.me_ref, f32[256,8]{1,0:T(8,128)S(1)} %copy.32.gates_ref, bf16[256,1024]{1,0:T(8,128)(2,1)S(1)} %copy-done, bf16[256,1024]{1,0:T(8,128)(2,1)S(1)} %copy-done.2, bf16[256,1024]{1,0:T(8,128)(2,1)S(1)} %copy-done.1, ...), custom_call_target="tpu_custom_call" | custom-call | flops 6442450944 | bytes 31989764 | tf_op jit(solution)/shard_map/preact/pallas_call | solution.py:127
  131.4 7.1 %mix_odd.1 = bf16[2,256,1024]{2,1,0:T(8,128)(2,1)S(1)} custom-call(s32[1]{0:T(128)} %bitcast.me_ref, bf16[256,3072]{1,0:T(8,128)(2,1)S(1)} %get-tuple-element.6.act_ref, bf16[3072,4096]{1,0:T(8,128)(2,1)} %bitcast.21), custom_call_target="tpu_custom_call" | custom-call | flops 3221225472 | bytes 27787268 | tf_op jit(solution)/shard_map/mix_odd/pallas_call | solution.py:127
  138.6 14.5 %grad_preact.1.grad_ref = bf16[256,3072]{1,0:T(8,128)(2,1)S(1)} custom-call(s32[1]{0:T(128)} %bitcast.me_ref, f32[256,3072]{1,0:T(8,128)S(1)} %get-tuple-element.7.slope_ref, bf16[256,1024]{1,0:T(8,128)(2,1)S(1)} %constant_dynamic-update-slice_fusion.refs_0_, bf16[256,1024]{1,0:T(8,128)(2,1)S(1)} %collective-permute-done.33.refs_1_, ...), custom_call_target="tpu_custom_call" | custom-call | flops 6442450944 | bytes 31981572 | tf_op jit(solution)/shard_map/grad_preact/pallas_call | solution.py:127
  153.2 7.9 %back_odd.1 = bf16[2,256,1024]{2,1,0:T(8,128)(2,1)S(1)} custom-call(s32[1]{0:T(128)} %bitcast.me_ref, bf16[256,3072]{1,0:T(8,128)(2,1)S(1)} %grad_preact.1.grad_ref, bf16[8,4096,384]{2,1,0:T(8,128)(2,1)} %w_ref.3), custom_call_target="tpu_custom_call" | custom-call | flops 3221225472 | bytes 27787268 | tf_op jit(solution)/shard_map/back_odd/pallas_call | solution.py:127
  161.6 7.9 %back_even.1 = bf16[2,256,1024]{2,1,0:T(8,128)(2,1)S(1)} custom-call(s32[1]{0:T(128)} %bitcast.me_ref, bf16[256,3072]{1,0:T(8,128)(2,1)S(1)} %grad_preact.1.grad_ref, bf16[8,4096,384]{2,1,0:T(8,128)(2,1)} %w_ref.3), custom_call_target="tpu_custom_call" | custom-call | flops 3221225472 | bytes 27787268 | tf_op jit(solution)/shard_map/back_even/pallas_call | solution.py:127
  169.5 7.1 %mix_even.1 = bf16[2,256,1024]{2,1,0:T(8,128)(2,1)S(1)} custom-call(s32[1]{0:T(128)} %bitcast.me_ref, bf16[256,3072]{1,0:T(8,128)(2,1)S(1)} %get-tuple-element.6.act_ref, bf16[3072,4096]{1,0:T(8,128)(2,1)} %bitcast.23), custom_call_target="tpu_custom_call" | custom-call | flops 3221225472 | bytes 27787268 | tf_op jit(solution)/shard_map/mix_even/pallas_call | solution.py:127
  176.8 1.6 collective-permute-start.18
  179.2 14.2 %d_w_in.1 = bf16[8,4096,384]{2,1,0:T(8,128)(2,1)} custom-call(s32[1]{0:T(128)} %bitcast.me_ref, bf16[256,3072]{1,0:T(8,128)(2,1)S(1)} %grad_preact.1.grad_ref, bf16[1024,256]{1,0:T(8,128)(2,1)S(1)} %bitcast.19, bf16[1024,256]{1,0:T(8,128)(2,1)} %bitcast.7.refs_1_, bf16[1024,256]{1,0:T(8,128)(2,1)S(1)} %bitcast.20, bf16[1024,256]{1,0:T(8,128)(2,1)} %bitcast.9.refs_3_), custom_call_target="tpu_custom_call" | custom-call | flops 6442450944 | bytes 28835844 | tf_op jit(solution)/shard_map/d_w_in/pallas_call | solution.py:127
  193.7 1.5 collective-permute-start.19
  195.2 2.1 collective-permute-start.25
  197.4 1.7 collective-permute-start.24
  199.1 2.9 %collective-permute-done.37 = bf16[256,1024]{1,0:T(8,128)(2,1)S(1)} collective-permute-done((bf16[256,1024]{1,0:T(8,128)(2,1)S(1)}, bf16[256,1024]{1,0:T(8,128)(2,1)S(1)}, u32[]{:S(2)}, u32[]{:S(2)}) %collective-permute-start.37) | collective-permute-done | bytes 524320 | tf_op jit(solution)/shard_map/ppermute | solution.py:19
  203.2 2.8 %collective-permute-start.21 = (bf16[32,1024]{1,0:T(8,128)(2,1)S(1)}, bf16[32,1024]{1,0:T(8,128)(2,1)S(1)}, u32[]{:S(2)}, u32[]{:S(2)}) collective-permute-start(bf16[32,1024]{1,0:T(8,128)(2,1)S(1)} %get-tuple-element.20), channel_id=1, source_target_pairs={{0,12},{4,8},{8,4},{12,0},{16,28},{20,24},{24,20},{28,16},{1,13},{... | collective-permute-start | bytes 196616 | tf_op jit(solution)/shard_map/ppermute | solution.py:19
  208.0 2.0 collective-permute-start.44
  210.0 11.8 %d_w_out.1 = bf16[3072,4096]{1,0:T(8,128)(2,1)} custom-call(s32[1]{0:T(128)} %bitcast.me_ref, bf16[256,3072]{1,0:T(8,128)(2,1)S(1)} %get-tuple-element.6.act_ref, bf16[256,1024]{1,0:T(8,128)(2,1)S(1)} %constant_dynamic-update-slice_fusion.refs_0_, bf16[256,1024]{1,0:T(8,128)(2,1)S(1)} %collective-permute-done.33.refs_1_, ...), custom_call_target="tpu_custom_call" | custom-call | flops 6442450944 | bytes 28835844 | tf_op jit(solution)/shard_map/d_w_out/pallas_call | solution.py:127
  223.6 3.9 %collective-permute-start.41 = (bf16[32,1024]{1,0:T(8,128)(2,1)S(1)}, bf16[32,1024]{1,0:T(8,128)(2,1)S(1)}, u32[]{:S(2)}, u32[]{:S(2)}) collective-permute-start(bf16[32,1024]{1,0:T(8,128)(2,1)S(1)} %get-tuple-element.12), channel_id=1, source_target_pairs={{0,16},{4,20},{8,24},{12,28},{16,0},{20,4},{24,8},{28,12},{1,17},{... | collective-permute-start | bytes 196616 | tf_op jit(solution)/shard_map/ppermute | solution.py:19
  227.5 1.5 collective-permute-start.39
  229.7 2.3 collective-permute-done.42
  232.9 1.5 collective-permute-done.40
  (87 shorter events, 25.5 us)
Async XLA Ops:
  1.6 13.4 %collective-permute-start.13 = (bf16[32,1024]{0,1:T(8,128)(2,1)S(1)}, bf16[32,1024]{0,1:T(8,128)(2,1)S(1)}, u32[]{:S(2)}, u32[]{:S(2)}) collective-permute-start(bf16[32,1024]{0,1:T(8,128)(2,1)S(1)} %copy.31), channel_id=1, source_target_pairs={{0,28},{4,24},{8,20},{12,16},{16,12},{20,8},{24,4},{28,0},{1,29},{... | collective-permute-start | bytes 196616 | tf_op jit(solution)/shard_map/ppermute | solution.py:19
  7.7 31.9 %collective-permute-start.12 = (bf16[32,1024]{0,1:T(8,128)(2,1)S(1)}, bf16[32,1024]{0,1:T(8,128)(2,1)S(1)}, u32[]{:S(2)}, u32[]{:S(2)}) collective-permute-start(bf16[32,1024]{0,1:T(8,128)(2,1)S(1)} %copy.31), channel_id=1, source_target_pairs={{0,24},{4,28},{8,16},{12,20},{16,8},{20,12},{24,0},{28,4},{1,25},{... | collective-permute-start | bytes 196616 | tf_op jit(solution)/shard_map/ppermute | solution.py:19
  7.9 41.4 %collective-permute-start.11 = (bf16[32,1024]{0,1:T(8,128)(2,1)S(1)}, bf16[32,1024]{0,1:T(8,128)(2,1)S(1)}, u32[]{:S(2)}, u32[]{:S(2)}) collective-permute-start(bf16[32,1024]{0,1:T(8,128)(2,1)S(1)} %copy.31), channel_id=1, source_target_pairs={{0,20},{4,16},{8,28},{12,24},{16,4},{20,0},{24,12},{28,8},{1,21},{... | collective-permute-start | bytes 196616 | tf_op jit(solution)/shard_map/ppermute | solution.py:19
  8.7 45.3 %collective-permute-start.10 = (bf16[32,1024]{0,1:T(8,128)(2,1)S(1)}, bf16[32,1024]{0,1:T(8,128)(2,1)S(1)}, u32[]{:S(2)}, u32[]{:S(2)}) collective-permute-start(bf16[32,1024]{0,1:T(8,128)(2,1)S(1)} %copy.31), channel_id=1, source_target_pairs={{0,16},{4,20},{8,24},{12,28},{16,0},{20,4},{24,8},{28,12},{1,17},{... | collective-permute-start | bytes 196616 | tf_op jit(solution)/shard_map/ppermute | solution.py:19
  10.7 45.4 %collective-permute-start.9 = (bf16[32,1024]{0,1:T(8,128)(2,1)S(1)}, bf16[32,1024]{0,1:T(8,128)(2,1)S(1)}, u32[]{:S(2)}, u32[]{:S(2)}) collective-permute-start(bf16[32,1024]{0,1:T(8,128)(2,1)S(1)} %copy.31), channel_id=1, source_target_pairs={{0,12},{4,8},{8,4},{12,0},{16,28},{20,24},{24,20},{28,16},{1,13},{... | collective-permute-start | bytes 196616 | tf_op jit(solution)/shard_map/ppermute | solution.py:19
  15.0 41.1 %collective-permute-start.8 = (bf16[32,1024]{0,1:T(8,128)(2,1)S(1)}, bf16[32,1024]{0,1:T(8,128)(2,1)S(1)}, u32[]{:S(2)}, u32[]{:S(2)}) collective-permute-start(bf16[32,1024]{0,1:T(8,128)(2,1)S(1)} %copy.31), channel_id=1, source_target_pairs={{0,8},{4,12},{8,0},{12,4},{16,24},{20,28},{24,16},{28,20},{1,9},{5... | collective-permute-start | bytes 196616 | tf_op jit(solution)/shard_map/ppermute | solution.py:19
  39.5 19.5 %collective-permute-start.7 = (bf16[32,1024]{0,1:T(8,128)(2,1)S(1)}, bf16[32,1024]{0,1:T(8,128)(2,1)S(1)}, u32[]{:S(2)}, u32[]{:S(2)}) collective-permute-start(bf16[32,1024]{0,1:T(8,128)(2,1)S(1)} %copy.31), channel_id=1, source_target_pairs={{0,4},{4,0},{8,12},{12,8},{16,20},{20,16},{24,28},{28,24},{1,5},{5... | collective-permute-start | bytes 196616 | tf_op jit(solution)/shard_map/ppermute | solution.py:19
  49.4 13.5 %collective-permute-start.26 = (bf16[32,1024]{1,0:T(8,128)(2,1)}, bf16[32,1024]{1,0:T(8,128)(2,1)S(1)}, u32[]{:S(2)}, u32[]{:S(2)}) collective-permute-start(bf16[32,1024]{1,0:T(8,128)(2,1)} %param.7), channel_id=1, source_target_pairs={{0,4},{4,0},{8,12},{12,8},{16,20},{20,16},{24,28},{28,24},{1,5},{5... | collective-permute-start | bytes 196616 | tf_op jit(solution)/shard_map/ppermute | solution.py:19
  54.0 17.5 %collective-permute-start.31 = (bf16[32,1024]{1,0:T(8,128)(2,1)}, bf16[32,1024]{1,0:T(8,128)(2,1)S(1)}, u32[]{:S(2)}, u32[]{:S(2)}) collective-permute-start(bf16[32,1024]{1,0:T(8,128)(2,1)} %param.7), channel_id=1, source_target_pairs={{0,24},{4,28},{8,16},{12,20},{16,8},{20,12},{24,0},{28,4},{1,25},{... | collective-permute-start | bytes 196616 | tf_op jit(solution)/shard_map/ppermute | solution.py:19
  56.1 15.3 %collective-permute-start.30 = (bf16[32,1024]{1,0:T(8,128)(2,1)}, bf16[32,1024]{1,0:T(8,128)(2,1)S(1)}, u32[]{:S(2)}, u32[]{:S(2)}) collective-permute-start(bf16[32,1024]{1,0:T(8,128)(2,1)} %param.7), channel_id=1, source_target_pairs={{0,20},{4,16},{8,28},{12,24},{16,4},{20,0},{24,12},{28,8},{1,21},{... | collective-permute-start | bytes 196616 | tf_op jit(solution)/shard_map/ppermute | solution.py:19
  56.1 15.2 %collective-permute-start.29 = (bf16[32,1024]{1,0:T(8,128)(2,1)}, bf16[32,1024]{1,0:T(8,128)(2,1)S(1)}, u32[]{:S(2)}, u32[]{:S(2)}) collective-permute-start(bf16[32,1024]{1,0:T(8,128)(2,1)} %param.7), channel_id=1, source_target_pairs={{0,16},{4,20},{8,24},{12,28},{16,0},{20,4},{24,8},{28,12},{1,17},{... | collective-permute-start | bytes 196616 | tf_op jit(solution)/shard_map/ppermute | solution.py:19
  59.0 10.7 %collective-permute-start.28 = (bf16[32,1024]{1,0:T(8,128)(2,1)}, bf16[32,1024]{1,0:T(8,128)(2,1)S(1)}, u32[]{:S(2)}, u32[]{:S(2)}) collective-permute-start(bf16[32,1024]{1,0:T(8,128)(2,1)} %param.7), channel_id=1, source_target_pairs={{0,12},{4,8},{8,4},{12,0},{16,28},{20,24},{24,20},{28,16},{1,13},{... | collective-permute-start | bytes 196616 | tf_op jit(solution)/shard_map/ppermute | solution.py:19
  62.8 5.2 %collective-permute-start.27 = (bf16[32,1024]{1,0:T(8,128)(2,1)}, bf16[32,1024]{1,0:T(8,128)(2,1)S(1)}, u32[]{:S(2)}, u32[]{:S(2)}) collective-permute-start(bf16[32,1024]{1,0:T(8,128)(2,1)} %param.7), channel_id=1, source_target_pairs={{0,8},{4,12},{8,0},{12,4},{16,24},{20,28},{24,16},{28,20},{1,9},{5... | collective-permute-start | bytes 196616 | tf_op jit(solution)/shard_map/ppermute | solution.py:19
  68.0 7.3 %collective-permute-start.32 = (bf16[32,1024]{1,0:T(8,128)(2,1)}, bf16[32,1024]{1,0:T(8,128)(2,1)S(1)}, u32[]{:S(2)}, u32[]{:S(2)}) collective-permute-start(bf16[32,1024]{1,0:T(8,128)(2,1)} %param.7), channel_id=1, source_target_pairs={{0,28},{4,24},{8,20},{12,16},{16,12},{20,8},{24,4},{28,0},{1,29},{... | collective-permute-start | bytes 196616 | tf_op jit(solution)/shard_map/ppermute | solution.py:19
  69.7 14.9 %collective-permute-start.15 = (bf16[256,1024]{0,1:T(8,128)(2,1)S(1)}, bf16[256,1024]{0,1:T(8,128)(2,1)S(1)}, u32[]{:S(2)}, u32[]{:S(2)}) collective-permute-start(bf16[256,1024]{0,1:T(8,128)(2,1)S(1)} %concatenate.14), channel_id=1, source_target_pairs={{0,2},{1,3},{2,0},{3,1},{4,6},{5,7},{6,4},{7,5},{8,10},{9,11},{10,... | collective-permute-start | bytes 1572872 | tf_op jit(solution)/shard_map/ppermute | solution.py:19
  71.3 36.9 %collective-permute-start.14 = (bf16[256,1024]{0,1:T(8,128)(2,1)S(1)}, bf16[256,1024]{0,1:T(8,128)(2,1)}, u32[]{:S(2)}, u32[]{:S(2)}) collective-permute-start(bf16[256,1024]{0,1:T(8,128)(2,1)S(1)} %concatenate.14), channel_id=1, source_target_pairs={{0,1},{1,0},{2,3},{3,2},{4,5},{5,4},{6,7},{7,6},{8,9},{9,8},{10,11... | collective-permute-start | bytes 1572872 | tf_op jit(solution)/shard_map/ppermute | solution.py:19
  75.3 32.4 %collective-permute-start.34 = (bf16[256,1024]{1,0:T(8,128)(2,1)S(1)}, bf16[256,1024]{1,0:T(8,128)(2,1)S(1)}, u32[]{:S(2)}, u32[]{:S(2)}) collective-permute-start(bf16[256,1024]{1,0:T(8,128)(2,1)S(1)} %constant_dynamic-update-slice_fusion.refs_0_), channel_id=1, source_target_pairs={{0,2},{1,3},{2,0},{3,1},{4,6},{5,7},{6,4},{7,5},{8,10},{9,11},{10,... | collective-permute-start | bytes 1572872 | tf_op jit(solution)/shard_map/ppermute | solution.py:19
  84.7 25.6 %collective-permute-start.16 = (bf16[256,1024]{0,1:T(8,128)(2,1)S(1)}, bf16[256,1024]{0,1:T(8,128)(2,1)}, u32[]{:S(2)}, u32[]{:S(2)}) collective-permute-start(bf16[256,1024]{0,1:T(8,128)(2,1)S(1)} %collective-permute-done.15), channel_id=1, source_target_pairs={{0,1},{1,0},{2,3},{3,2},{4,5},{5,4},{6,7},{7,6},{8,9},{9,8},{10,11... | collective-permute-start | bytes 1572872 | tf_op jit(solution)/shard_map/ppermute | solution.py:19
  85.3 6.4 %collective-permute-start.6 = (f32[32,16]{0,1:T(8,128)S(1)}, f32[32,16]{0,1:T(8,128)S(1)}, u32[]{:S(2)}, u32[]{:S(2)}) collective-permute-start(f32[32,16]{0,1:T(8,128)S(1)} %pad_maximum_fusion), channel_id=1, source_target_pairs={{0,28},{4,24},{8,20},{12,16},{16,12},{20,8},{24,4},{28,0},{1,29},{... | collective-permute-start | bytes 6152 | tf_op jit(solution)/shard_map/ppermute | solution.py:19
  88.4 5.4 %collective-permute-start.5 = (f32[32,16]{0,1:T(8,128)S(1)}, f32[32,16]{0,1:T(8,128)S(1)}, u32[]{:S(2)}, u32[]{:S(2)}) collective-permute-start(f32[32,16]{0,1:T(8,128)S(1)} %pad_maximum_fusion), channel_id=1, source_target_pairs={{0,24},{4,28},{8,16},{12,20},{16,8},{20,12},{24,0},{28,4},{1,25},{... | collective-permute-start | bytes 6152 | tf_op jit(solution)/shard_map/ppermute | solution.py:19
  91.7 5.4 %collective-permute-start.4 = (f32[32,16]{0,1:T(8,128)S(1)}, f32[32,16]{0,1:T(8,128)S(1)}, u32[]{:S(2)}, u32[]{:S(2)}) collective-permute-start(f32[32,16]{0,1:T(8,128)S(1)} %pad_maximum_fusion), channel_id=1, source_target_pairs={{0,20},{4,16},{8,28},{12,24},{16,4},{20,0},{24,12},{28,8},{1,21},{... | collective-permute-start | bytes 6152 | tf_op jit(solution)/shard_map/ppermute | solution.py:19
  93.8 4.5 %collective-permute-start.3 = (f32[32,16]{0,1:T(8,128)S(1)}, f32[32,16]{0,1:T(8,128)S(1)}, u32[]{:S(2)}, u32[]{:S(2)}) collective-permute-start(f32[32,16]{0,1:T(8,128)S(1)} %pad_maximum_fusion), channel_id=1, source_target_pairs={{0,16},{4,20},{8,24},{12,28},{16,0},{20,4},{24,8},{28,12},{1,17},{... | collective-permute-start | bytes 6152 | tf_op jit(solution)/shard_map/ppermute | solution.py:19
  97.2 4.5 %collective-permute-start.2 = (f32[32,16]{0,1:T(8,128)S(1)}, f32[32,16]{0,1:T(8,128)S(1)}, u32[]{:S(2)}, u32[]{:S(2)}) collective-permute-start(f32[32,16]{0,1:T(8,128)S(1)} %pad_maximum_fusion), channel_id=1, source_target_pairs={{0,12},{4,8},{8,4},{12,0},{16,28},{20,24},{24,20},{28,16},{1,13},{... | collective-permute-start | bytes 6152 | tf_op jit(solution)/shard_map/ppermute | solution.py:19
  98.4 4.8 %collective-permute-start.1 = (f32[32,16]{0,1:T(8,128)S(1)}, f32[32,16]{0,1:T(8,128)S(1)}, u32[]{:S(2)}, u32[]{:S(2)}) collective-permute-start(f32[32,16]{0,1:T(8,128)S(1)} %pad_maximum_fusion), channel_id=1, source_target_pairs={{0,8},{4,12},{8,0},{12,4},{16,24},{20,28},{24,16},{28,20},{1,9},{5... | collective-permute-start | bytes 6152 | tf_op jit(solution)/shard_map/ppermute | solution.py:19
  101.7 3.7 %collective-permute-start = (f32[32,16]{0,1:T(8,128)S(1)}, f32[32,16]{0,1:T(8,128)S(1)}, u32[]{:S(2)}, u32[]{:S(2)}) collective-permute-start(f32[32,16]{0,1:T(8,128)S(1)} %pad_maximum_fusion), channel_id=1, source_target_pairs={{0,4},{4,0},{8,12},{12,8},{16,20},{20,16},{24,28},{28,24},{1,5},{5... | collective-permute-start | bytes 6152 | tf_op jit(solution)/shard_map/ppermute | solution.py:19
  106.7 31.9 %collective-permute-start.33 = (bf16[256,1024]{1,0:T(8,128)(2,1)S(1)}, bf16[256,1024]{1,0:T(8,128)(2,1)S(1)}, u32[]{:S(2)}, u32[]{:S(2)}) collective-permute-start(bf16[256,1024]{1,0:T(8,128)(2,1)S(1)} %constant_dynamic-update-slice_fusion.refs_0_), channel_id=1, source_target_pairs={{0,1},{1,0},{2,3},{3,2},{4,5},{5,4},{6,7},{7,6},{8,9},{9,8},{10,11... | collective-permute-start | bytes 1572872 | tf_op jit(solution)/shard_map/ppermute | solution.py:19
  107.7 30.9 %collective-permute-start.35 = (bf16[256,1024]{1,0:T(8,128)(2,1)S(1)}, bf16[256,1024]{1,0:T(8,128)(2,1)S(1)}, u32[]{:S(2)}, u32[]{:S(2)}) collective-permute-start(bf16[256,1024]{1,0:T(8,128)(2,1)S(1)} %collective-permute-done.34.refs_2_), channel_id=1, source_target_pairs={{0,1},{1,0},{2,3},{3,2},{4,5},{5,4},{6,7},{7,6},{8,9},{9,8},{10,11... | collective-permute-start | bytes 1572872 | tf_op jit(solution)/shard_map/ppermute | solution.py:19
  112.3 1.0 copy-start
  113.4 1.0 copy-start.1
  114.4 1.0 copy-start.2
  138.5 38.1 %collective-permute-start.17 = (bf16[2,256,1024]{2,1,0:T(8,128)(2,1)S(1)}, bf16[2,256,1024]{2,1,0:T(8,128)(2,1)S(1)}, u32[]{:S(2)}, u32[]{:S(2)}) collective-permute-start(bf16[2,256,1024]{2,1,0:T(8,128)(2,1)S(1)} %mix_odd.1), channel_id=1, source_target_pairs={{0,1},{1,0},{2,3},{3,2},{4,5},{5,4},{6,7},{7,6},{8,9},{9,8},{10,11... | collective-permute-start | bytes 3145736 | tf_op jit(solution)/shard_map/ppermute | solution.py:19
  161.1 17.3 %collective-permute-start.36 = (bf16[2,256,1024]{2,1,0:T(8,128)(2,1)S(1)}, bf16[2,256,1024]{2,1,0:T(8,128)(2,1)S(1)}, u32[]{:S(2)}, u32[]{:S(2)}) collective-permute-start(bf16[2,256,1024]{2,1,0:T(8,128)(2,1)S(1)} %back_odd.1), channel_id=1, source_target_pairs={{0,1},{1,0},{2,3},{3,2},{4,5},{5,4},{6,7},{7,6},{8,9},{9,8},{10,11... | collective-permute-start | bytes 3145736 | tf_op jit(solution)/shard_map/ppermute | solution.py:19
  176.8 16.6 %collective-permute-start.18 = (bf16[256,1024]{1,0:T(8,128)(2,1)S(1)}, bf16[256,1024]{1,0:T(8,128)(2,1)S(1)}, u32[]{:S(2)}, u32[]{:S(2)}) collective-permute-start(bf16[256,1024]{1,0:T(8,128)(2,1)S(1)} %fusion.2), channel_id=1, source_target_pairs={{0,2},{1,3},{2,0},{3,1},{4,6},{5,7},{6,4},{7,5},{8,10},{9,11},{10,... | collective-permute-start | bytes 1572872 | tf_op jit(solution)/shard_map/ppermute | solution.py:19
  178.6 23.4 %collective-permute-start.37 = (bf16[256,1024]{1,0:T(8,128)(2,1)S(1)}, bf16[256,1024]{1,0:T(8,128)(2,1)S(1)}, u32[]{:S(2)}, u32[]{:S(2)}) collective-permute-start(bf16[256,1024]{1,0:T(8,128)(2,1)S(1)} %fusion.3), channel_id=1, source_target_pairs={{0,2},{1,3},{2,0},{3,1},{4,6},{5,7},{6,4},{7,5},{8,10},{9,11},{10,... | collective-permute-start | bytes 1572872 | tf_op jit(solution)/shard_map/ppermute | solution.py:19
  193.7 9.5 %collective-permute-start.19 = (bf16[32,1024]{1,0:T(8,128)(2,1)S(1)}, bf16[32,1024]{1,0:T(8,128)(2,1)S(1)}, u32[]{:S(2)}, u32[]{:S(2)}) collective-permute-start(bf16[32,1024]{1,0:T(8,128)(2,1)S(1)} %get-tuple-element.15), channel_id=1, source_target_pairs={{0,4},{4,0},{8,12},{12,8},{16,20},{20,16},{24,28},{28,24},{1,5},{5... | collective-permute-start | bytes 196616 | tf_op jit(solution)/shard_map/ppermute | solution.py:19
  195.2 10.7 %collective-permute-start.25 = (bf16[32,1024]{1,0:T(8,128)(2,1)S(1)}, bf16[32,1024]{1,0:T(8,128)(2,1)S(1)}, u32[]{:S(2)}, u32[]{:S(2)}) collective-permute-start(bf16[32,1024]{1,0:T(8,128)(2,1)S(1)} %get-tuple-element.16), channel_id=1, source_target_pairs={{0,28},{4,24},{8,20},{12,16},{16,12},{20,8},{24,4},{28,0},{1,29},{... | collective-permute-start | bytes 196616 | tf_op jit(solution)/shard_map/ppermute | solution.py:19
  197.4 8.6 %collective-permute-start.24 = (bf16[32,1024]{1,0:T(8,128)(2,1)S(1)}, bf16[32,1024]{1,0:T(8,128)(2,1)S(1)}, u32[]{:S(2)}, u32[]{:S(2)}) collective-permute-start(bf16[32,1024]{1,0:T(8,128)(2,1)S(1)} %get-tuple-element.17), channel_id=1, source_target_pairs={{0,24},{4,28},{8,16},{12,20},{16,8},{20,12},{24,0},{28,4},{1,25},{... | collective-permute-start | bytes 196616 | tf_op jit(solution)/shard_map/ppermute | solution.py:19
  199.1 8.9 %collective-permute-start.23 = (bf16[32,1024]{1,0:T(8,128)(2,1)S(1)}, bf16[32,1024]{1,0:T(8,128)(2,1)S(1)}, u32[]{:S(2)}, u32[]{:S(2)}) collective-permute-start(bf16[32,1024]{1,0:T(8,128)(2,1)S(1)} %get-tuple-element.18), channel_id=1, source_target_pairs={{0,20},{4,16},{8,28},{12,24},{16,4},{20,0},{24,12},{28,8},{1,21},{... | collective-permute-start | bytes 196616 | tf_op jit(solution)/shard_map/ppermute | solution.py:19
  202.0 19.8 %collective-permute-start.22 = (bf16[32,1024]{1,0:T(8,128)(2,1)S(1)}, bf16[32,1024]{1,0:T(8,128)(2,1)S(1)}, u32[]{:S(2)}, u32[]{:S(2)}) collective-permute-start(bf16[32,1024]{1,0:T(8,128)(2,1)S(1)} %get-tuple-element.19), channel_id=1, source_target_pairs={{0,16},{4,20},{8,24},{12,28},{16,0},{20,4},{24,8},{28,12},{1,17},{... | collective-permute-start | bytes 196616 | tf_op jit(solution)/shard_map/ppermute | solution.py:19
  203.2 19.9 %collective-permute-start.21 = (bf16[32,1024]{1,0:T(8,128)(2,1)S(1)}, bf16[32,1024]{1,0:T(8,128)(2,1)S(1)}, u32[]{:S(2)}, u32[]{:S(2)}) collective-permute-start(bf16[32,1024]{1,0:T(8,128)(2,1)S(1)} %get-tuple-element.20), channel_id=1, source_target_pairs={{0,12},{4,8},{8,4},{12,0},{16,28},{20,24},{24,20},{28,16},{1,13},{... | collective-permute-start | bytes 196616 | tf_op jit(solution)/shard_map/ppermute | solution.py:19
  206.0 17.6 %collective-permute-start.20 = (bf16[32,1024]{1,0:T(8,128)(2,1)S(1)}, bf16[32,1024]{1,0:T(8,128)(2,1)S(1)}, u32[]{:S(2)}, u32[]{:S(2)}) collective-permute-start(bf16[32,1024]{1,0:T(8,128)(2,1)S(1)} %get-tuple-element.21), channel_id=1, source_target_pairs={{0,8},{4,12},{8,0},{12,4},{16,24},{20,28},{24,16},{28,20},{1,9},{5... | collective-permute-start | bytes 196616 | tf_op jit(solution)/shard_map/ppermute | solution.py:19
  206.0 21.5 %collective-permute-start.38 = (bf16[32,1024]{1,0:T(8,128)(2,1)S(1)}, bf16[32,1024]{1,0:T(8,128)(2,1)S(1)}, u32[]{:S(2)}, u32[]{:S(2)}) collective-permute-start(bf16[32,1024]{1,0:T(8,128)(2,1)S(1)} %get-tuple-element.8), channel_id=1, source_target_pairs={{0,4},{4,0},{8,12},{12,8},{16,20},{20,16},{24,28},{28,24},{1,5},{5... | collective-permute-start | bytes 196616 | tf_op jit(solution)/shard_map/ppermute | solution.py:19
  208.0 19.5 %collective-permute-start.44 = (bf16[32,1024]{1,0:T(8,128)(2,1)S(1)}, bf16[32,1024]{1,0:T(8,128)(2,1)S(1)}, u32[]{:S(2)}, u32[]{:S(2)}) collective-permute-start(bf16[32,1024]{1,0:T(8,128)(2,1)S(1)} %get-tuple-element.9), channel_id=1, source_target_pairs={{0,28},{4,24},{8,20},{12,16},{16,12},{20,8},{24,4},{28,0},{1,29},{... | collective-permute-start | bytes 196616 | tf_op jit(solution)/shard_map/ppermute | solution.py:19
  221.8 7.9 %collective-permute-start.43 = (bf16[32,1024]{1,0:T(8,128)(2,1)S(1)}, bf16[32,1024]{1,0:T(8,128)(2,1)S(1)}, u32[]{:S(2)}, u32[]{:S(2)}) collective-permute-start(bf16[32,1024]{1,0:T(8,128)(2,1)S(1)} %get-tuple-element.10), channel_id=1, source_target_pairs={{0,24},{4,28},{8,16},{12,20},{16,8},{20,12},{24,0},{28,4},{1,25},{... | collective-permute-start | bytes 196616 | tf_op jit(solution)/shard_map/ppermute | solution.py:19
  223.1 8.9 %collective-permute-start.42 = (bf16[32,1024]{1,0:T(8,128)(2,1)S(1)}, bf16[32,1024]{1,0:T(8,128)(2,1)S(1)}, u32[]{:S(2)}, u32[]{:S(2)}) collective-permute-start(bf16[32,1024]{1,0:T(8,128)(2,1)S(1)} %get-tuple-element.11), channel_id=1, source_target_pairs={{0,20},{4,16},{8,28},{12,24},{16,4},{20,0},{24,12},{28,8},{1,21},{... | collective-permute-start | bytes 196616 | tf_op jit(solution)/shard_map/ppermute | solution.py:19
  223.6 9.4 %collective-permute-start.41 = (bf16[32,1024]{1,0:T(8,128)(2,1)S(1)}, bf16[32,1024]{1,0:T(8,128)(2,1)S(1)}, u32[]{:S(2)}, u32[]{:S(2)}) collective-permute-start(bf16[32,1024]{1,0:T(8,128)(2,1)S(1)} %get-tuple-element.12), channel_id=1, source_target_pairs={{0,16},{4,20},{8,24},{12,28},{16,0},{20,4},{24,8},{28,12},{1,17},{... | collective-permute-start | bytes 196616 | tf_op jit(solution)/shard_map/ppermute | solution.py:19
  227.5 7.0 %collective-permute-start.40 = (bf16[32,1024]{1,0:T(8,128)(2,1)S(1)}, bf16[32,1024]{1,0:T(8,128)(2,1)S(1)}, u32[]{:S(2)}, u32[]{:S(2)}) collective-permute-start(bf16[32,1024]{1,0:T(8,128)(2,1)S(1)} %get-tuple-element.13), channel_id=1, source_target_pairs={{0,12},{4,8},{8,4},{12,0},{16,28},{20,24},{24,20},{28,16},{1,13},{... | collective-permute-start | bytes 196616 | tf_op jit(solution)/shard_map/ppermute | solution.py:19
  227.5 7.0 %collective-permute-start.39 = (bf16[32,1024]{1,0:T(8,128)(2,1)S(1)}, bf16[32,1024]{1,0:T(8,128)(2,1)S(1)}, u32[]{:S(2)}, u32[]{:S(2)}) collective-permute-start(bf16[32,1024]{1,0:T(8,128)(2,1)S(1)} %get-tuple-element.14), channel_id=1, source_target_pairs={{0,8},{4,12},{8,0},{12,4},{16,24},{20,28},{24,16},{28,20},{1,9},{5... | collective-permute-start | bytes 196616 | tf_op jit(solution)/shard_map/ppermute | solution.py:19
  (1 other events, 1.0 us)

commit v2 on v1

v2 whole, which is shorter than its diff:
```python
import functools

import jax
import jax.numpy as jnp
from jax import lax
from jax.experimental import pallas as pl
from jax.experimental.pallas import tpu as pltpu
from jax.sharding import PartitionSpec as P

MIB = 1024 * 1024
F32 = jnp.float32
BF16 = jnp.bfloat16


def swap(value, axis, bits):
    size = lax.axis_size(axis)
    return lax.ppermute(value, axis, [(i, i ^ bits) for i in range(size)])


def gather_all(value):
    shape = (lax.axis_size("expert"), lax.axis_size("tensor"), *value.shape)
    return lax.all_gather(value, ("expert", "tensor"), axis=0, tiled=False).reshape(shape)


def scatter_rows(value, rows):
    blocks = value.reshape(-1, rows, value.shape[1])
    blocks = lax.all_to_all(blocks, "expert", split_axis=0, concat_axis=0, tiled=True)
    return jnp.sum(blocks.astype(F32), axis=0)


def scatter_chunks(even, odd):
    size = lax.axis_size("tensor")
    got = swap(odd, "tensor", 1)
    parts = [even[i].astype(F32) + got[i].astype(F32) for i in range(size // 2)]
    bit = 2
    while bit < size:
        kept = []
        for i in range(len(parts) // 2):
            sent = parts[2 * i + 1].astype(BF16)
            kept.append(parts[2 * i] + swap(sent, "tensor", bit).astype(F32))
        parts = kept
        bit *= 2
    return parts[0].astype(BF16)


def column(gates, index):
    lane = lax.broadcasted_iota(jnp.int32, gates.shape, 1)
    return jnp.sum(jnp.where(lane == index, gates, 0.0), axis=1, keepdims=True)


def dot(a, b, dims=((1,), (0,))):
    return lax.dot_general(a, b, (dims, ((), ())), preferred_element_type=F32)


def chunk(ref, c):
    part = ref[:, c]
    return part.reshape(part.shape[0] * part.shape[1], part.shape[2])


def preact_kernel(me_ref, gates_ref, x_ref, *refs):
    ws, (act_ref, slope_ref) = refs[:-2], refs[-2:]
    pre = sum(dot(chunk(x_ref, c), w[0]) for c, w in enumerate(ws))
    sig = jax.nn.sigmoid(pre)
    gate = column(gates_ref[...], pl.program_id(0))
    act_ref[...] = (gate * (pre * sig)).astype(BF16)
    slope_ref[...] = gate * (sig * (1.0 + pre * (1.0 - sig)))


def slope_kernel(me_ref, slope_ref, y_ref, *refs):
    ws, grad_ref = refs[:-1], refs[-1]
    grad = sum(dot(chunk(y_ref, c), w[...], ((1,), (1,))) for c, w in enumerate(ws))
    grad_ref[...] = (grad * slope_ref[...]).astype(BF16)


def mix_kernel(me_ref, act_ref, *refs):
    ws, out_ref = refs[:-1], refs[-1]
    deep = ws[0].shape[0]
    total = sum(dot(act_ref[:, q * deep : (q + 1) * deep], w[...]) for q, w in enumerate(ws))
    out_ref[0] = total.astype(BF16)


def back_kernel(me_ref, grad_ref, *refs):
    ws, out_ref = refs[:-1], refs[-1]
    group, _, hid = ws[0].shape
    total = 0.0
    for q, w in enumerate(ws):
        for i in range(group):
            e = q * group + i
            total = total + dot(grad_ref[:, e * hid : (e + 1) * hid], w[i], ((1,), (1,)))
    out_ref[0] = total.astype(BF16)


def write_out(step, steps, slot, c, value, out, buffer, sems):
    copy = pltpu.make_async_copy(buffer.at[slot, c], out, sems.at[slot, c])

    @pl.when(step >= 2)
    def _():
        copy.wait()

    buffer[slot, c] = value().astype(BF16)
    copy.start()


def drain(step, steps, out, buffer, sems):
    @pl.when(step == steps - 1)
    def _():
        for slot in range(min(2, steps)):
            for c in range(buffer.shape[1]):
                pltpu.make_async_copy(buffer.at[slot, c], out, sems.at[slot, c]).wait()


def d_out_kernel(steps, me_ref, act_ref, y_ref, out_ref, buffer, sems):
    e = pl.program_id(0)
    _, n, hid, width = buffer.shape
    act = act_ref[...].T
    rows = pl.ds(pl.multiple_of(e * hid, hid), hid)
    for c in range(n):
        out = out_ref.at[rows, pl.ds(c * width, width)]
        write_out(e, steps, e % 2, c, lambda: dot(act, chunk(y_ref, c)), out, buffer, sems)
    drain(e, steps, out_ref.at[rows, pl.ds(0, width)], buffer, sems)


def d_in_kernel(steps, me_ref, grad_ref, x_ref, out_ref, flipped, buffer, sems):
    e = pl.program_id(0)
    _, n, width, hid = buffer.shape

    @pl.when(e == 0)
    def _():
        for c in range(n):
            flipped[c] = chunk(x_ref, c).T

    grad = grad_ref[...]
    for c in range(n):
        out = out_ref.at[e, pl.ds(c * width, width), :]
        write_out(e, steps, e % 2, c, lambda: dot(flipped[c], grad), out, buffer, sems)
    drain(e, steps, out_ref.at[e, pl.ds(0, width), :], buffer, sems)


def call(kernel, name, grid, in_specs, out_specs, out_shape, args, flops, limit, scratch=()):
    moved = sum(a.size * a.dtype.itemsize for a in {id(a): a for a in args}.values())
    moved += sum(o.size * o.dtype.itemsize for o in jax.tree.leaves(out_shape))
    return pl.pallas_call(
        kernel,
        grid_spec=pltpu.PrefetchScalarGridSpec(
            num_scalar_prefetch=1,
            grid=grid,
            in_specs=in_specs,
            out_specs=out_specs,
            scratch_shapes=scratch,
        ),
        out_shape=out_shape,
        name=name,
        cost_estimate=pl.CostEstimate(flops=flops, bytes_accessed=moved, transcendentals=0),
        compiler_params=pltpu.CompilerParams(vmem_limit_bytes=limit),
    )(*args)


def once(shape, index):
    return pl.BlockSpec(shape, index, pipeline_mode=pl.Buffered(1))


def shards(tokens, cotangent, routing, gates, w_in, w_out):
    n = lax.axis_size("tensor")
    groups = lax.axis_size("expert")
    local, width, hid = w_in.shape
    rows, quarter = tokens.shape
    total = groups * rows
    top = routing.shape[1]
    me = lax.axis_index("tensor").astype(jnp.int32).reshape(1)

    xs = gather_all(tokens)
    routed = jnp.concatenate([routing.astype(F32), gates], axis=1)
    routed = lax.all_gather(routed, "expert", axis=0, tiled=True)
    ys = gather_all(cotangent)
    first = lax.axis_index("expert") * local
    experts = (first + jnp.arange(local, dtype=jnp.int32)).astype(F32)
    match = routed[:, :top, None] == experts[None, None, :]
    gate = jnp.sum(jnp.where(match, routed[:, top:, None], 0.0), axis=1)

    held = min(groups, max(1, 256 // rows))
    tile = held * rows
    tiles = groups // held
    limit = (32 if tiles == 1 else 56) * MIB
    cols = min(512, quarter)
    per = quarter // cols
    flat_out = w_out.reshape(local * hid, width)
    flops = 2 * total * local * hid * width
    flat = jax.ShapeDtypeStruct((total, local * hid), BF16)
    streams = min(4, local)

    x_spec = once((held, n, rows, quarter), lambda e, t, me: (t, 0, 0, 0))
    act, slope = call(
        preact_kernel,
        "preact",
        (local, tiles),
        [pl.BlockSpec((tile, local), lambda e, t, me: (t, 0)), x_spec]
        + [
            pl.BlockSpec((1, quarter, hid), lambda e, t, me, c=c: (e, c, 0))
            for c in range(n)
        ],
        [pl.BlockSpec((tile, hid), lambda e, t, me: (t, e))] * 2,
        [flat, jax.ShapeDtypeStruct(flat.shape, F32)],
        (me, gate, xs, *[w_in] * n),
        flops,
        limit,
    )

    def parts(kernel, name, left, weights, odd):
        is_out = weights.ndim == 2

        def w_spec(q):
            def index(i, j, t, me):
                block = (me[0] ^ (2 * i + odd)) * per + j
                return (q, block) if is_out else (q, block, 0)

            shape = (local * hid // streams, cols) if is_out else (local // streams, cols, hid)
            return pl.BlockSpec(shape, index)

        return call(
            kernel,
            name,
            (n // 2, per, tiles),
            [pl.BlockSpec((tile, local * hid), lambda i, j, t, me: (t, 0))]
            + [w_spec(q) for q in range(streams)],
            pl.BlockSpec((1, tile, cols), lambda i, j, t, me: (i, t, j)),
            jax.ShapeDtypeStruct((n // 2, total, quarter), BF16),
            (me, left, *[weights] * streams),
            flops // 2,
            limit,
        )

    mix_odd = parts(mix_kernel, "mix_odd", act, flat_out, 1)
    mix_even = parts(mix_kernel, "mix_even", act, flat_out, 0)
    mixed = scatter_rows(scatter_chunks(mix_even, mix_odd), rows).astype(BF16)

    grad = call(
        slope_kernel,
        "grad_preact",
        (local, tiles),
        [pl.BlockSpec((tile, hid), lambda e, t, me: (t, e)), x_spec]
        + [pl.BlockSpec((hid, quarter), lambda e, t, me, c=c: (e, c)) for c in range(n)],
        pl.BlockSpec((tile, hid), lambda e, t, me: (t, e)),
        flat,
        (me, slope, ys, *[flat_out] * n),
        flops,
        limit,
    )

    back_odd = parts(back_kernel, "back_odd", grad, w_in, 1)
    back_even = parts(back_kernel, "back_even", grad, w_in, 0)
    d_tokens = scatter_rows(scatter_chunks(back_even, back_odd), rows).astype(BF16)

    whole_spec = once((groups, n, rows, quarter), lambda e, me: (0, 0, 0, 0))
    row_spec = pl.BlockSpec((total, hid), lambda e, me: (0, e))
    anywhere = pl.BlockSpec(memory_space=pl.ANY)
    sems = pltpu.SemaphoreType.DMA((2, n))
    d_w_out = call(
        functools.partial(d_out_kernel, local),
        "d_w_out",
        (local,),
        [row_spec, whole_spec],
        anywhere,
        jax.ShapeDtypeStruct((local * hid, width), BF16),
        (me, act, ys),
        flops,
        limit,
        [pltpu.VMEM((2, n, hid, quarter), BF16), sems],
    ).reshape(w_out.shape)
    d_w_in = call(
        functools.partial(d_in_kernel, local),
        "d_w_in",
        (local,),
        [row_spec, whole_spec],
        anywhere,
        jax.ShapeDtypeStruct(w_in.shape, BF16),
        (me, grad, xs),
        flops,
        limit,
        [
            pltpu.VMEM((n, quarter, total), BF16),
            pltpu.VMEM((2, n, quarter, hid), BF16),
            sems,
        ],
    )
    return mixed, d_tokens, d_w_in, d_w_out


def solution(mesh):
    rows = P("expert", "tensor")
    routes = P("expert", None)
    columns_in = P("expert", None, "tensor")
    rows_out = P("expert", "tensor", None)
    return jax.shard_map(
        shards,
        mesh=mesh,
        in_specs=(rows, rows, routes, routes, columns_in, rows_out),
        out_specs=(rows, rows, columns_in, rows_out),
        check_vma=False,
    )
```

time: 236 us -> 249 us (1.055)
  starting transfers between devices: 84.2 us -> 13.4 us
  blocking collectives: 0 us -> 32.3 us
  waiting for transfers between devices: 44.8 us -> 76.5 us
  between operations: 0.92 us -> 14.2 us
  other arithmetic: 3.79 us -> 12 us
  local copies, waits for them, and re-layouts: 16 us -> 9.52 us
  Pallas kernels: 85.5 us -> 90.1 us
    ppermute x45 -> x4, starting transfers between devices: 84.2 us -> 3.42 us  [swap(): return lax.ppermute(value, axis, [(i, i ^ bits) for i in range(size)])]
    all_gather x0 -> x2, waiting for transfers between devices: none -> 59.5 us  [gather_all(): lax.all_gather(value, ('expert', 'tensor'), axis=0, tiled=False)]
    all_gather x0 -> x1, blocking collectives: none -> 32.3 us  [shards(): routed = lax.all_gather(routed, 'expert', axis=0, tiled=True)]
    ppermute x45 -> x4, waiting for transfers between devices: 44.8 us -> 15.6 us  [swap(): return lax.ppermute(value, axis, [(i, i ^ bits) for i in range(size)])]
    all_to_all x0 -> x2, starting transfers between devices: none -> 9.93 us  [scatter_rows(): lax.all_to_all(blocks, 'expert', split_axis=0, concat_axis=0, tiled=True)]
    ppermute x3 -> x0, local copies, waits for them, and re-layouts: 5.12 us -> none  [swap(): return lax.ppermute(value, axis, [(i, i ^ bits) for i in range(size)])]
    pallas_call x8, Pallas kernels: 85.5 us -> 90.1 us  [call(): pl.pallas_call(kernel, grid_spec=pltpu.PrefetchScalarGridSpec(num_scalar_...]
    concatenate x4 -> x0, local copies, waits for them, and re-layouts: 4.59 us -> none  [gather_rows(): jnp.concatenate([value] + [swap(value, 'expert', s) for s in range(1, siz...]
  transfers between devices with their start and end apart: 45 -> 8, of which waited for: 17 -> 4; matrix products, arithmetic and copies ran while one was open for 6% -> 4% of each run, Pallas kernels for 36% -> 36%
where the time goes in v2:
time: 249 us; the launch traced here: 248 us
  Pallas kernels  90.1 us (36%)
  waiting for transfers between devices  76.5 us (31%)
  blocking collectives  32.3 us (13%)
  between operations  14.2 us (6%)
  starting transfers between devices  13.4 us (5%)
  other arithmetic  12 us (5%)
  local copies, waits for them, and re-layouts  9.52 us (4%)
    pallas_call x8, Pallas kernels, call(): pl.pallas_call(kernel, grid_spec=pltpu.PrefetchScalarGridSpec(num_scalar_...  90.1 us
    all_gather x2, waiting for transfers between devices, gather_all(): lax.all_gather(value, ('expert', 'tensor'), axis=0, tiled=False)  59.5 us
    all_gather x1, blocking collectives, shards(): routed = lax.all_gather(routed, 'expert', axis=0, tiled=True)  32.3 us
    ppermute x4, waiting for transfers between devices, swap(): return lax.ppermute(value, axis, [(i, i ^ bits) for i in range(size)])  15.6 us
    all_to_all x2, starting transfers between devices, scatter_rows(): lax.all_to_all(blocks, 'expert', split_axis=0, concat_axis=0, tiled=True)  9.93 us
    unnamed x15, local copies, waits for them, and re-layouts  9.37 us
  transfers between devices with their start and end apart: 8, of which 4 were waited for; matrix products, arithmetic and copies ran while one was open for 4% of the time, Pallas kernels for 36%

profile of v2, /device:TPU:0, one launch (start us, length us, event | category | flops | bytes accessed | tf_op | source)
XLA Modules:
  0.0 248.0 jit_solution(16786925991399244892)
XLA Ops:
  7.2 0.0 all-gather.6.cloned.1.call-start
  7.2 0.7 all-gather.6.cloned.1.call-update
  7.9 0.0 all-gather.8.cloned.1.call-start
  7.9 0.7 all-gather.8.cloned.1.call-update
  8.7 0.7 convert_element_type.70
  9.3 0.7 maximum_bitcast_fusion
  10.0 32.3 %all-gather.2 = f32[8,32,16]{1,2,0:T(8,128)S(1)} all-gather(f32[1,32,16]{1,2,0:T(8,128)S(1)} %maximum_bitcast_fusion), channel_id=1, replica_groups=mesh['expert'=8,'tensor'=4] {'expert'}, dimensions={0}, use_global_device_ids=true | all-gather | bytes 18432 | tf_op jit(solution)/shard_map/all_gather | solution.py:173
  42.4 0.1 reshape.62
  42.5 0.1 select_reduce_fusion
  42.6 0.1 copy.17.gates_ref
  42.7 27.3 %all-gather.6.cloned.1.call-done = bf16[1024,1024]{1,0:T(8,128)(2,1)} async-done(((bf16[32,1024]{1,0:T(8,128)(2,1)}), bf16[1024,1024]{1,0:T(8,128)(2,1)}) %all-gather.6.cloned.1.call-update) | async-done | bytes 2097168 | tf_op jit(solution)/shard_map/all_gather | solution.py:22
  70.0 0.0 copy-start
  70.0 1.6 copy-done
  71.6 14.7 %preact.1 = (bf16[256,3072]{1,0:T(8,128)(2,1)S(1)}, f32[256,3072]{1,0:T(8,128)S(1)}) custom-call(s32[1]{0:T(128)} %bitcast.me_ref, f32[256,8]{1,0:T(8,128)S(1)} %copy.17.gates_ref, bf16[8,4,32,1024]{3,2,1,0:T(8,128)(2,1)S(1)} %bitcast.23, bf16[8,4096,384]{2,1,0:T(8,128)(2,1)} %refs_3_.5, bf16[8,4096,384]{2,1,0:T(8,128)(2,1)} %refs_3_.5, ...), custom_call_target="tpu_custom_call" | custom-call | flops 6442450944 | bytes 31989764 | tf_op jit(solution)/shard_map/preact/pallas_call | solution.py:142
  86.3 0.0 copy-start.5
  86.3 1.7 copy-done.5
  87.9 7.8 %mix_odd.1 = bf16[2,256,1024]{2,1,0:T(8,128)(2,1)} custom-call(s32[1]{0:T(128)} %bitcast.me_ref, bf16[256,3072]{1,0:T(8,128)(2,1)S(1)} %get-tuple-element.6.act_ref, bf16[3072,4096]{1,0:T(8,128)(2,1)} %bitcast.27, bf16[3072,4096]{1,0:T(8,128)(2,1)} %bitcast.28, bf16[3072,4096]{1,0:T(8,128)(2,1)} %bitcast.29, bf16[3072,4096]{1,0:T(8,128)(2,1)} %bitcast.30), custom_call_target="tpu_custom_call" | custom-call | flops 3221225472 | bytes 27787268 | tf_op jit(solution)/shard_map/mix_odd/pallas_call | solution.py:142
  95.7 0.3 collective-permute-start
  96.0 32.2 %all-gather.8.cloned.1.call-done = bf16[1024,1024]{1,0:T(8,128)(2,1)} async-done(((bf16[32,1024]{1,0:T(8,128)(2,1)}), bf16[1024,1024]{1,0:T(8,128)(2,1)}) %all-gather.8.cloned.1.call-update) | async-done | bytes 2097168 | tf_op jit(solution)/shard_map/all_gather | solution.py:22
  128.1 1.6 copy-done.2
  129.7 1.9 copy-done.6
  131.6 14.4 %grad_preact.1.grad_ref = bf16[256,3072]{1,0:T(8,128)(2,1)S(1)} custom-call(s32[1]{0:T(128)} %bitcast.me_ref, f32[256,3072]{1,0:T(8,128)S(1)} %copy-done.6, bf16[8,4,32,1024]{3,2,1,0:T(8,128)(2,1)S(1)} %bitcast.25, bf16[3072,4096]{1,0:T(8,128)(2,1)} %bitcast.31, bf16[3072,4096]{1,0:T(8,128)(2,1)} %bitcast.32, bf16[3072,4096]{1,0:T(8,128)(2,1)} %bitcast.33, ...), custom_call_target="tpu_custom_call" | custom-call | flops 6442450944 | bytes 31981572 | tf_op jit(solution)/shard_map/grad_preact/pallas_call | solution.py:142
  146.0 8.6 %back_odd.1 = bf16[2,256,1024]{2,1,0:T(8,128)(2,1)} custom-call(s32[1]{0:T(128)} %bitcast.me_ref, bf16[256,3072]{1,0:T(8,128)(2,1)S(1)} %grad_preact.1.grad_ref, bf16[8,4096,384]{2,1,0:T(8,128)(2,1)} %refs_3_.5, bf16[8,4096,384]{2,1,0:T(8,128)(2,1)} %refs_3_.5, bf16[8,4096,384]{2,1,0:T(8,128)(2,1)} %refs_3_.5, bf16[8,4096,384]{2,1,0:T(8,128)(2,1)} %refs_3_.5), custom_call_target="tpu_custom_call" | custom-call | flops 3221225472 | bytes 27787268 | tf_op jit(solution)/shard_map/back_odd/pallas_call | solution.py:142
  154.6 0.3 collective-permute-start.2
  154.9 7.0 %mix_even.1 = bf16[2,256,1024]{2,1,0:T(8,128)(2,1)S(1)} custom-call(s32[1]{0:T(128)} %bitcast.me_ref, bf16[256,3072]{1,0:T(8,128)(2,1)S(1)} %get-tuple-element.6.act_ref, bf16[3072,4096]{1,0:T(8,128)(2,1)} %bitcast.35, bf16[3072,4096]{1,0:T(8,128)(2,1)} %bitcast.36, bf16[3072,4096]{1,0:T(8,128)(2,1)} %bitcast.37, bf16[3072,4096]{1,0:T(8,128)(2,1)} %bitcast.38), custom_call_target="tpu_custom_call" | custom-call | flops 3221225472 | bytes 27787268 | tf_op jit(solution)/shard_map/mix_even/pallas_call | solution.py:142
  161.9 0.0 collective-permute-done
  161.9 1.2 fusion.2
  163.1 1.5 collective-permute-start.1
  164.7 7.8 %back_even.1 = bf16[2,256,1024]{2,1,0:T(8,128)(2,1)S(1)} custom-call(s32[1]{0:T(128)} %bitcast.me_ref, bf16[256,3072]{1,0:T(8,128)(2,1)S(1)} %grad_preact.1.grad_ref, bf16[8,4096,384]{2,1,0:T(8,128)(2,1)} %refs_3_.5, bf16[8,4096,384]{2,1,0:T(8,128)(2,1)} %refs_3_.5, bf16[8,4096,384]{2,1,0:T(8,128)(2,1)} %refs_3_.5, bf16[8,4096,384]{2,1,0:T(8,128)(2,1)} %refs_3_.5), custom_call_target="tpu_custom_call" | custom-call | flops 3221225472 | bytes 27787268 | tf_op jit(solution)/shard_map/back_even/pallas_call | solution.py:142
  172.5 0.0 copy-start.4
  172.5 1.0 copy-done.4
  173.5 3.8 %collective-permute-done.1 = bf16[256,1024]{1,0:T(8,128)(2,1)S(1)} collective-permute-done((bf16[256,1024]{1,0:T(8,128)(2,1)S(1)}, bf16[256,1024]{1,0:T(8,128)(2,1)S(1)}, u32[]{:S(2)}, u32[]{:S(2)}) %collective-permute-start.1) | collective-permute-done | bytes 524320 | tf_op jit(solution)/shard_map/ppermute | solution.py:17
  177.3 2.1 fusion.1
  179.4 4.3 %all-to-all-start = ((bf16[8,32,1024]{2,1,0:T(8,128)(2,1)}), bf16[8,32,1024]{2,1,0:T(8,128)(2,1)}, u32[]{:S(2)}, u32[]{:S(2)}) async-start(bf16[8,32,1024]{2,1,0:T(8,128)(2,1)} %bitcast.40), calls=%async_computation | async-start | bytes 1048576 | tf_op jit(solution)/shard_map/all_to_all | solution.py:27
  183.7 0.0 collective-permute-done.2
  183.7 1.4 fusion.3
  185.1 1.4 collective-permute-start.3
  186.5 11.8 %collective-permute-done.3 = bf16[256,1024]{1,0:T(8,128)(2,1)S(1)} collective-permute-done((bf16[256,1024]{1,0:T(8,128)(2,1)S(1)}, bf16[256,1024]{1,0:T(8,128)(2,1)S(1)}, u32[]{:S(2)}, u32[]{:S(2)}) %collective-permute-start.3) | collective-permute-done | bytes 524320 | tf_op jit(solution)/shard_map/ppermute | solution.py:17
  198.3 2.3 fusion
  200.6 0.0 all-to-all-done
  200.6 5.6 %all-to-all-start.1 = ((bf16[8,32,1024]{2,1,0:T(8,128)(2,1)}), bf16[8,32,1024]{2,1,0:T(8,128)(2,1)}, u32[]{:S(2)}, u32[]{:S(2)}) async-start(bf16[8,32,1024]{2,1,0:T(8,128)(2,1)} %bitcast.41), calls=%async_computation.1 | async-start | bytes 1048576 | tf_op jit(solution)/shard_map/all_to_all | solution.py:27
  206.2 1.6 copy-done.3
  207.8 14.0 %d_w_out.1 = bf16[3072,4096]{1,0:T(8,128)(2,1)} custom-call(s32[1]{0:T(128)} %bitcast.me_ref, bf16[256,3072]{1,0:T(8,128)(2,1)S(1)} %get-tuple-element.6.act_ref, bf16[8,4,32,1024]{3,2,1,0:T(8,128)(2,1)S(1)} %bitcast.26), custom_call_target="tpu_custom_call" | custom-call | flops 6442450944 | bytes 28835844 | tf_op jit(solution)/shard_map/d_w_out/pallas_call | solution.py:142
  221.8 0.0 copy-done.1
  221.8 15.9 %d_w_in.1 = bf16[8,4096,384]{2,1,0:T(8,128)(2,1)} custom-call(s32[1]{0:T(128)} %bitcast.me_ref, bf16[256,3072]{1,0:T(8,128)(2,1)S(1)} %grad_preact.1.grad_ref, bf16[8,4,32,1024]{3,2,1,0:T(8,128)(2,1)S(1)} %bitcast.24), custom_call_target="tpu_custom_call" | custom-call | flops 6442450944 | bytes 28835844 | tf_op jit(solution)/shard_map/d_w_in/pallas_call | solution.py:142
  237.7 1.8 reduce_sum.34
  239.4 0.0 all-to-all-done.1
  239.4 1.8 reduce_sum.35
  (7 shorter events, 0.0 us)
Async XLA Ops:
  7.2 62.8 %all-gather.6.cloned.1.call-start = ((), (), s32[]{:S(2)}) async-start(), calls=%async_computation.2 | async-start | bytes 2162688 | tf_op jit(solution)/shard_map/all_gather | solution.py:22
  7.9 120.2 %all-gather.8.cloned.1.call-start = ((), (), s32[]{:S(2)}) async-start(), calls=%async_computation.3 | async-start | bytes 2162688 | tf_op jit(solution)/shard_map/all_gather | solution.py:22
  70.0 1.6 copy-start
  86.3 1.7 copy-start.5
  95.7 66.2 %collective-permute-start = (bf16[2,256,1024]{2,1,0:T(8,128)(2,1)}, bf16[2,256,1024]{2,1,0:T(8,128)(2,1)}, u32[]{:S(2)}, u32[]{:S(2)}) collective-permute-start(bf16[2,256,1024]{2,1,0:T(8,128)(2,1)} %mix_odd.1), channel_id=1, source_target_pairs={{0,1},{1,0},{2,3},{3,2},{4,5},{5,4},{6,7},{7,6},{8,9},{9,8},{10,11... | collective-permute-start | bytes 3145736 | tf_op jit(solution)/shard_map/ppermute | solution.py:17
  128.1 1.6 copy-start.2
  129.7 1.9 copy-start.6
  154.6 29.1 %collective-permute-start.2 = (bf16[2,256,1024]{2,1,0:T(8,128)(2,1)}, bf16[2,256,1024]{2,1,0:T(8,128)(2,1)}, u32[]{:S(2)}, u32[]{:S(2)}) collective-permute-start(bf16[2,256,1024]{2,1,0:T(8,128)(2,1)} %back_odd.1), channel_id=1, source_target_pairs={{0,1},{1,0},{2,3},{3,2},{4,5},{5,4},{6,7},{7,6},{8,9},{9,8},{10,11... | collective-permute-start | bytes 3145736 | tf_op jit(solution)/shard_map/ppermute | solution.py:17
  163.1 14.1 %collective-permute-start.1 = (bf16[256,1024]{1,0:T(8,128)(2,1)S(1)}, bf16[256,1024]{1,0:T(8,128)(2,1)S(1)}, u32[]{:S(2)}, u32[]{:S(2)}) collective-permute-start(bf16[256,1024]{1,0:T(8,128)(2,1)S(1)} %fusion.2), channel_id=1, source_target_pairs={{0,2},{1,3},{2,0},{3,1},{4,6},{5,7},{6,4},{7,5},{8,10},{9,11},{10,... | collective-permute-start | bytes 1572872 | tf_op jit(solution)/shard_map/ppermute | solution.py:17
  172.5 1.0 copy-start.4
  179.4 21.2 %all-to-all-start = ((bf16[8,32,1024]{2,1,0:T(8,128)(2,1)}), bf16[8,32,1024]{2,1,0:T(8,128)(2,1)}, u32[]{:S(2)}, u32[]{:S(2)}) async-start(bf16[8,32,1024]{2,1,0:T(8,128)(2,1)} %bitcast.40), calls=%async_computation | async-start | bytes 1048576 | tf_op jit(solution)/shard_map/all_to_all | solution.py:27
  185.1 13.2 %collective-permute-start.3 = (bf16[256,1024]{1,0:T(8,128)(2,1)S(1)}, bf16[256,1024]{1,0:T(8,128)(2,1)S(1)}, u32[]{:S(2)}, u32[]{:S(2)}) collective-permute-start(bf16[256,1024]{1,0:T(8,128)(2,1)S(1)} %fusion.3), channel_id=1, source_target_pairs={{0,2},{1,3},{2,0},{3,1},{4,6},{5,7},{6,4},{7,5},{8,10},{9,11},{10,... | collective-permute-start | bytes 1572872 | tf_op jit(solution)/shard_map/ppermute | solution.py:17
  200.6 38.9 %all-to-all-start.1 = ((bf16[8,32,1024]{2,1,0:T(8,128)(2,1)}), bf16[8,32,1024]{2,1,0:T(8,128)(2,1)}, u32[]{:S(2)}, u32[]{:S(2)}) async-start(bf16[8,32,1024]{2,1,0:T(8,128)(2,1)} %bitcast.41), calls=%async_computation.1 | async-start | bytes 1048576 | tf_op jit(solution)/shard_map/all_to_all | solution.py:27
  206.2 1.6 copy-start.3
  207.8 14.0 %copy-start.1 = (bf16[1024,1024]{1,0:T(8,128)(2,1)S(1)}, bf16[1024,1024]{1,0:T(8,128)(2,1)}, u32[]{:S(2)}) copy-start(bf16[1024,1024]{1,0:T(8,128)(2,1)} %all-gather.6.cloned.1.call-done) | copy-start | bytes 6291460
Sparse Core Ops, SparseCore 0:
  10.9 59.0 all-gather.5
  72.8 55.2 all-gather.7

commit v3 on v2

v3 whole, which is shorter than its diff:
```python
import functools

import jax
import jax.numpy as jnp
from jax import lax
from jax.experimental import pallas as pl
from jax.experimental.pallas import tpu as pltpu
from jax.sharding import PartitionSpec as P

MIB = 1024 * 1024
DEPTH = 3
F32 = jnp.float32
BF16 = jnp.bfloat16
ANYWHERE = pl.BlockSpec(memory_space=pl.ANY)


def swap(value, axis, bits):
    size = lax.axis_size(axis)
    return lax.ppermute(value, axis, [(i, i ^ bits) for i in range(size)])


def gather_rows(value):
    copies = jnp.broadcast_to(value[None], (lax.axis_size("expert"), *value.shape))
    return lax.all_to_all(copies, "expert", split_axis=0, concat_axis=0, tiled=True)


def gather_chunks(value):
    chunks = {0: value}
    bit = lax.axis_size("tensor") // 2
    while bit:
        chunks.update({s | bit: swap(c, "tensor", bit) for s, c in list(chunks.items())})
        bit //= 2
    return [chunks[s] for s in range(len(chunks))]


def scatter_rows(value, rows):
    blocks = value.reshape(-1, rows, value.shape[1])
    blocks = lax.all_to_all(blocks, "expert", split_axis=0, concat_axis=0, tiled=True)
    return jnp.sum(blocks.astype(F32), axis=0)


def scatter_chunks(even, odd):
    size = lax.axis_size("tensor")
    got = swap(odd, "tensor", 1)
    parts = [even[i].astype(F32) + got[i].astype(F32) for i in range(size // 2)]
    bit, passed = 2, ()
    while bit < size:
        kept = []
        for i in range(len(parts) // 2):
            sent = parts[2 * i + 1].astype(BF16)
            passed = passed or (sent,)
            kept.append(parts[2 * i] + swap(sent, "tensor", bit).astype(F32))
        parts = kept
        bit *= 2
    return parts[0].astype(BF16), passed


def pack_routes(routing, gates, lanes=128):
    high = lax.reduce_precision(gates, 8, 7)
    middle = lax.reduce_precision(gates - high, 8, 7)
    low = gates - high - middle
    packed = jnp.concatenate([routing.astype(F32), high, middle, low], axis=1)
    return jnp.pad(packed, ((0, 0), (0, lanes - packed.shape[1]))).astype(BF16)


def unpack_gates(packed, top, first, local):
    packed = packed[:, : 4 * top].astype(F32)
    chosen, high, middle, low = (packed[:, i * top : (i + 1) * top] for i in range(4))
    value = high + middle + low
    experts = (first + jnp.arange(local, dtype=jnp.int32)).astype(F32)
    match = chosen[:, :, None] == experts[None, None, :]
    return jnp.sum(jnp.where(match, value[:, :, None], 0.0), axis=1)


def column(gates, index):
    lane = lax.broadcasted_iota(jnp.int32, gates.shape, 1)
    return jnp.sum(jnp.where(lane == index, gates, 0.0), axis=1, keepdims=True)


def dot(a, b, dims=((1,), (0,))):
    return lax.dot_general(a, b, (dims, ((), ())), preferred_element_type=F32)


def flat_rows(part):
    return part.reshape(part.shape[0] * part.shape[1], part.shape[2])


def stream(copies, step, steps, first):
    @pl.when(first & (step == 0))
    def _():
        for ahead in range(min(DEPTH - 1, steps)):
            for copy in copies(ahead):
                copy.start()

    @pl.when(first & (step + DEPTH - 1 < steps))
    def _():
        for copy in copies(step + DEPTH - 1):
            copy.start()

    @pl.when(first)
    def _():
        for copy in copies(step):
            copy.wait()


def block(index, size):
    return pl.ds(pl.multiple_of(index * size, size), size)


def preact_kernel(pieces, steps, me_ref, gates_ref, *refs):
    xs, (w_ref, act_ref, slope_ref, buffer, sems) = refs[: len(pieces)], refs[-5:]
    e = pl.program_id(0)
    _, n, width, hid = buffer.shape

    def copies(step):
        slot = step % DEPTH
        return [
            pltpu.make_async_copy(
                w_ref.at[step, block(me_ref[0] ^ s, width), :], buffer.at[slot, s], sems.at[slot, s]
            )
            for s in range(n)
        ]

    stream(copies, e, steps, pl.program_id(1) == 0)
    pre = 0.0
    for x, (s, start) in zip(xs, pieces):
        w = buffer[e % DEPTH, s, start : start + x.shape[2], :]
        pre = pre + dot(flat_rows(x[...]), w)
    sig = jax.nn.sigmoid(pre)
    gate = column(gates_ref[...], e)
    act_ref[...] = (gate * (pre * sig)).astype(BF16)
    slope_ref[...] = gate * (sig * (1.0 + pre * (1.0 - sig)))


def slope_kernel(pieces, steps, me_ref, slope_ref, *refs):
    ys, w_ref, (grad_ref, buffer, sems) = refs[: len(pieces)], refs[len(pieces)], refs[-3:]
    e = pl.program_id(0)
    _, n, hid, width = buffer.shape

    def copies(step):
        slot = step % DEPTH
        return [
            pltpu.make_async_copy(
                w_ref.at[block(step, hid), block(me_ref[0] ^ s, width)],
                buffer.at[slot, s],
                sems.at[slot, s],
            )
            for s in range(n)
        ]

    stream(copies, e, steps, pl.program_id(1) == 0)
    grad = 0.0
    for y, (s, start) in zip(ys, pieces):
        w = buffer[e % DEPTH, s, :, start : start + y.shape[2]]
        grad = grad + dot(flat_rows(y[...]), w, ((1,), (1,)))
    grad_ref[...] = (grad * slope_ref[...]).astype(BF16)


def mix_kernel(steps, per, odd, me_ref, act_ref, w_ref, *refs):
    out_ref, buffer, sems = refs[-3:]
    _, pieces, deep, cols = buffer.shape
    step = pl.program_id(0)

    def copies(step):
        slot = step % DEPTH
        column_block = (me_ref[0] ^ (2 * (step // per) + odd)) * per + step % per
        return [
            pltpu.make_async_copy(
                w_ref.at[pl.ds(q * deep, deep), block(column_block, cols)],
                buffer.at[slot, q],
                sems.at[slot, q],
            )
            for q in range(pieces)
        ]

    stream(copies, step, steps, pl.program_id(1) == 0)
    weights = buffer[step % DEPTH].reshape(pieces * deep, cols)
    out_ref[0] = dot(act_ref[...], weights).astype(BF16)


def back_kernel(steps, per, odd, me_ref, grad_ref, w_ref, *refs):
    out_ref, buffer, sems = refs[-3:]
    _, pieces, group, cols, hid = buffer.shape
    step = pl.program_id(0)

    def copies(step):
        slot = step % DEPTH
        column_block = (me_ref[0] ^ (2 * (step // per) + odd)) * per + step % per
        return [
            pltpu.make_async_copy(
                w_ref.at[pl.ds(q * group, group), block(column_block, cols), :],
                buffer.at[slot, q],
                sems.at[slot, q],
            )
            for q in range(pieces)
        ]

    stream(copies, step, steps, pl.program_id(1) == 0)
    total = 0.0
    for e in range(pieces * group):
        w = buffer[step % DEPTH, e // group, e % group]
        total = total + dot(grad_ref[:, e * hid : (e + 1) * hid], w, ((1,), (1,)))
    out_ref[0] = total.astype(BF16)


def drain(step, steps, out, buffer, sems):
    @pl.when(step == steps - 1)
    def _():
        for slot in range(min(2, steps)):
            for s in range(buffer.shape[1]):
                pltpu.make_async_copy(buffer.at[slot, s], out, sems.at[slot, s]).wait()


def write_step(step, steps, values, outs, buffer, sems):
    slot = step % 2

    @pl.when(step >= 2)
    def _():
        for s, out in enumerate(outs):
            pltpu.make_async_copy(buffer.at[slot, s], out, sems.at[slot, s]).wait()

    for s, value in enumerate(values()):
        buffer[slot, s] = value.astype(BF16)
    for s, out in enumerate(outs):
        pltpu.make_async_copy(buffer.at[slot, s], out, sems.at[slot, s]).start()
    drain(step, steps, outs[0], buffer, sems)


def d_out_kernel(pieces, steps, me_ref, act_ref, *refs):
    ys, (out_ref, buffer, sems) = refs[: len(pieces)], refs[-3:]
    e = pl.program_id(0)
    _, n, hid, width = buffer.shape
    act = act_ref[...].T
    outs = [out_ref.at[block(e, hid), block(me_ref[0] ^ s, width)] for s in range(n)]

    def values():
        for s in range(n):
            yield dot(act, flat_rows(ys[s][...]))

    write_step(e, steps, values, outs, buffer, sems)


def d_in_kernel(pieces, steps, me_ref, grad_ref, *refs):
    xs, (out_ref, flipped, buffer, sems) = refs[: len(pieces)], refs[-4:]
    e = pl.program_id(0)
    _, n, width, hid = buffer.shape

    @pl.when(e == 0)
    def _():
        for x, (s, start) in zip(xs, pieces):
            flipped[s, start : start + x.shape[2], :] = flat_rows(x[...]).T

    grad = grad_ref[...]
    outs = [out_ref.at[e, block(me_ref[0] ^ s, width), :] for s in range(n)]

    def values():
        for s in range(n):
            yield dot(flipped[s], grad)

    write_step(e, steps, values, outs, buffer, sems)


def call(kernel, name, grid, in_specs, out_specs, out_shape, args, flops, limit, scratch, after=()):
    moved = sum(a.size * a.dtype.itemsize for a in args)
    moved += sum(o.size * o.dtype.itemsize for o in jax.tree.leaves(out_shape))
    return pl.pallas_call(
        kernel,
        grid_spec=pltpu.PrefetchScalarGridSpec(
            num_scalar_prefetch=1,
            grid=grid,
            in_specs=in_specs + [ANYWHERE] * len(after),
            out_specs=out_specs,
            scratch_shapes=scratch,
        ),
        out_shape=out_shape,
        name=name,
        cost_estimate=pl.CostEstimate(flops=flops, bytes_accessed=moved, transcendentals=0),
        compiler_params=pltpu.CompilerParams(vmem_limit_bytes=limit),
    )(*args, *after)


def once(shape, index):
    return pl.BlockSpec(shape, index, pipeline_mode=pl.Buffered(1))


def shards(tokens, cotangent, routing, gates, w_in, w_out):
    n = lax.axis_size("tensor")
    groups = lax.axis_size("expert")
    local, width, hid = w_in.shape
    rows, quarter = tokens.shape
    half = quarter // 2
    total = groups * rows
    top = routing.shape[1]
    me = lax.axis_index("tensor").astype(jnp.int32).reshape(1)

    packed = jnp.concatenate([tokens[:, :half], pack_routes(routing, gates)], axis=1)
    left = gather_rows(packed)
    right = gather_rows(tokens[:, half:])
    whole = gather_rows(cotangent)
    lefts, rights = gather_chunks(left), gather_chunks(right)
    ys = gather_chunks(whole)
    xs = lefts + rights
    x_pieces = [(s, 0) for s in range(n)] + [(s, half) for s in range(n)]
    y_pieces = [(s, 0) for s in range(n)]
    x_widths, y_widths = [half] * (2 * n), [quarter] * n
    first = lax.axis_index("expert") * local
    gate = unpack_gates(left[:, :, half:].reshape(total, -1), top, first, local)

    held = min(groups, max(1, 256 // rows))
    tile = held * rows
    tiles = groups // held
    limit = (32 if tiles == 1 else 56) * MIB
    cols = min(512, quarter)
    per = quarter // cols
    flat_out = w_out.reshape(local * hid, width)
    flops = 2 * total * local * hid * width
    flat = jax.ShapeDtypeStruct((total, local * hid), BF16)
    streams = min(4, local)

    def tile_specs(widths):
        return [once((held, rows, w), lambda e, t, me: (t, 0, 0)) for w in widths]

    def ring(*shape):
        return [
            pltpu.VMEM((DEPTH, *shape), BF16),
            pltpu.SemaphoreType.DMA((DEPTH, shape[0])),
        ]

    act, slope = call(
        functools.partial(preact_kernel, x_pieces, local),
        "preact",
        (local, tiles),
        [pl.BlockSpec((tile, local), lambda e, t, me: (t, 0))] + tile_specs(x_widths) + [ANYWHERE],
        [pl.BlockSpec((tile, hid), lambda e, t, me: (t, e))] * 2,
        [flat, jax.ShapeDtypeStruct(flat.shape, F32)],
        (me, gate, *xs, w_in),
        flops,
        limit,
        ring(n, quarter, hid),
    )

    def parts(kernel, name, left, weights, odd, after=()):
        if weights.ndim == 2:
            shape = (streams, local * hid // streams, cols)
        else:
            shape = (streams, local // streams, cols, hid)
        steps = n // 2 * per
        return call(
            functools.partial(kernel, steps, per, odd),
            name,
            (steps, tiles),
            [pl.BlockSpec((tile, local * hid), lambda i, t, me: (t, 0)), ANYWHERE],
            pl.BlockSpec((1, tile, cols), lambda i, t, me: (i // per, t, i % per)),
            jax.ShapeDtypeStruct((n // 2, total, quarter), BF16),
            (me, left, weights),
            flops // 2,
            limit,
            ring(*shape),
            after,
        )

    mix_odd = parts(mix_kernel, "mix_odd", act, flat_out, 1)
    mix_even = parts(mix_kernel, "mix_even", act, flat_out, 0, (mix_odd,))
    mix_sum, mix_passed = scatter_chunks(mix_even, mix_odd)
    mixed = scatter_rows(mix_sum, rows).astype(BF16)

    grad = call(
        functools.partial(slope_kernel, y_pieces, local),
        "grad_preact",
        (local, tiles),
        [pl.BlockSpec((tile, hid), lambda e, t, me: (t, e))] + tile_specs(y_widths) + [ANYWHERE],
        pl.BlockSpec((tile, hid), lambda e, t, me: (t, e)),
        flat,
        (me, slope, *ys, flat_out),
        flops,
        limit,
        ring(n, hid, quarter),
        mix_passed,
    )

    back_odd = parts(back_kernel, "back_odd", grad, w_in, 1, (mix_sum,))
    back_even = parts(back_kernel, "back_even", grad, w_in, 0, (back_odd,))
    back_sum, back_passed = scatter_chunks(back_even, back_odd)
    d_tokens = scatter_rows(back_sum, rows).astype(BF16)

    def whole_specs(widths):
        return [once((groups, rows, w), lambda e, me: (0, 0, 0)) for w in widths]

    row_spec = pl.BlockSpec((total, hid), lambda e, me: (0, e))
    sems = pltpu.SemaphoreType.DMA((2, n))
    d_w_out = call(
        functools.partial(d_out_kernel, y_pieces, local),
        "d_w_out",
        (local,),
        [row_spec] + whole_specs(y_widths),
        ANYWHERE,
        jax.ShapeDtypeStruct((local * hid, width), BF16),
        (me, act, *ys),
        flops,
        limit,
        [pltpu.VMEM((2, n, hid, quarter), BF16), sems],
        back_passed,
    )
    d_w_in = call(
        functools.partial(d_in_kernel, x_pieces, local),
        "d_w_in",
        (local,),
        [row_spec] + whole_specs(x_widths),
        ANYWHERE,
        jax.ShapeDtypeStruct(w_in.shape, BF16),
        (me, grad, *xs),
        flops,
        limit,
        [
            pltpu.VMEM((n, quarter, total), BF16),
            pltpu.VMEM((2, n, quarter, hid), BF16),
            sems,
        ],
        (d_w_out, back_sum),
    )
    return mixed, d_tokens, d_w_in, d_w_out.reshape(w_out.shape)


def solution(mesh):
    rows = P("expert", "tensor")
    routes = P("expert", None)
    columns_in = P("expert", None, "tensor")
    rows_out = P("expert", "tensor", None)
    return jax.shard_map(
        shards,
        mesh=mesh,
        in_specs=(rows, rows, routes, routes, columns_in, rows_out),
        out_specs=(rows, rows, columns_in, rows_out),
        check_vma=False,
    )
```

time: 249 us -> 195 us (0.78)
  blocking collectives: 32.3 us -> 0 us
  waiting for transfers between devices: 76.5 us -> 46.9 us
  starting transfers between devices: 13.4 us -> 33.8 us
  between operations: 14.2 us -> 1.03 us
  Pallas kernels: 90.1 us -> 81.8 us
  local copies, waits for them, and re-layouts: 9.52 us -> 17.5 us
    all_gather x2 -> x0, waiting for transfers between devices: 59.5 us -> none  [gather_all(): lax.all_gather(value, ('expert', 'tensor'), axis=0, tiled=False)]
    all_gather x1 -> x0, blocking collectives: 32.3 us -> none  [shards(): routed = lax.all_gather(routed, 'expert', axis=0, tiled=True)]
    all_to_all x0 -> x3, waiting for transfers between devices: none -> 15.9 us  [gather_rows(): lax.all_to_all(copies, 'expert', split_axis=0, concat_axis=0, tiled=True)]
    all_to_all x0 -> x3, starting transfers between devices: none -> 14.4 us  [gather_rows(): lax.all_to_all(copies, 'expert', split_axis=0, concat_axis=0, tiled=True)]
    ppermute x4 -> x13, waiting for transfers between devices: 15.6 us -> 26.5 us  [swap(): return lax.ppermute(value, axis, [(i, i ^ bits) for i in range(size)])]
    pallas_call x8, Pallas kernels: 90.1 us -> 81.8 us  [call(): pl.pallas_call(kernel, grid_spec=pltpu.PrefetchScalarGridSpec(num_scalar_...]
    ppermute x4 -> x13, starting transfers between devices: 3.42 us -> 8.01 us  [swap(): return lax.ppermute(value, axis, [(i, i ^ bits) for i in range(size)])]
    all_to_all x2, waiting for transfers between devices: 0.01 us -> 4.53 us  [scatter_rows(): lax.all_to_all(blocks, 'expert', split_axis=0, concat_axis=0, tiled=True)]
  transfers between devices with their start and end apart: 8 -> 18, of which waited for: 4 -> 6; matrix products, arithmetic and copies ran while one was open for 4% -> 5% of each run, Pallas kernels for 36% -> 38%
where the time goes in v3:
time: 195 us; the launch traced here: 193 us
  Pallas kernels  81.8 us (42%)
  waiting for transfers between devices  46.9 us (24%)
  starting transfers between devices  33.8 us (17%)
  local copies, waits for them, and re-layouts  17.5 us (9%)
  other arithmetic  12.4 us (6%)
    pallas_call x8, Pallas kernels, call(): pl.pallas_call(kernel, grid_spec=pltpu.PrefetchScalarGridSpec(num_scalar_...  81.8 us
    ppermute x13, waiting for transfers between devices, swap(): return lax.ppermute(value, axis, [(i, i ^ bits) for i in range(size)])  26.5 us
    all_to_all x3, waiting for transfers between devices, gather_rows(): lax.all_to_all(copies, 'expert', split_axis=0, concat_axis=0, tiled=True)  15.9 us
    all_to_all x3, starting transfers between devices, gather_rows(): lax.all_to_all(copies, 'expert', split_axis=0, concat_axis=0, tiled=True)  14.4 us
    unnamed x65, local copies, waits for them, and re-layouts  12.6 us
    all_to_all x2, starting transfers between devices, scatter_rows(): lax.all_to_all(blocks, 'expert', split_axis=0, concat_axis=0, tiled=True)  11.4 us
    ppermute x13, starting transfers between devices, swap(): return lax.ppermute(value, axis, [(i, i ^ bits) for i in range(size)])  8.01 us
    all_to_all x2, waiting for transfers between devices, scatter_rows(): lax.all_to_all(blocks, 'expert', split_axis=0, concat_axis=0, tiled=True)  4.53 us
  transfers between devices with their start and end apart: 18, of which 6 were waited for; matrix products, arithmetic and copies ran while one was open for 5% of the time, Pallas kernels for 38%

profile of v3, /device:TPU:0, one launch (start us, length us, event | category | flops | bytes accessed | tf_op | source)
XLA Modules:
  0.0 193.4 jit_solution(13256434031534760831)
XLA Ops:
  0.6 0.8 fusion.8
  1.4 0.7 broadcast_in_dim.17
  2.1 7.3 %all-to-all-start.1 = ((bf16[8,32,512]{2,1,0:T(8,128)(2,1)}), bf16[8,32,512]{2,1,0:T(8,128)(2,1)S(1)}, u32[]{:S(2)}, u32[]{:S(2)}) async-start(bf16[8,32,512]{2,1,0:T(8,128)(2,1)} %broadcast_in_dim.17), calls=%async_computation.1 | async-start | bytes 524288 | tf_op jit(solution)/shard_map/all_to_all | solution.py:24
  10.1 0.7 reduce-precision_convert_fusion.1
  10.9 7.4 %all-to-all-done.1.refs_4_ = bf16[8,32,512]{2,1,0:T(8,128)(2,1)S(1)} async-done(((bf16[8,32,512]{2,1,0:T(8,128)(2,1)}), bf16[8,32,512]{2,1,0:T(8,128)(2,1)S(1)}, u32[]{:S(2)}, u32[]{:S(2)}) %all-to-all-start.1) | async-done | bytes 262176 | tf_op jit(solution)/shard_map/all_to_all | solution.py:24
  18.3 0.8 broadcast_in_dim.14
  19.1 3.6 %all-to-all-start = ((bf16[8,32,640]{2,1,0:T(8,128)(2,1)}), bf16[8,32,640]{2,1,0:T(8,128)(2,1)S(1)}, u32[]{:S(2)}, u32[]{:S(2)}) async-start(bf16[8,32,640]{2,1,0:T(8,128)(2,1)} %broadcast_in_dim.14), calls=%async_computation | async-start | bytes 655360 | tf_op jit(solution)/shard_map/all_to_all | solution.py:24
  22.7 1.5 collective-permute-start.4
  24.2 8.4 %all-to-all-done.refs_0_ = bf16[8,32,640]{2,1,0:T(8,128)(2,1)S(1)} async-done(((bf16[8,32,640]{2,1,0:T(8,128)(2,1)}), bf16[8,32,640]{2,1,0:T(8,128)(2,1)S(1)}, u32[]{:S(2)}, u32[]{:S(2)}) %all-to-all-start) | async-done | bytes 327712 | tf_op jit(solution)/shard_map/all_to_all | solution.py:24
  32.7 1.7 broadcast_in_dim.18
  34.4 3.6 %all-to-all-start.3 = ((bf16[8,32,1024]{2,1,0:T(8,128)(2,1)}), bf16[8,32,1024]{2,1,0:T(8,128)(2,1)S(1)}, u32[]{:S(2)}, u32[]{:S(2)}) async-start(bf16[8,32,1024]{2,1,0:T(8,128)(2,1)} %broadcast_in_dim.18), calls=%async_computation.3 | async-start | bytes 1048576 | tf_op jit(solution)/shard_map/all_to_all | solution.py:24
  37.9 1.5 collective-permute-start.1
  40.2 6.5 %collective-permute-done.1.refs_2_ = bf16[8,32,640]{2,1,0:T(8,128)(2,1)S(1)} collective-permute-done((bf16[8,32,640]{2,1,0:T(8,128)(2,1)S(1)}, bf16[8,32,640]{2,1,0:T(8,128)(2,1)S(1)}, u32[]{:S(2)}, u32[]{:S(2)}) %collective-permute-start.1) | collective-permute-done | bytes 327712 | tf_op jit(solution)/shard_map/ppermute | solution.py:19
  47.1 0.8 copy.14.gates_ref
  47.9 0.7 copy-done.25
  48.6 0.7 copy-done.28
  49.3 0.7 copy-done.19
  50.1 1.0 copy-done.20
  51.0 0.9 copy-done.23
  52.0 0.9 copy-done.26
  53.0 0.9 copy-done.29
  53.9 0.9 copy-done.31
  54.8 13.7 %preact.1 = (bf16[256,3072]{1,0:T(8,128)(2,1)S(1)}, f32[256,3072]{1,0:T(8,128)S(1)}) custom-call(s32[1]{0:T(128)} %bitcast.me_ref, f32[256,8]{1,0:T(8,128)S(1)} %copy-done.31, bf16[8,32,640]{2,1,0:T(8,128)(2,1)S(1)} %all-to-all-done.refs_0_, bf16[8,32,640]{2,1,0:T(8,128)(2,1)S(1)} %collective-permute-done.refs_1_, ...), custom_call_target="tpu_custom_call" | custom-call | flops 6442450944 | bytes 32251908 | tf_op jit(solution)/shard_map/preact/pallas_call | solution.py:266
  68.5 7.3 %mix_odd.1.refs_0_ = bf16[2,256,1024]{2,1,0:T(8,128)(2,1)S(1)} custom-call(s32[1]{0:T(128)} %bitcast.me_ref, bf16[256,3072]{1,0:T(8,128)(2,1)S(1)} %get-tuple-element.6.act_ref, bf16[3072,4096]{1,0:T(8,128)(2,1)} %bitcast.20), custom_call_target="tpu_custom_call" | custom-call | flops 3221225472 | bytes 27787268 | tf_op jit(solution)/shard_map/mix_odd/pallas_call | solution.py:266
  76.4 1.5 collective-permute-start.9
  77.9 12.4 %collective-permute-done.9.refs_2_ = bf16[8,32,1024]{2,1,0:T(8,128)(2,1)S(1)} collective-permute-done((bf16[8,32,1024]{2,1,0:T(8,128)(2,1)S(1)}, bf16[8,32,1024]{2,1,0:T(8,128)(2,1)S(1)}, u32[]{:S(2)}, u32[]{:S(2)}) %collective-permute-start.9) | collective-permute-done | bytes 524320 | tf_op jit(solution)/shard_map/ppermute | solution.py:19
  90.3 6.4 %mix_even.1 = bf16[2,256,1024]{2,1,0:T(8,128)(2,1)S(1)} custom-call(s32[1]{0:T(128)} %bitcast.me_ref, bf16[256,3072]{1,0:T(8,128)(2,1)S(1)} %get-tuple-element.6.act_ref, bf16[3072,4096]{1,0:T(8,128)(2,1)} %bitcast.21, bf16[2,256,1024]{2,1,0:T(8,128)(2,1)S(1)} %mix_odd.1.refs_0_), custom_call_target="tpu_custom_call" | custom-call | flops 3221225472 | bytes 27787268 | tf_op jit(solution)/shard_map/mix_even/pallas_call | solution.py:266
  96.7 1.2 fusion.2.refs_5_
  98.0 1.6 collective-permute-start.7
  99.6 1.4 copy-done.1
  101.0 12.9 %grad_preact.1.grad_ref = bf16[256,3072]{1,0:T(8,128)(2,1)S(1)} custom-call(s32[1]{0:T(128)} %bitcast.me_ref, f32[256,3072]{1,0:T(8,128)S(1)} %copy-done.6, bf16[8,32,1024]{2,1,0:T(8,128)(2,1)S(1)} %copy-done.1, bf16[8,32,1024]{2,1,0:T(8,128)(2,1)S(1)} %collective-permute-done.8.refs_1_, bf16[8,32,1024]{2,1,0:T(8,128)(2,1)S(1)} %collective-permute-done.9.refs_2_, ...), custom_call_target="tpu_custom_call" | custom-call | flops 6442450944 | bytes 31981572 | tf_op jit(solution)/shard_map/grad_preact/pallas_call | solution.py:266
  114.0 1.3 fusion.1.refs_0_
  115.3 8.1 %back_odd.1.refs_0_ = bf16[2,256,1024]{2,1,0:T(8,128)(2,1)} custom-call(s32[1]{0:T(128)} %bitcast.me_ref, bf16[256,3072]{1,0:T(8,128)(2,1)S(1)} %grad_preact.1.grad_ref, bf16[8,4096,384]{2,1,0:T(8,128)(2,1)} %w_ref.3, bf16[256,1024]{1,0:T(8,128)(2,1)S(1)} %fusion.1.refs_0_), custom_call_target="tpu_custom_call" | custom-call | flops 3221225472 | bytes 27787268 | tf_op jit(solution)/shard_map/back_odd/pallas_call | solution.py:266
  123.6 5.7 %all-to-all-start.2 = ((bf16[8,32,1024]{2,1,0:T(8,128)(2,1)}), bf16[8,32,1024]{2,1,0:T(8,128)(2,1)}, u32[]{:S(2)}, u32[]{:S(2)}) async-start(bf16[8,32,1024]{2,1,0:T(8,128)(2,1)} %bitcast.19), calls=%async_computation.2 | async-start | bytes 1048576 | tf_op jit(solution)/shard_map/all_to_all | solution.py:38
  129.3 8.0 %back_even.1 = bf16[2,256,1024]{2,1,0:T(8,128)(2,1)} custom-call(s32[1]{0:T(128)} %bitcast.me_ref, bf16[256,3072]{1,0:T(8,128)(2,1)S(1)} %grad_preact.1.grad_ref, bf16[8,4096,384]{2,1,0:T(8,128)(2,1)} %w_ref.3, bf16[2,256,1024]{2,1,0:T(8,128)(2,1)} %back_odd.1.refs_0_), custom_call_target="tpu_custom_call" | custom-call | flops 3221225472 | bytes 27787268 | tf_op jit(solution)/shard_map/back_even/pallas_call | solution.py:266
  137.3 2.2 %fusion.3.refs_4_ = bf16[256,1024]{1,0:T(8,128)(2,1)} fusion(bf16[2,256,1024]{2,1,0:T(8,128)(2,1)} %collective-permute-done.11, bf16[2,256,1024]{2,1,0:T(8,128)(2,1)} %back_even.1), kind=kLoop, calls=%fused_computation.7 | loop fusion | flops 1048576 | bytes 1572864 | tf_op jit(solution)/shard_map/convert_element_type | solution.py:50
  140.0 4.5 %all-to-all-done.2 = bf16[8,32,1024]{2,1,0:T(8,128)(2,1)} async-done(((bf16[8,32,1024]{2,1,0:T(8,128)(2,1)}), bf16[8,32,1024]{2,1,0:T(8,128)(2,1)}, u32[]{:S(2)}, u32[]{:S(2)}) %all-to-all-start.2) | async-done | bytes 524320 | tf_op jit(solution)/shard_map/all_to_all | solution.py:38
  144.5 1.8 reduce_sum.34
  146.3 7.5 %collective-permute-done.12 = bf16[256,1024]{1,0:T(8,128)(2,1)} collective-permute-done((bf16[256,1024]{1,0:T(8,128)(2,1)}, bf16[256,1024]{1,0:T(8,128)(2,1)}, u32[]{:S(2)}, u32[]{:S(2)}) %collective-permute-start.12) | collective-permute-done | bytes 524320 | tf_op jit(solution)/shard_map/ppermute | solution.py:19
  153.8 2.4 %fusion.refs_9_ = bf16[256,1024]{1,0:T(8,128)(2,1)} fusion(bf16[256,1024]{1,0:T(8,128)(2,1)} %collective-permute-done.12, bf16[2,256,1024]{2,1,0:T(8,128)(2,1)} %collective-permute-done.11, bf16[2,256,1024]{2,1,0:T(8,128)(2,1)} %back_even.1), kind=kLoop, calls=%fused_computation.1 | loop fusion | flops 1572864 | bytes 2097152 | tf_op jit(solution)/shard_map/convert_element_type | solution.py:55
  156.3 5.7 %all-to-all-start.4 = ((bf16[8,32,1024]{2,1,0:T(8,128)(2,1)}), bf16[8,32,1024]{2,1,0:T(8,128)(2,1)}, u32[]{:S(2)}, u32[]{:S(2)}) async-start(bf16[8,32,1024]{2,1,0:T(8,128)(2,1)} %bitcast.18), calls=%async_computation.4 | async-start | bytes 1048576 | tf_op jit(solution)/shard_map/all_to_all | solution.py:38
  161.9 1.0 copy-done.2
  163.0 1.0 copy-done.10
  164.0 1.0 copy-done.12
  165.1 1.0 copy-done.14
  166.1 11.7 %d_w_out.1.refs_8_ = bf16[3072,4096]{1,0:T(8,128)(2,1)} custom-call(s32[1]{0:T(128)} %bitcast.me_ref, bf16[256,3072]{1,0:T(8,128)(2,1)S(1)} %get-tuple-element.6.act_ref, bf16[8,32,1024]{2,1,0:T(8,128)(2,1)S(1)} %copy-done.2, bf16[8,32,1024]{2,1,0:T(8,128)(2,1)S(1)} %copy-done.12, bf16[8,32,1024]{2,1,0:T(8,128)(2,1)S(1)} %copy-done.10, ...), custom_call_target="tpu_custom_call" | custom-call | flops 6442450944 | bytes 28835844 | tf_op jit(solution)/shard_map/d_w_out/pallas_call | solution.py:266
  178.0 13.6 %d_w_in.1 = bf16[8,4096,384]{2,1,0:T(8,128)(2,1)} custom-call(s32[1]{0:T(128)} %bitcast.me_ref, bf16[256,3072]{1,0:T(8,128)(2,1)S(1)} %grad_preact.1.grad_ref, bf16[8,32,640]{2,1,0:T(8,128)(2,1)S(1)} %all-to-all-done.refs_0_, bf16[8,32,640]{2,1,0:T(8,128)(2,1)S(1)} %copy-done.18, bf16[8,32,640]{2,1,0:T(8,128)(2,1)S(1)} %copy-done.16, ...), custom_call_target="tpu_custom_call" | custom-call | flops 6442450944 | bytes 29097988 | tf_op jit(solution)/shard_map/d_w_in/pallas_call | solution.py:266
  191.6 1.8 reduce_sum.35
  (83 shorter events, 3.2 us)
Async XLA Ops:
  2.1 16.2 %all-to-all-start.1 = ((bf16[8,32,512]{2,1,0:T(8,128)(2,1)}), bf16[8,32,512]{2,1,0:T(8,128)(2,1)S(1)}, u32[]{:S(2)}, u32[]{:S(2)}) async-start(bf16[8,32,512]{2,1,0:T(8,128)(2,1)} %broadcast_in_dim.17), calls=%async_computation.1 | async-start | bytes 524288 | tf_op jit(solution)/shard_map/all_to_all | solution.py:24
  18.3 50.2 %copy-start.7 = (bf16[8,32,512]{2,1,0:T(8,128)(2,1)}, bf16[8,32,512]{2,1,0:T(8,128)(2,1)S(1)}, u32[]{:S(2)}) copy-start(bf16[8,32,512]{2,1,0:T(8,128)(2,1)S(1)} %all-to-all-done.1.refs_4_) | copy-start | bytes 786436
  19.1 13.6 %all-to-all-start = ((bf16[8,32,640]{2,1,0:T(8,128)(2,1)}), bf16[8,32,640]{2,1,0:T(8,128)(2,1)S(1)}, u32[]{:S(2)}, u32[]{:S(2)}) async-start(bf16[8,32,640]{2,1,0:T(8,128)(2,1)} %broadcast_in_dim.14), calls=%async_computation | async-start | bytes 655360 | tf_op jit(solution)/shard_map/all_to_all | solution.py:24
  22.7 17.4 %collective-permute-start.4 = (bf16[8,32,512]{2,1,0:T(8,128)(2,1)S(1)}, bf16[8,32,512]{2,1,0:T(8,128)(2,1)S(1)}, u32[]{:S(2)}, u32[]{:S(2)}) collective-permute-start(bf16[8,32,512]{2,1,0:T(8,128)(2,1)S(1)} %all-to-all-done.1.refs_4_), channel_id=1, source_target_pairs={{0,2},{1,3},{2,0},{3,1},{4,6},{5,7},{6,4},{7,5},{8,10},{9,11},{10,... | collective-permute-start | bytes 786440 | tf_op jit(solution)/shard_map/ppermute | solution.py:19
  34.4 42.0 %all-to-all-start.3 = ((bf16[8,32,1024]{2,1,0:T(8,128)(2,1)}), bf16[8,32,1024]{2,1,0:T(8,128)(2,1)S(1)}, u32[]{:S(2)}, u32[]{:S(2)}) async-start(bf16[8,32,1024]{2,1,0:T(8,128)(2,1)} %broadcast_in_dim.18), calls=%async_computation.3 | async-start | bytes 1048576 | tf_op jit(solution)/shard_map/all_to_all | solution.py:24
  37.9 8.7 %collective-permute-start.1 = (bf16[8,32,640]{2,1,0:T(8,128)(2,1)S(1)}, bf16[8,32,640]{2,1,0:T(8,128)(2,1)S(1)}, u32[]{:S(2)}, u32[]{:S(2)}) collective-permute-start(bf16[8,32,640]{2,1,0:T(8,128)(2,1)S(1)} %all-to-all-done.refs_0_), channel_id=1, source_target_pairs={{0,2},{1,3},{2,0},{3,1},{4,6},{5,7},{6,4},{7,5},{8,10},{9,11},{10,... | collective-permute-start | bytes 983048 | tf_op jit(solution)/shard_map/ppermute | solution.py:19
  39.5 8.4 %collective-permute-start.3 = (bf16[8,32,512]{2,1,0:T(8,128)(2,1)S(1)}, bf16[8,32,512]{2,1,0:T(8,128)(2,1)S(1)}, u32[]{:S(2)}, u32[]{:S(2)}) collective-permute-start(bf16[8,32,512]{2,1,0:T(8,128)(2,1)S(1)} %all-to-all-done.1.refs_4_), channel_id=1, source_target_pairs={{0,1},{1,0},{2,3},{3,2},{4,5},{5,4},{6,7},{7,6},{8,9},{9,8},{10,11... | collective-permute-start | bytes 786440 | tf_op jit(solution)/shard_map/ppermute | solution.py:19
  39.5 9.1 %collective-permute-start = (bf16[8,32,640]{2,1,0:T(8,128)(2,1)S(1)}, bf16[8,32,640]{2,1,0:T(8,128)(2,1)S(1)}, u32[]{:S(2)}, u32[]{:S(2)}) collective-permute-start(bf16[8,32,640]{2,1,0:T(8,128)(2,1)S(1)} %all-to-all-done.refs_0_), channel_id=1, source_target_pairs={{0,1},{1,0},{2,3},{3,2},{4,5},{5,4},{6,7},{7,6},{8,9},{9,8},{10,11... | collective-permute-start | bytes 983048 | tf_op jit(solution)/shard_map/ppermute | solution.py:19
  40.1 9.2 %copy-start.22 = (bf16[8,32,512]{2,1,0:T(8,128)(2,1)}, bf16[8,32,512]{2,1,0:T(8,128)(2,1)S(1)}, u32[]{:S(2)}) copy-start(bf16[8,32,512]{2,1,0:T(8,128)(2,1)S(1)} %collective-permute-done.4.refs_6_) | copy-start | bytes 786436
  40.1 8.5 %collective-permute-start.5 = (bf16[8,32,512]{2,1,0:T(8,128)(2,1)S(1)}, bf16[8,32,512]{2,1,0:T(8,128)(2,1)S(1)}, u32[]{:S(2)}, u32[]{:S(2)}) collective-permute-start(bf16[8,32,512]{2,1,0:T(8,128)(2,1)S(1)} %collective-permute-done.4.refs_6_), channel_id=1, source_target_pairs={{0,1},{1,0},{2,3},{3,2},{4,5},{5,4},{6,7},{7,6},{8,9},{9,8},{10,11... | collective-permute-start | bytes 786440 | tf_op jit(solution)/shard_map/ppermute | solution.py:19
  46.7 21.8 %copy-start.15 = (bf16[8,32,640]{2,1,0:T(8,128)(2,1)}, bf16[8,32,640]{2,1,0:T(8,128)(2,1)S(1)}, u32[]{:S(2)}) copy-start(bf16[8,32,640]{2,1,0:T(8,128)(2,1)S(1)} %collective-permute-done.1.refs_2_) | copy-start | bytes 983044
  46.7 2.7 %collective-permute-start.2 = (bf16[8,32,640]{2,1,0:T(8,128)(2,1)S(1)}, bf16[8,32,640]{2,1,0:T(8,128)(2,1)S(1)}, u32[]{:S(2)}, u32[]{:S(2)}) collective-permute-start(bf16[8,32,640]{2,1,0:T(8,128)(2,1)S(1)} %collective-permute-done.1.refs_2_), channel_id=1, source_target_pairs={{0,1},{1,0},{2,3},{3,2},{4,5},{5,4},{6,7},{7,6},{8,9},{9,8},{10,11... | collective-permute-start | bytes 983048 | tf_op jit(solution)/shard_map/ppermute | solution.py:19
  48.6 19.9 %copy-start.17 = (bf16[8,32,640]{2,1,0:T(8,128)(2,1)}, bf16[8,32,640]{2,1,0:T(8,128)(2,1)S(1)}, u32[]{:S(2)}) copy-start(bf16[8,32,640]{2,1,0:T(8,128)(2,1)S(1)} %collective-permute-done.refs_1_) | copy-start | bytes 983044
  48.6 0.7 copy-start.28
  50.1 1.0 copy-start.20
  51.0 0.9 copy-start.23
  52.0 0.9 copy-start.26
  52.9 0.9 copy-start.29
  53.9 0.9 copy-start.31
  68.5 7.3 %copy-start.5 = (f32[256,3072]{1,0:T(8,128)}, f32[256,3072]{1,0:T(8,128)S(1)}, u32[]{:S(2)}) copy-start(f32[256,3072]{1,0:T(8,128)S(1)} %get-tuple-element.7.slope_ref) | copy-start | bytes 9437188
  75.8 20.9 %collective-permute-start.6 = (bf16[2,256,1024]{2,1,0:T(8,128)(2,1)S(1)}, bf16[2,256,1024]{2,1,0:T(8,128)(2,1)}, u32[]{:S(2)}, u32[]{:S(2)}) collective-permute-start(bf16[2,256,1024]{2,1,0:T(8,128)(2,1)S(1)} %mix_odd.1.refs_0_), channel_id=1, source_target_pairs={{0,1},{1,0},{2,3},{3,2},{4,5},{5,4},{6,7},{7,6},{8,9},{9,8},{10,11... | collective-permute-start | bytes 3145736 | tf_op jit(solution)/shard_map/ppermute | solution.py:19
  76.4 23.2 %copy-start = (bf16[8,32,1024]{2,1,0:T(8,128)(2,1)}, bf16[8,32,1024]{2,1,0:T(8,128)(2,1)S(1)}, u32[]{:S(2)}) copy-start(bf16[8,32,1024]{2,1,0:T(8,128)(2,1)S(1)} %all-to-all-done.3.refs_0_) | copy-start | bytes 1572868
  76.4 23.2 %copy-start.6 = (f32[256,3072]{1,0:T(8,128)S(1)}, f32[256,3072]{1,0:T(8,128)}, u32[]{:S(2)}) copy-start(f32[256,3072]{1,0:T(8,128)} %copy-done.5) | copy-start | bytes 9437188
  76.4 13.9 %collective-permute-start.9 = (bf16[8,32,1024]{2,1,0:T(8,128)(2,1)S(1)}, bf16[8,32,1024]{2,1,0:T(8,128)(2,1)S(1)}, u32[]{:S(2)}, u32[]{:S(2)}) collective-permute-start(bf16[8,32,1024]{2,1,0:T(8,128)(2,1)S(1)} %all-to-all-done.3.refs_0_), channel_id=1, source_target_pairs={{0,2},{1,3},{2,0},{3,1},{4,6},{5,7},{6,4},{7,5},{8,10},{9,11},{10,... | collective-permute-start | bytes 1572872 | tf_op jit(solution)/shard_map/ppermute | solution.py:19
  77.9 21.6 %collective-permute-start.8 = (bf16[8,32,1024]{2,1,0:T(8,128)(2,1)S(1)}, bf16[8,32,1024]{2,1,0:T(8,128)(2,1)S(1)}, u32[]{:S(2)}, u32[]{:S(2)}) collective-permute-start(bf16[8,32,1024]{2,1,0:T(8,128)(2,1)S(1)} %all-to-all-done.3.refs_0_), channel_id=1, source_target_pairs={{0,1},{1,0},{2,3},{3,2},{4,5},{5,4},{6,7},{7,6},{8,9},{9,8},{10,11... | collective-permute-start | bytes 1572872 | tf_op jit(solution)/shard_map/ppermute | solution.py:19
  90.3 23.6 %copy-start.9 = (bf16[8,32,1024]{2,1,0:T(8,128)(2,1)}, bf16[8,32,1024]{2,1,0:T(8,128)(2,1)S(1)}, u32[]{:S(2)}) copy-start(bf16[8,32,1024]{2,1,0:T(8,128)(2,1)S(1)} %collective-permute-done.9.refs_2_) | copy-start | bytes 1572868
  90.3 9.2 %collective-permute-start.10 = (bf16[8,32,1024]{2,1,0:T(8,128)(2,1)S(1)}, bf16[8,32,1024]{2,1,0:T(8,128)(2,1)S(1)}, u32[]{:S(2)}, u32[]{:S(2)}) collective-permute-start(bf16[8,32,1024]{2,1,0:T(8,128)(2,1)S(1)} %collective-permute-done.9.refs_2_), channel_id=1, source_target_pairs={{0,1},{1,0},{2,3},{3,2},{4,5},{5,4},{6,7},{7,6},{8,9},{9,8},{10,11... | collective-permute-start | bytes 1572872 | tf_op jit(solution)/shard_map/ppermute | solution.py:19
  98.0 16.0 %collective-permute-start.7 = (bf16[256,1024]{1,0:T(8,128)(2,1)S(1)}, bf16[256,1024]{1,0:T(8,128)(2,1)S(1)}, u32[]{:S(2)}, u32[]{:S(2)}) collective-permute-start(bf16[256,1024]{1,0:T(8,128)(2,1)S(1)} %fusion.2.refs_5_), channel_id=1, source_target_pairs={{0,2},{1,3},{2,0},{3,1},{4,6},{5,7},{6,4},{7,5},{8,10},{9,11},{10,... | collective-permute-start | bytes 1572872 | tf_op jit(solution)/shard_map/ppermute | solution.py:19
  99.6 23.9 %copy-start.11 = (bf16[8,32,1024]{2,1,0:T(8,128)(2,1)}, bf16[8,32,1024]{2,1,0:T(8,128)(2,1)S(1)}, u32[]{:S(2)}) copy-start(bf16[8,32,1024]{2,1,0:T(8,128)(2,1)S(1)} %collective-permute-done.8.refs_1_) | copy-start | bytes 1572868
  99.6 23.9 %copy-start.13 = (bf16[8,32,1024]{2,1,0:T(8,128)(2,1)}, bf16[8,32,1024]{2,1,0:T(8,128)(2,1)S(1)}, u32[]{:S(2)}) copy-start(bf16[8,32,1024]{2,1,0:T(8,128)(2,1)S(1)} %collective-permute-done.10.refs_3_) | copy-start | bytes 1572868
  99.6 1.4 copy-start.1
  115.3 8.3 %copy-start.4 = (bf16[256,1024]{1,0:T(8,128)(2,1)}, bf16[256,1024]{1,0:T(8,128)(2,1)S(1)}, u32[]{:S(2)}) copy-start(bf16[256,1024]{1,0:T(8,128)(2,1)S(1)} %fusion.1.refs_0_) | copy-start | bytes 1572868
  123.4 13.8 %collective-permute-start.11 = (bf16[2,256,1024]{2,1,0:T(8,128)(2,1)}, bf16[2,256,1024]{2,1,0:T(8,128)(2,1)}, u32[]{:S(2)}, u32[]{:S(2)}) collective-permute-start(bf16[2,256,1024]{2,1,0:T(8,128)(2,1)} %back_odd.1.refs_0_), channel_id=1, source_target_pairs={{0,1},{1,0},{2,3},{3,2},{4,5},{5,4},{6,7},{7,6},{8,9},{9,8},{10,11... | collective-permute-start | bytes 3145736 | tf_op jit(solution)/shard_map/ppermute | solution.py:19
  123.6 21.0 %all-to-all-start.2 = ((bf16[8,32,1024]{2,1,0:T(8,128)(2,1)}), bf16[8,32,1024]{2,1,0:T(8,128)(2,1)}, u32[]{:S(2)}, u32[]{:S(2)}) async-start(bf16[8,32,1024]{2,1,0:T(8,128)(2,1)} %bitcast.19), calls=%async_computation.2 | async-start | bytes 1048576 | tf_op jit(solution)/shard_map/all_to_all | solution.py:38
  139.5 14.3 %collective-permute-start.12 = (bf16[256,1024]{1,0:T(8,128)(2,1)}, bf16[256,1024]{1,0:T(8,128)(2,1)}, u32[]{:S(2)}, u32[]{:S(2)}) collective-permute-start(bf16[256,1024]{1,0:T(8,128)(2,1)} %fusion.3.refs_4_), channel_id=1, source_target_pairs={{0,2},{1,3},{2,0},{3,1},{4,6},{5,7},{6,4},{7,5},{8,10},{9,11},{10,... | collective-permute-start | bytes 1572872 | tf_op jit(solution)/shard_map/ppermute | solution.py:19
  156.3 35.4 %all-to-all-start.4 = ((bf16[8,32,1024]{2,1,0:T(8,128)(2,1)}), bf16[8,32,1024]{2,1,0:T(8,128)(2,1)}, u32[]{:S(2)}, u32[]{:S(2)}) async-start(bf16[8,32,1024]{2,1,0:T(8,128)(2,1)} %bitcast.18), calls=%async_computation.4 | async-start | bytes 1048576 | tf_op jit(solution)/shard_map/all_to_all | solution.py:38
  161.9 1.0 copy-start.2
  163.0 1.0 copy-start.10
  164.0 1.0 copy-start.12
  165.1 1.0 copy-start.14
  166.1 11.8 %copy-start.3 = (bf16[256,1024]{1,0:T(8,128)(2,1)S(1)}, bf16[256,1024]{1,0:T(8,128)(2,1)}, u32[]{:S(2)}) copy-start(bf16[256,1024]{1,0:T(8,128)(2,1)} %fusion.refs_9_) | copy-start | bytes 1572868
  166.1 11.8 %copy-start.8 = (bf16[8,32,512]{2,1,0:T(8,128)(2,1)S(1)}, bf16[8,32,512]{2,1,0:T(8,128)(2,1)}, u32[]{:S(2)}) copy-start(bf16[8,32,512]{2,1,0:T(8,128)(2,1)} %copy-done.7) | copy-start | bytes 786436
  166.1 11.8 %copy-start.16 = (bf16[8,32,640]{2,1,0:T(8,128)(2,1)S(1)}, bf16[8,32,640]{2,1,0:T(8,128)(2,1)}, u32[]{:S(2)}) copy-start(bf16[8,32,640]{2,1,0:T(8,128)(2,1)} %copy-done.15) | copy-start | bytes 983044
  166.1 11.8 %copy-start.18 = (bf16[8,32,640]{2,1,0:T(8,128)(2,1)S(1)}, bf16[8,32,640]{2,1,0:T(8,128)(2,1)}, u32[]{:S(2)}) copy-start(bf16[8,32,640]{2,1,0:T(8,128)(2,1)} %copy-done.17) | copy-start | bytes 983044
  166.1 11.8 %copy-start.21 = (bf16[8,32,640]{2,1,0:T(8,128)(2,1)S(1)}, bf16[8,32,640]{2,1,0:T(8,128)(2,1)}, u32[]{:S(2)}) copy-start(bf16[8,32,640]{2,1,0:T(8,128)(2,1)} %copy-done.19) | copy-start | bytes 983044
  166.1 11.8 %copy-start.24 = (bf16[8,32,512]{2,1,0:T(8,128)(2,1)S(1)}, bf16[8,32,512]{2,1,0:T(8,128)(2,1)}, u32[]{:S(2)}) copy-start(bf16[8,32,512]{2,1,0:T(8,128)(2,1)} %copy-done.22) | copy-start | bytes 786436
  166.1 11.8 %copy-start.27 = (bf16[8,32,512]{2,1,0:T(8,128)(2,1)S(1)}, bf16[8,32,512]{2,1,0:T(8,128)(2,1)}, u32[]{:S(2)}) copy-start(bf16[8,32,512]{2,1,0:T(8,128)(2,1)} %copy-done.25) | copy-start | bytes 786436
  166.1 11.8 %copy-start.30 = (bf16[8,32,512]{2,1,0:T(8,128)(2,1)S(1)}, bf16[8,32,512]{2,1,0:T(8,128)(2,1)}, u32[]{:S(2)}) copy-start(bf16[8,32,512]{2,1,0:T(8,128)(2,1)} %copy-done.28) | copy-start | bytes 786436
  (2 other events, 1.4 us)

commit v4 on v3

v4 whole, which is shorter than its diff:
```python
import functools
import math

import jax
import jax.numpy as jnp
from jax import lax
from jax.experimental import pallas as pl
from jax.experimental.pallas import tpu as pltpu
from jax.sharding import PartitionSpec as P

MIB = 1024 * 1024
LANES = 128
F32 = jnp.float32
BF16 = jnp.bfloat16
EXACT = lax.Precision.HIGHEST
ANYWHERE = pl.BlockSpec(memory_space=pl.ANY)
DEPTH = 3


def swap(value, axis, bits):
    size = lax.axis_size(axis)
    return lax.ppermute(value, axis, [(i, i ^ bits) for i in range(size)])


def exchange_rows(blocks):
    return lax.all_to_all(blocks, "expert", split_axis=0, concat_axis=0, tiled=True)


def gather_chunks(value):
    chunks = {0: value}
    bit = lax.axis_size("tensor") // 2
    while bit:
        chunks.update({s | bit: swap(c, "tensor", bit) for s, c in list(chunks.items())})
        bit //= 2
    return [chunks[s] for s in range(len(chunks))]


def scatter_rows(value, rows):
    return jnp.sum(exchange_rows(value.reshape(-1, rows, value.shape[1])).astype(F32), axis=0)


def scatter_chunks(even, odd):
    size = lax.axis_size("tensor")
    got = swap(odd, "tensor", 1)
    parts = [even[i].astype(F32) + got[i].astype(F32) for i in range(size // 2)]
    bit, passed = 2, ()
    while bit < size:
        kept = []
        for i in range(len(parts) // 2):
            sent = parts[2 * i + 1].astype(BF16)
            passed = passed or (sent,)
            kept.append(parts[2 * i] + swap(sent, "tensor", bit).astype(F32))
        parts = kept
        bit *= 2
    return parts[0].astype(BF16), passed


def dot(a, b, dims=((1,), (0,)), precision=None):
    return lax.dot_general(
        a, b, (dims, ((), ())), precision=precision, preferred_element_type=F32
    )


def iota(shape, dim):
    return lax.broadcasted_iota(jnp.int32, shape, dim)


def flat_rows(part):
    return part.reshape(part.shape[0] * part.shape[1], part.shape[2])


def block(index, size):
    return pl.ds(pl.multiple_of(index * size, size), size)


def placed(space, shape, dtype=BF16):
    return space(shape, dtype)


def stream(copies, step, steps):
    @pl.when(step == 0)
    def _():
        for ahead in range(min(DEPTH - 1, steps)):
            for copy in copies(ahead):
                copy.start()

    @pl.when(step + DEPTH - 1 < steps)
    def _():
        for copy in copies(step + DEPTH - 1):
            copy.start()


def gather(to_row_ref, sources, held_ref, rows_ref, sems):
    copies = [
        pltpu.make_async_copy(
            source.at[:, :, pl.ds(0, held_ref.shape[3])], held_ref.at[s], sems.at[s]
        )
        for s, source in enumerate(sources)
    ]
    for copy in copies:
        copy.start()
    for s, copy in enumerate(copies):
        copy.wait()
        rows_ref[s] = dot(to_row_ref[...], flat_rows(held_ref[s])).astype(BF16)


def pack_kernel(me_ref, token_ref, routing_ref, gates_ref, out_ref):
    _, width = token_ref.shape
    top = routing_ref.shape[1]
    gates = gates_ref[...]
    high = gates.astype(BF16)
    middle = (gates - high.astype(F32)).astype(BF16)
    low = (gates - high.astype(F32) - middle.astype(F32)).astype(BF16)
    parts = (routing_ref[...].astype(F32).astype(BF16), high, middle, low)
    lanes = (top, LANES)
    packed = sum(
        dot(part, (iota(lanes, 0) + i * top == iota(lanes, 1)).astype(F32).astype(BF16))
        for i, part in enumerate(parts)
    ).astype(BF16)
    for group in range(out_ref.shape[0]):
        out_ref[group, :, :width] = token_ref[...]
        out_ref[group, :, width:] = packed


def repeat_kernel(me_ref, token_ref, *refs):
    out_ref = refs[-1]
    for group in range(out_ref.shape[0]):
        out_ref[group] = token_ref[...]


def plan_kernel(top, local, me_ref, packed_ref, to_token_ref, to_row_ref, gate_ref):
    total, rows = to_token_ref.shape
    room = rows // local
    packed = flat_rows(packed_ref[...]).astype(F32)
    chosen = packed[:, :top]
    value = sum(packed[:, i * top : (i + 1) * top] for i in (1, 2, 3))
    lane = iota((total, local), 1)
    match = jnp.zeros((total, local), F32)
    gate = jnp.zeros((total, local), F32)
    for e in range(local):
        hit = chosen == (me_ref[1] + e).astype(F32)
        here = lane == e
        found = jnp.sum(jnp.where(hit, 1.0, 0.0), axis=1, keepdims=True)
        match = jnp.where(here, found, match)
        gate = jnp.where(here, jnp.sum(jnp.where(hit, value, 0.0), axis=1, keepdims=True), gate)
    step = min(total, 256)
    earlier = (iota((step, step), 0) > iota((step, step), 1)).astype(F32).astype(BF16)
    spread = (iota((local, rows), 1) // room == iota((local, rows), 0)).astype(F32)
    count = jnp.zeros((1, local), F32)
    gates = jnp.zeros((rows, local), F32)
    for start in range(0, total, step):
        part = match[start : start + step]
        before = dot(earlier, part.astype(BF16)) + count
        count = count + jnp.sum(part, axis=0, keepdims=True)
        place = dot(jnp.where(part > 0.0, before, -1.0), spread, precision=EXACT)
        slot = (iota((step, rows), 1) % room).astype(F32)
        one_hot = jnp.where(place == slot, 1.0, 0.0)
        to_token_ref[start : start + step, :] = one_hot.astype(BF16)
        flipped = one_hot.T
        to_row_ref[:, start : start + step] = flipped.astype(BF16)
        gates = gates + dot(flipped, gate[start : start + step], precision=EXACT)
    own = iota((rows, local), 0) // room == iota((rows, local), 1)
    gate_ref[...] = jnp.sum(jnp.where(own, gates, 0.0), axis=1, keepdims=True)


def preact_kernel(n, steps, me_ref, to_row_ref, gate_ref, *refs):
    xs, w_ref = refs[:n], refs[n]
    act_ref, spread_ref, slope_ref, held_ref, rows_ref, x_sems, buffer, sems = refs[-8:]
    room, width = act_ref.shape[0], rows_ref.shape[2]
    e = pl.program_id(0)

    def copies(step):
        slot = step % DEPTH
        return [
            pltpu.make_async_copy(
                w_ref.at[step, block(me_ref[0] ^ s, width), :], buffer.at[slot, s], sems.at[slot, s]
            )
            for s in range(n)
        ]

    stream(copies, e, steps)

    @pl.when(e == 0)
    def _():
        gather(to_row_ref, xs, held_ref, rows_ref, x_sems)

    for copy in copies(e):
        copy.wait()
    pre = sum(dot(rows_ref[s, block(e, room), :], buffer[e % DEPTH, s]) for s in range(n))
    sig = jax.nn.sigmoid(pre)
    gate = gate_ref[...]
    act = (gate * (pre * sig)).astype(BF16)
    act_ref[...] = act
    spread_ref[...] = dot(to_row_ref[block(e, room), :], act, ((0,), (0,))).astype(BF16)
    slope_ref[...] = gate * (sig * (1.0 + pre * (1.0 - sig)))


def slope_kernel(n, steps, me_ref, to_row_ref, slope_ref, *refs):
    ys, w_ref = refs[:n], refs[n]
    grad_ref, spread_ref, held_ref, rows_ref, y_sems, buffer, sems = refs[-7:]
    room, hid = grad_ref.shape
    width = rows_ref.shape[2]
    e = pl.program_id(0)

    def copies(step):
        slot = step % DEPTH
        return [
            pltpu.make_async_copy(
                w_ref.at[block(step, hid), block(me_ref[0] ^ s, width)],
                buffer.at[slot, s],
                sems.at[slot, s],
            )
            for s in range(n)
        ]

    stream(copies, e, steps)

    @pl.when(e == 0)
    def _():
        gather(to_row_ref, ys, held_ref, rows_ref, y_sems)

    for copy in copies(e):
        copy.wait()
    grad = sum(
        dot(rows_ref[s, block(e, room), :], buffer[e % DEPTH, s], ((1,), (1,))) for s in range(n)
    )
    grad = (grad * slope_ref[...]).astype(BF16)
    grad_ref[...] = grad
    spread_ref[...] = dot(to_row_ref[block(e, room), :], grad, ((0,), (0,))).astype(BF16)


def column_block(me_ref, step, per, odd):
    return (me_ref[0] ^ (2 * (step // per) + odd)) * per + step % per


def mix_kernel(steps, per, odd, me_ref, to_token_ref, act_ref, w_ref, *refs):
    out_ref, rows_ref, buffer, sems = refs[-4:]
    _, local, hid, cols = buffer.shape
    room = rows_ref.shape[0] // local
    step = pl.program_id(0)

    def copies(step):
        slot = step % DEPTH
        columns = block(column_block(me_ref, step, per, odd), cols)
        return [
            pltpu.make_async_copy(
                w_ref.at[pl.ds(e * hid, hid), columns], buffer.at[slot, e], sems.at[slot, e]
            )
            for e in range(local)
        ]

    stream(copies, step, steps)
    for copy in copies(step):
        copy.wait()
    for e in range(local):
        here = slice(e * room, (e + 1) * room)
        rows_ref[here, :] = dot(act_ref[here, :], buffer[step % DEPTH, e]).astype(BF16)
    out_ref[0] = dot(to_token_ref[...], rows_ref[...]).astype(BF16)


def back_kernel(steps, per, odd, me_ref, to_token_ref, grad_ref, w_ref, *refs):
    out_ref, rows_ref, buffer, sems = refs[-4:]
    _, local, cols, _ = buffer.shape
    room = rows_ref.shape[0] // local
    step = pl.program_id(0)

    def copies(step):
        slot = step % DEPTH
        columns = block(column_block(me_ref, step, per, odd), cols)
        return [
            pltpu.make_async_copy(
                w_ref.at[e, columns, :], buffer.at[slot, e], sems.at[slot, e]
            )
            for e in range(local)
        ]

    stream(copies, step, steps)
    for copy in copies(step):
        copy.wait()
    for e in range(local):
        here = slice(e * room, (e + 1) * room)
        part = dot(grad_ref[here, :], buffer[step % DEPTH, e], ((1,), (1,)))
        rows_ref[here, :] = part.astype(BF16)
    out_ref[0] = dot(to_token_ref[...], rows_ref[...]).astype(BF16)


def drain(step, steps, out, buffer, sems):
    @pl.when(step == steps - 1)
    def _():
        for slot in range(min(2, steps)):
            for s in range(buffer.shape[1]):
                pltpu.make_async_copy(buffer.at[slot, s], out, sems.at[slot, s]).wait()


def write_step(step, steps, values, outs, buffer, sems):
    slot = step % 2

    @pl.when(step >= 2)
    def _():
        for s, out in enumerate(outs):
            pltpu.make_async_copy(buffer.at[slot, s], out, sems.at[slot, s]).wait()

    for s, value in enumerate(values()):
        buffer[slot, s] = value.astype(BF16)
    for s, out in enumerate(outs):
        pltpu.make_async_copy(buffer.at[slot, s], out, sems.at[slot, s]).start()
    drain(step, steps, outs[0], buffer, sems)


def d_out_kernel(n, steps, me_ref, act_ref, *refs):
    ys, (out_ref, buffer, sems) = refs[:n], refs[-3:]
    e = pl.program_id(0)
    _, n, hid, width = buffer.shape
    act = act_ref[...].T
    outs = [out_ref.at[block(e, hid), block(me_ref[0] ^ s, width)] for s in range(n)]

    def values():
        for s in range(n):
            yield dot(act, flat_rows(ys[s][...]))

    write_step(e, steps, values, outs, buffer, sems)


def d_in_kernel(n, steps, me_ref, grad_ref, *refs):
    xs, (out_ref, flipped, buffer, sems) = refs[:n], refs[-4:]
    e = pl.program_id(0)
    _, n, width, hid = buffer.shape

    @pl.when(e == 0)
    def _():
        for s in range(n):
            flipped[s] = flat_rows(xs[s][...]).T

    grad = grad_ref[...]
    outs = [out_ref.at[e, block(me_ref[0] ^ s, width), :] for s in range(n)]

    def values():
        for s in range(n):
            yield dot(flipped[s], grad)

    write_step(e, steps, values, outs, buffer, sems)


def call(kernel, name, grid, in_specs, out_specs, out_shape, args, flops, limit, scratch=(), after=()):
    moved = sum(a.size * a.dtype.itemsize for a in args)
    outs = out_shape if isinstance(out_shape, list) else [out_shape]
    moved += sum(math.prod(o.shape) * jnp.dtype(o.dtype).itemsize for o in outs)
    return pl.pallas_call(
        kernel,
        grid_spec=pltpu.PrefetchScalarGridSpec(
            num_scalar_prefetch=1,
            grid=grid,
            in_specs=in_specs + [ANYWHERE] * len(after),
            out_specs=out_specs,
            scratch_shapes=scratch,
        ),
        out_shape=out_shape,
        name=name,
        cost_estimate=pl.CostEstimate(flops=flops, bytes_accessed=moved, transcendentals=0),
        compiler_params=pltpu.CompilerParams(vmem_limit_bytes=limit * MIB),
    )(*args, *after)


def once(*shape):
    return pl.BlockSpec(shape, lambda *_: (0,) * len(shape), pipeline_mode=pl.Buffered(1))


def shards(tokens, cotangent, routing, gates, w_in, w_out):
    n = lax.axis_size("tensor")
    groups = lax.axis_size("expert")
    local, width, hid = w_in.shape
    rows, quarter = tokens.shape
    total = groups * rows
    top = routing.shape[1]
    room = groups * (rows // 4)
    slots = local * room
    tensor_index = lax.axis_index("tensor").astype(jnp.int32)
    first = lax.axis_index("expert").astype(jnp.int32) * local
    me = jnp.stack([tensor_index, first])
    big = total > 256
    flops = 2 * slots * hid * width
    limit = 56 if big else 36
    dense = jax.ShapeDtypeStruct((total, local * hid), BF16)
    packed = call(
        pack_kernel,
        "pack",
        (1,),
        [once(rows, quarter), once(rows, top), once(rows, top)],
        once(groups, rows, quarter + LANES),
        jax.ShapeDtypeStruct((groups, rows, quarter + LANES), BF16),
        (me, tokens, routing, gates),
        0,
        24 if big else 4,
    )
    left = exchange_rows(packed)
    xs = gather_chunks(left)
    whole = exchange_rows(
        call(
            repeat_kernel,
            "repeat",
            (1,),
            [once(rows, quarter)],
            once(groups, rows, quarter),
            jax.ShapeDtypeStruct((groups, rows, quarter), BF16),
            (me, cotangent),
            0,
            24 if big else 4,
            (),
            (left,),
        )
    )
    ys = gather_chunks(whole)
    to_token, to_row, gate = call(
        functools.partial(plan_kernel, top, local),
        "plan",
        (1,),
        [
            pl.BlockSpec(
                (groups, rows, LANES),
                lambda i, me: (0, 0, quarter // LANES),
                pipeline_mode=pl.Buffered(1),
            )
        ],
        [once(total, slots), once(slots, total), once(slots, 1)],
        [
            jax.ShapeDtypeStruct((total, slots), BF16),
            jax.ShapeDtypeStruct((slots, total), BF16),
            jax.ShapeDtypeStruct((slots, 1), F32),
        ],
        (me, left),
        0,
        48 if big else 6,
    )

    def ring(*shape):
        return [
            pltpu.VMEM((DEPTH, *shape), BF16),
            pltpu.SemaphoreType.DMA((DEPTH, shape[0])),
        ]

    chunk_specs = [once(groups, rows, quarter)] * n
    loose = [ANYWHERE] * (n + 1)
    row_block = pl.BlockSpec((room, hid), lambda e, me: (e, 0))
    dense_block = pl.BlockSpec((total, hid), lambda e, me: (0, e))
    row_shape = jax.ShapeDtypeStruct((slots, hid), BF16)
    gathered = [
        pltpu.VMEM((n, groups, rows, quarter), BF16),
        pltpu.VMEM((n, slots, quarter), BF16),
        pltpu.SemaphoreType.DMA((n,)),
    ]
    flat_out = w_out.reshape(local * hid, width)
    act, act_dense, slope = call(
        functools.partial(preact_kernel, n, local),
        "preact",
        (local,),
        [once(slots, total), pl.BlockSpec((room, 1), lambda e, me: (e, 0))] + loose,
        [row_block, dense_block, row_block],
        [row_shape, dense, jax.ShapeDtypeStruct((slots, hid), F32)],
        (me, to_row, gate, *xs, w_in),
        flops,
        limit,
        gathered + ring(n, quarter, hid),
        (whole,),
    )
    cols = min(512, quarter)
    per = quarter // cols
    steps = n // 2 * per

    def parts(kernel, name, held, weights, odd, after=()):
        shape = (local, hid, cols) if weights.ndim == 2 else (local, cols, hid)
        return call(
            functools.partial(kernel, steps, per, odd),
            name,
            (steps,),
            [once(total, slots), once(slots, hid), ANYWHERE],
            pl.BlockSpec((1, total, cols), lambda i, me: (i // per, 0, i % per)),
            jax.ShapeDtypeStruct((n // 2, total, quarter), BF16),
            (me, to_token, held, weights),
            flops // 2,
            limit,
            [pltpu.VMEM((slots, cols), BF16)] + ring(*shape),
            after,
        )

    mix_odd = parts(mix_kernel, "mix_odd", act, flat_out, 1)
    mix_even = parts(mix_kernel, "mix_even", act, flat_out, 0, (mix_odd,))
    mix_sum, mix_passed = scatter_chunks(mix_even, mix_odd)
    mixed = scatter_rows(mix_sum, rows).astype(BF16)

    grad, grad_dense = call(
        functools.partial(slope_kernel, n, local),
        "grad_preact",
        (local,),
        [once(slots, total), row_block] + loose,
        [row_block, dense_block],
        [row_shape, dense],
        (me, to_row, slope, *ys, flat_out),
        flops,
        limit,
        gathered + ring(n, hid, quarter),
        mix_passed,
    )

    back_odd = parts(back_kernel, "back_odd", grad, w_in, 1)
    back_even = parts(back_kernel, "back_even", grad, w_in, 0, (back_odd,))
    back_sum, back_passed = scatter_chunks(back_even, back_odd)
    d_tokens = scatter_rows(back_sum, rows).astype(BF16)

    sems = pltpu.SemaphoreType.DMA((2, n))
    d_w_out = call(
        functools.partial(d_out_kernel, n, local),
        "d_w_out",
        (local,),
        [dense_block] + chunk_specs,
        pl.BlockSpec(memory_space=pltpu.HBM),
        placed(pltpu.HBM, (local * hid, width)),
        (me, act_dense, *ys),
        2 * total * local * hid * width,
        limit,
        [pltpu.VMEM((2, n, hid, quarter), BF16), sems],
        (*back_passed, mix_sum),
    )
    d_w_in = call(
        functools.partial(d_in_kernel, n, local),
        "d_w_in",
        (local,),
        [dense_block] + chunk_specs,
        pl.BlockSpec(memory_space=pltpu.HBM),
        placed(pltpu.HBM, w_in.shape),
        (me, grad_dense, *xs),
        2 * total * local * hid * width,
        limit,
        [
            pltpu.VMEM((n, quarter, total), BF16),
            pltpu.VMEM((2, n, quarter, hid), BF16),
            sems,
        ],
        (back_sum,),
    )
    return mixed, d_tokens, d_w_in, d_w_out.reshape(w_out.shape)


def solution(mesh):
    rows = P("expert", "tensor")
    routes = P("expert", None)
    columns_in = P("expert", None, "tensor")
    rows_out = P("expert", "tensor", None)
    return jax.shard_map(
        shards,
        mesh=mesh,
        in_specs=(rows, rows, routes, routes, columns_in, rows_out),
        out_specs=(rows, rows, columns_in, rows_out),
        check_vma=False,
    )
```

time: 195 us -> 189 us (0.969)
  blocking collectives: 0 us -> 23.6 us
  starting transfers between devices: 33.8 us -> 17.5 us
  waiting for transfers between devices: 46.9 us -> 40.9 us
  other arithmetic: 12.4 us -> 7.24 us
  local copies, waits for them, and re-layouts: 17.5 us -> 12.8 us
  Pallas kernels: 81.8 us -> 85.2 us
    all_to_all x0 -> x1, blocking collectives: none -> 23.6 us  [exchange_rows(): lax.all_to_all(blocks, 'expert', split_axis=0, concat_axis=0, tiled=True)]
    all_to_all x5 -> x3, waiting for transfers between devices: 20.4 us -> 3.82 us  [exchange_rows(): lax.all_to_all(blocks, 'expert', split_axis=0, concat_axis=0, tiled=True)]
    all_to_all x5 -> x3, starting transfers between devices: 25.8 us -> 13.4 us  [exchange_rows(): lax.all_to_all(blocks, 'expert', split_axis=0, concat_axis=0, tiled=True)]
    ppermute x13 -> x10, waiting for transfers between devices: 26.5 us -> 37.1 us  [swap(): return lax.ppermute(value, axis, [(i, i ^ bits) for i in range(size)])]
    ppermute x13 -> x10, starting transfers between devices: 8.01 us -> 4.07 us  [swap(): return lax.ppermute(value, axis, [(i, i ^ bits) for i in range(size)])]
    pallas_call x8 -> x11, Pallas kernels: 81.8 us -> 85.2 us  [call(): pl.pallas_call(kernel, grid_spec=pltpu.PrefetchScalarGridSpec(num_scalar_...]
    broadcast_in_dim x3 -> x0, local copies, waits for them, and re-layouts: 3.21 us -> none  [gather_rows(): jnp.broadcast_to(value[None], (lax.axis_size('expert'), *value.shape))]
    unnamed x65 -> x46, local copies, waits for them, and re-layouts: 12.6 us -> 12.8 us
  transfers between devices with their start and end apart: 18 -> 13, of which waited for: 6 -> 5; matrix products, arithmetic and copies ran while one was open for 5% -> 3% of each run, Pallas kernels for 38% -> 24%
where the time goes in v4:
time: 189 us; the launch traced here: 188 us
  Pallas kernels  85.2 us (45%)
  waiting for transfers between devices  40.9 us (22%)
  blocking collectives  23.6 us (12%)
  starting transfers between devices  17.5 us (9%)
  local copies, waits for them, and re-layouts  12.8 us (7%)
  other arithmetic  7.24 us (4%)
    pallas_call x11, Pallas kernels, call(): pl.pallas_call(kernel, grid_spec=pltpu.PrefetchScalarGridSpec(num_scalar_...  85.2 us
    ppermute x10, waiting for transfers between devices, swap(): return lax.ppermute(value, axis, [(i, i ^ bits) for i in range(size)])  37.1 us
    all_to_all x1, blocking collectives, exchange_rows(): lax.all_to_all(blocks, 'expert', split_axis=0, concat_axis=0, tiled=True)  23.6 us
    all_to_all x3, starting transfers between devices, exchange_rows(): lax.all_to_all(blocks, 'expert', split_axis=0, concat_axis=0, tiled=True)  13.4 us
    unnamed x46, local copies, waits for them, and re-layouts  12.8 us
    ppermute x10, starting transfers between devices, swap(): return lax.ppermute(value, axis, [(i, i ^ bits) for i in range(size)])  4.07 us
    all_to_all x3, waiting for transfers between devices, exchange_rows(): lax.all_to_all(blocks, 'expert', split_axis=0, concat_axis=0, tiled=True)  3.82 us
  transfers between devices with their start and end apart: 13, of which 5 were waited for; matrix products, arithmetic and copies ran while one was open for 3% of the time, Pallas kernels for 24%

profile of v4, /device:TPU:0, one launch (start us, length us, event | category | flops | bytes accessed | tf_op | source)
XLA Modules:
  0.0 188.2 jit_solution(2409823894886860595)
XLA Ops:
  0.6 0.8 copy.10.routing_ref
  1.4 0.8 copy.11.gates_ref
  2.2 0.1 pad_add_fusion.me_ref
  2.2 0.8 copy-done.20
  3.1 0.7 pack.1
  3.8 23.6 %all_to_all.20.packed_ref.refs_0_ = bf16[8,32,1152]{2,1,0:T(8,128)(2,1)S(1)} all-to-all(bf16[8,32,1152]{2,1,0:T(8,128)(2,1)S(1)} %pack.1), channel_id=1, replica_groups=mesh['expert'=8,'tensor'=4] {'expert'}, dimensions={0} | all-to-all | bytes 1179648 | tf_op jit(solution)/shard_map/all_to_all | solution.py:26
  27.4 1.5 collective-permute-start.1
  28.9 0.8 copy-done.21
  29.7 1.4 repeat.1
  31.1 3.5 %all-to-all-start.1 = ((bf16[8,32,1024]{2,1,0:T(8,128)(2,1)}), bf16[8,32,1024]{2,1,0:T(8,128)(2,1)S(1)}, u32[]{:S(2)}, u32[]{:S(2)}) async-start(bf16[8,32,1024]{2,1,0:T(8,128)(2,1)} %repeat.1), calls=%async_computation.1 | async-start | bytes 1048576 | tf_op jit(solution)/shard_map/all_to_all | solution.py:26
  34.6 0.1 collective-permute-start
  34.7 6.6 %collective-permute-done.1.refs_2_ = bf16[8,32,1152]{2,1,0:T(8,128)(2,1)S(1)} collective-permute-done((bf16[8,32,1152]{2,1,0:T(8,128)(2,1)S(1)}, bf16[8,32,1152]{2,1,0:T(8,128)(2,1)S(1)}, u32[]{:S(2)}, u32[]{:S(2)}) %collective-permute-start.1) | collective-permute-done | bytes 589856 | tf_op jit(solution)/shard_map/ppermute | solution.py:22
  41.3 2.3 %plan.1 = (bf16[256,512]{1,0:T(8,128)(2,1)S(1)}, bf16[512,256]{1,0:T(8,128)(2,1)S(1)}, f32[512,1]{1,0:T(8,128)S(1)}) custom-call(s32[2]{0:T(128)S(1)} %pad_add_fusion.me_ref, bf16[8,32,1152]{2,1,0:T(8,128)(2,1)S(1)} %all_to_all.20.packed_ref.refs_0_), custom_call_target="tpu_custom_call" | custom-call | bytes 1116168 | tf_op jit(solution)/shard_map/plan/pallas_call | solution.py:348
  43.6 0.7 copy-done.18
  44.3 3.8 %all-to-all-done.1.refs_5_.refs_0_ = bf16[8,32,1024]{2,1,0:T(8,128)(2,1)S(1)} async-done(((bf16[8,32,1024]{2,1,0:T(8,128)(2,1)}), bf16[8,32,1024]{2,1,0:T(8,128)(2,1)S(1)}, u32[]{:S(2)}, u32[]{:S(2)}) %all-to-all-start.1) | async-done | bytes 524320 | tf_op jit(solution)/shard_map/all_to_all | solution.py:26
  48.1 1.1 copy-done.19
  49.2 10.6 %preact.1 = (bf16[512,384]{1,0:T(8,128)(2,1)S(1)}, bf16[256,3072]{1,0:T(8,128)(2,1)S(1)}, f32[512,384]{1,0:T(8,128)S(1)}) custom-call(s32[2]{0:T(128)S(1)} %pad_add_fusion.me_ref, bf16[512,256]{1,0:T(8,128)(2,1)S(1)} %get-tuple-element.13.to_row_ref, f32[512,1]{1,0:T(8,128)S(1)} %copy-done.19, bf16[8,32,1152]{2,1,0:T(8,128)(2,1)S(1)} %all_to_all.20.packed_ref.refs_0_, ...), custom_call_target="tpu_custom_call" | custom-call | flops 1610612736 | bytes 30541832 | tf_op jit(solution)/shard_map/preact/pallas_call | solution.py:348
  59.9 6.6 %mix_odd.1.refs_0_ = bf16[2,256,1024]{2,1,0:T(8,128)(2,1)S(1)} custom-call(s32[2]{0:T(128)S(1)} %pad_add_fusion.me_ref, bf16[256,512]{1,0:T(8,128)(2,1)S(1)} %get-tuple-element.12.to_token_ref, bf16[512,384]{1,0:T(8,128)(2,1)S(1)} %get-tuple-element.15.act_ref, bf16[3072,4096]{1,0:T(8,128)(2,1)} %bitcast.18), custom_call_target="tpu_custom_call" | custom-call | flops 805306368 | bytes 26869768 | tf_op jit(solution)/shard_map/mix_odd/pallas_call | solution.py:348
  66.5 0.1 collective-permute-start.3
  66.6 0.6 collective-permute-start.6
  67.2 0.2 collective-permute-start.5
  67.3 13.6 %collective-permute-done.6.refs_2_ = bf16[8,32,1024]{2,1,0:T(8,128)(2,1)S(1)} collective-permute-done((bf16[8,32,1024]{2,1,0:T(8,128)(2,1)S(1)}, bf16[8,32,1024]{2,1,0:T(8,128)(2,1)S(1)}, u32[]{:S(2)}, u32[]{:S(2)}) %collective-permute-start.6) | collective-permute-done | bytes 524320 | tf_op jit(solution)/shard_map/ppermute | solution.py:22
  80.9 6.6 %mix_even.1 = bf16[2,256,1024]{2,1,0:T(8,128)(2,1)S(1)} custom-call(s32[2]{0:T(128)S(1)} %pad_add_fusion.me_ref, bf16[256,512]{1,0:T(8,128)(2,1)S(1)} %get-tuple-element.12.to_token_ref, bf16[512,384]{1,0:T(8,128)(2,1)S(1)} %get-tuple-element.15.act_ref, bf16[3072,4096]{1,0:T(8,128)(2,1)} %bitcast.19, bf16[2,256,1024]{2,1,0:T(8,128)(2,1)S(1)} %mix_odd.1.refs_0_), custom_call_target="tpu_custom_call" | custom-call | flops 805306368 | bytes 26869768 | tf_op jit(solution)/shard_map/mix_even/pallas_call | solution.py:348
  87.6 0.2 fusion.2.refs_5_
  87.8 14.0 %grad_preact.1 = (bf16[512,384]{1,0:T(8,128)(2,1)S(1)}, bf16[256,3072]{1,0:T(8,128)(2,1)S(1)}) custom-call(s32[2]{0:T(128)S(1)} %pad_add_fusion.me_ref, bf16[512,256]{1,0:T(8,128)(2,1)S(1)} %get-tuple-element.13.to_row_ref, f32[512,384]{1,0:T(8,128)S(1)} %get-tuple-element.16.slope_ref, bf16[8,32,1024]{2,1,0:T(8,128)(2,1)S(1)} %all-to-all-done.1.refs_5_.refs_0_, ...), custom_call_target="tpu_custom_call" | custom-call | flops 1610612736 | bytes 30277640 | tf_op jit(solution)/shard_map/grad_preact/pallas_call | solution.py:348
  101.9 8.2 %back_odd.1.refs_0_ = bf16[2,256,1024]{2,1,0:T(8,128)(2,1)S(1)} custom-call(s32[2]{0:T(128)S(1)} %pad_add_fusion.me_ref, bf16[256,512]{1,0:T(8,128)(2,1)S(1)} %get-tuple-element.12.to_token_ref, bf16[512,384]{1,0:T(8,128)(2,1)S(1)} %get-tuple-element.17.grad_ref, bf16[8,4096,384]{2,1,0:T(8,128)(2,1)} %w_ref.3), custom_call_target="tpu_custom_call" | custom-call | flops 805306368 | bytes 26869768 | tf_op jit(solution)/shard_map/back_odd/pallas_call | solution.py:348
  110.2 0.6 collective-permute-start.8
  110.7 0.5 collective-permute-start.4
  111.2 8.2 %back_even.1 = bf16[2,256,1024]{2,1,0:T(8,128)(2,1)S(1)} custom-call(s32[2]{0:T(128)S(1)} %pad_add_fusion.me_ref, bf16[256,512]{1,0:T(8,128)(2,1)S(1)} %get-tuple-element.12.to_token_ref, bf16[512,384]{1,0:T(8,128)(2,1)S(1)} %get-tuple-element.17.grad_ref, bf16[8,4096,384]{2,1,0:T(8,128)(2,1)} %w_ref.3, bf16[2,256,1024]{2,1,0:T(8,128)(2,1)S(1)} %back_odd.1.refs_0_), custom_call_target="tpu_custom_call" | custom-call | flops 805306368 | bytes 26869768 | tf_op jit(solution)/shard_map/back_even/pallas_call | solution.py:348
  119.5 5.2 %collective-permute-done.4 = bf16[256,1024]{1,0:T(8,128)(2,1)S(1)} collective-permute-done((bf16[256,1024]{1,0:T(8,128)(2,1)S(1)}, bf16[256,1024]{1,0:T(8,128)(2,1)S(1)}, u32[]{:S(2)}, u32[]{:S(2)}) %collective-permute-start.4) | collective-permute-done | bytes 524320 | tf_op jit(solution)/shard_map/ppermute | solution.py:22
  124.6 1.1 fusion.1.refs_5_
  125.7 4.1 %all-to-all-start.2 = ((bf16[8,32,1024]{2,1,0:T(8,128)(2,1)}), bf16[8,32,1024]{2,1,0:T(8,128)(2,1)}, u32[]{:S(2)}, u32[]{:S(2)}) async-start(bf16[8,32,1024]{2,1,0:T(8,128)(2,1)} %bitcast.5), calls=%async_computation.2 | async-start | bytes 1048576 | tf_op jit(solution)/shard_map/all_to_all | solution.py:26
  129.9 1.3 fusion.3.refs_4_
  131.2 0.6 collective-permute-start.9
  131.8 0.8 copy-done.12
  132.6 11.8 %collective-permute-done.9 = bf16[256,1024]{1,0:T(8,128)(2,1)S(1)} collective-permute-done((bf16[256,1024]{1,0:T(8,128)(2,1)S(1)}, bf16[256,1024]{1,0:T(8,128)(2,1)S(1)}, u32[]{:S(2)}, u32[]{:S(2)}) %collective-permute-start.9) | collective-permute-done | bytes 524320 | tf_op jit(solution)/shard_map/ppermute | solution.py:22
  144.4 2.1 %fusion.refs_4_ = bf16[256,1024]{1,0:T(8,128)(2,1)} fusion(bf16[256,1024]{1,0:T(8,128)(2,1)S(1)} %collective-permute-done.9, bf16[2,256,1024]{2,1,0:T(8,128)(2,1)} %collective-permute-done.8, bf16[2,256,1024]{2,1,0:T(8,128)(2,1)S(1)} %back_even.1), kind=kLoop, calls=%fused_computation.1 | loop fusion | flops 1572864 | bytes 2097152 | tf_op jit(solution)/shard_map/convert_element_type | solution.py:55
  146.5 5.7 %all-to-all-start.3 = ((bf16[8,32,1024]{2,1,0:T(8,128)(2,1)}), bf16[8,32,1024]{2,1,0:T(8,128)(2,1)S(1)}, u32[]{:S(2)}, u32[]{:S(2)}) async-start(bf16[8,32,1024]{2,1,0:T(8,128)(2,1)} %bitcast.8), calls=%async_computation.3 | async-start | bytes 1048576 | tf_op jit(solution)/shard_map/all_to_all | solution.py:26
  152.2 1.0 copy-done.7
  153.3 1.0 copy-done.9
  154.3 1.0 copy-done.11
  155.3 1.0 copy-done.13
  156.4 1.4 copy-done.15
  157.8 12.3 %d_w_out.1 = bf16[3072,4096]{1,0:T(8,128)(2,1)} custom-call(s32[2]{0:T(128)S(1)} %pad_add_fusion.me_ref, bf16[256,3072]{1,0:T(8,128)(2,1)S(1)} %copy-done.15, bf16[8,32,1024]{2,1,0:T(8,128)(2,1)S(1)} %all-to-all-done.1.refs_5_.refs_0_, bf16[8,32,1024]{2,1,0:T(8,128)(2,1)S(1)} %copy-done.9, bf16[8,32,1024]{2,1,0:T(8,128)(2,1)S(1)} %copy-done.7, ...), custom_call_target="tpu_custom_call" | custom-call | flops 6442450944 | bytes 28835848 | tf_op jit(solution)/shard_map/d_w_out/pallas_call | solution.py:348
  170.1 1.8 reduce_sum.24
  171.9 1.4 copy-done.17
  173.3 14.2 %d_w_in.1 = bf16[8,4096,384]{2,1,0:T(8,128)(2,1)} custom-call(s32[2]{0:T(128)S(1)} %pad_add_fusion.me_ref, bf16[256,3072]{1,0:T(8,128)(2,1)S(1)} %copy-done.17, bf16[8,32,1152]{2,1,0:T(8,128)(2,1)S(1)} %all_to_all.20.packed_ref.refs_0_, bf16[8,32,1152]{2,1,0:T(8,128)(2,1)S(1)} %copy-done.3, bf16[8,32,1152]{2,1,0:T(8,128)(2,1)S(1)} %copy-done.1, ...), custom_call_target="tpu_custom_call" | custom-call | flops 6442450944 | bytes 29097992 | tf_op jit(solution)/shard_map/d_w_in/pallas_call | solution.py:348
  187.5 0.7 reduce_sum.25
  (43 shorter events, 0.1 us)
Async XLA Ops:
  2.2 0.8 copy-start.20
  27.4 13.9 %collective-permute-start.1 = (bf16[8,32,1152]{2,1,0:T(8,128)(2,1)S(1)}, bf16[8,32,1152]{2,1,0:T(8,128)(2,1)S(1)}, u32[]{:S(2)}, u32[]{:S(2)}) collective-permute-start(bf16[8,32,1152]{2,1,0:T(8,128)(2,1)S(1)} %all_to_all.20.packed_ref.refs_0_), channel_id=1, source_target_pairs={{0,2},{1,3},{2,0},{3,1},{4,6},{5,7},{6,4},{7,5},{8,10},{9,11},{10,... | collective-permute-start | bytes 1769480 | tf_op jit(solution)/shard_map/ppermute | solution.py:22
  28.9 0.8 copy-start.21
  31.1 17.0 %all-to-all-start.1 = ((bf16[8,32,1024]{2,1,0:T(8,128)(2,1)}), bf16[8,32,1024]{2,1,0:T(8,128)(2,1)S(1)}, u32[]{:S(2)}, u32[]{:S(2)}) async-start(bf16[8,32,1024]{2,1,0:T(8,128)(2,1)} %repeat.1), calls=%async_computation.1 | async-start | bytes 1048576 | tf_op jit(solution)/shard_map/all_to_all | solution.py:26
  34.6 9.7 %collective-permute-start = (bf16[8,32,1152]{2,1,0:T(8,128)(2,1)S(1)}, bf16[8,32,1152]{2,1,0:T(8,128)(2,1)S(1)}, u32[]{:S(2)}, u32[]{:S(2)}) collective-permute-start(bf16[8,32,1152]{2,1,0:T(8,128)(2,1)S(1)} %all_to_all.20.packed_ref.refs_0_), channel_id=1, source_target_pairs={{0,1},{1,0},{2,3},{3,2},{4,5},{5,4},{6,7},{7,6},{8,9},{9,8},{10,11... | collective-permute-start | bytes 1769480 | tf_op jit(solution)/shard_map/ppermute | solution.py:22
  41.3 25.2 %copy-start = (bf16[8,32,1152]{2,1,0:T(8,128)(2,1)}, bf16[8,32,1152]{2,1,0:T(8,128)(2,1)S(1)}, u32[]{:S(2)}) copy-start(bf16[8,32,1152]{2,1,0:T(8,128)(2,1)S(1)} %collective-permute-done.1.refs_2_) | copy-start | bytes 1769476
  41.3 6.8 %collective-permute-start.2 = (bf16[8,32,1152]{2,1,0:T(8,128)(2,1)S(1)}, bf16[8,32,1152]{2,1,0:T(8,128)(2,1)S(1)}, u32[]{:S(2)}, u32[]{:S(2)}) collective-permute-start(bf16[8,32,1152]{2,1,0:T(8,128)(2,1)S(1)} %collective-permute-done.1.refs_2_), channel_id=1, source_target_pairs={{0,1},{1,0},{2,3},{3,2},{4,5},{5,4},{6,7},{7,6},{8,9},{9,8},{10,11... | collective-permute-start | bytes 1769480 | tf_op jit(solution)/shard_map/ppermute | solution.py:22
  43.6 0.7 copy-start.18
  44.3 22.2 %copy-start.2 = (bf16[8,32,1152]{2,1,0:T(8,128)(2,1)}, bf16[8,32,1152]{2,1,0:T(8,128)(2,1)S(1)}, u32[]{:S(2)}) copy-start(bf16[8,32,1152]{2,1,0:T(8,128)(2,1)S(1)} %collective-permute-done.refs_1_) | copy-start | bytes 1769476
  48.1 18.4 %copy-start.4 = (bf16[8,32,1152]{2,1,0:T(8,128)(2,1)}, bf16[8,32,1152]{2,1,0:T(8,128)(2,1)S(1)}, u32[]{:S(2)}) copy-start(bf16[8,32,1152]{2,1,0:T(8,128)(2,1)S(1)} %collective-permute-done.2.refs_3_) | copy-start | bytes 1769476
  48.1 1.1 copy-start.19
  59.8 27.7 %copy-start.14 = (bf16[256,3072]{1,0:T(8,128)(2,1)}, bf16[256,3072]{1,0:T(8,128)(2,1)S(1)}, u32[]{:S(2)}) copy-start(bf16[256,3072]{1,0:T(8,128)(2,1)S(1)} %get-tuple-element.19.act_ref) | copy-start | bytes 4718596
  66.5 21.1 %collective-permute-start.3 = (bf16[2,256,1024]{2,1,0:T(8,128)(2,1)S(1)}, bf16[2,256,1024]{2,1,0:T(8,128)(2,1)S(1)}, u32[]{:S(2)}, u32[]{:S(2)}) collective-permute-start(bf16[2,256,1024]{2,1,0:T(8,128)(2,1)S(1)} %mix_odd.1.refs_0_), channel_id=1, source_target_pairs={{0,1},{1,0},{2,3},{3,2},{4,5},{5,4},{6,7},{7,6},{8,9},{9,8},{10,11... | collective-permute-start | bytes 3145736 | tf_op jit(solution)/shard_map/ppermute | solution.py:22
  66.6 14.3 %collective-permute-start.6 = (bf16[8,32,1024]{2,1,0:T(8,128)(2,1)S(1)}, bf16[8,32,1024]{2,1,0:T(8,128)(2,1)S(1)}, u32[]{:S(2)}, u32[]{:S(2)}) collective-permute-start(bf16[8,32,1024]{2,1,0:T(8,128)(2,1)S(1)} %all-to-all-done.1.refs_5_.refs_0_), channel_id=1, source_target_pairs={{0,2},{1,3},{2,0},{3,1},{4,6},{5,7},{6,4},{7,5},{8,10},{9,11},{10,... | collective-permute-start | bytes 1572872 | tf_op jit(solution)/shard_map/ppermute | solution.py:22
  67.2 20.6 %collective-permute-start.5 = (bf16[8,32,1024]{2,1,0:T(8,128)(2,1)S(1)}, bf16[8,32,1024]{2,1,0:T(8,128)(2,1)S(1)}, u32[]{:S(2)}, u32[]{:S(2)}) collective-permute-start(bf16[8,32,1024]{2,1,0:T(8,128)(2,1)S(1)} %all-to-all-done.1.refs_5_.refs_0_), channel_id=1, source_target_pairs={{0,1},{1,0},{2,3},{3,2},{4,5},{5,4},{6,7},{7,6},{8,9},{9,8},{10,11... | collective-permute-start | bytes 1572872 | tf_op jit(solution)/shard_map/ppermute | solution.py:22
  80.9 20.9 %copy-start.6 = (bf16[8,32,1024]{2,1,0:T(8,128)(2,1)}, bf16[8,32,1024]{2,1,0:T(8,128)(2,1)S(1)}, u32[]{:S(2)}) copy-start(bf16[8,32,1024]{2,1,0:T(8,128)(2,1)S(1)} %collective-permute-done.6.refs_2_) | copy-start | bytes 1572868
  80.9 6.9 %collective-permute-start.7 = (bf16[8,32,1024]{2,1,0:T(8,128)(2,1)S(1)}, bf16[8,32,1024]{2,1,0:T(8,128)(2,1)S(1)}, u32[]{:S(2)}, u32[]{:S(2)}) collective-permute-start(bf16[8,32,1024]{2,1,0:T(8,128)(2,1)S(1)} %collective-permute-done.6.refs_2_), channel_id=1, source_target_pairs={{0,1},{1,0},{2,3},{3,2},{4,5},{5,4},{6,7},{7,6},{8,9},{9,8},{10,11... | collective-permute-start | bytes 1572872 | tf_op jit(solution)/shard_map/ppermute | solution.py:22
  87.8 22.3 %copy-start.8 = (bf16[8,32,1024]{2,1,0:T(8,128)(2,1)}, bf16[8,32,1024]{2,1,0:T(8,128)(2,1)S(1)}, u32[]{:S(2)}) copy-start(bf16[8,32,1024]{2,1,0:T(8,128)(2,1)S(1)} %collective-permute-done.5.refs_1_) | copy-start | bytes 1572868
  87.8 22.3 %copy-start.10 = (bf16[8,32,1024]{2,1,0:T(8,128)(2,1)}, bf16[8,32,1024]{2,1,0:T(8,128)(2,1)S(1)}, u32[]{:S(2)}) copy-start(bf16[8,32,1024]{2,1,0:T(8,128)(2,1)S(1)} %collective-permute-done.7.refs_3_) | copy-start | bytes 1572868
  101.9 17.6 %copy-start.16 = (bf16[256,3072]{1,0:T(8,128)(2,1)}, bf16[256,3072]{1,0:T(8,128)(2,1)S(1)}, u32[]{:S(2)}) copy-start(bf16[256,3072]{1,0:T(8,128)(2,1)S(1)} %get-tuple-element.18.grad_ref) | copy-start | bytes 4718596
  110.2 19.7 %collective-permute-start.8 = (bf16[2,256,1024]{2,1,0:T(8,128)(2,1)S(1)}, bf16[2,256,1024]{2,1,0:T(8,128)(2,1)}, u32[]{:S(2)}, u32[]{:S(2)}) collective-permute-start(bf16[2,256,1024]{2,1,0:T(8,128)(2,1)S(1)} %back_odd.1.refs_0_), channel_id=1, source_target_pairs={{0,1},{1,0},{2,3},{3,2},{4,5},{5,4},{6,7},{7,6},{8,9},{9,8},{10,11... | collective-permute-start | bytes 3145736 | tf_op jit(solution)/shard_map/ppermute | solution.py:22
  110.7 13.9 %collective-permute-start.4 = (bf16[256,1024]{1,0:T(8,128)(2,1)S(1)}, bf16[256,1024]{1,0:T(8,128)(2,1)S(1)}, u32[]{:S(2)}, u32[]{:S(2)}) collective-permute-start(bf16[256,1024]{1,0:T(8,128)(2,1)S(1)} %fusion.2.refs_5_), channel_id=1, source_target_pairs={{0,2},{1,3},{2,0},{3,1},{4,6},{5,7},{6,4},{7,5},{8,10},{9,11},{10,... | collective-permute-start | bytes 1572872 | tf_op jit(solution)/shard_map/ppermute | solution.py:22
  125.7 20.8 %all-to-all-start.2 = ((bf16[8,32,1024]{2,1,0:T(8,128)(2,1)}), bf16[8,32,1024]{2,1,0:T(8,128)(2,1)}, u32[]{:S(2)}, u32[]{:S(2)}) async-start(bf16[8,32,1024]{2,1,0:T(8,128)(2,1)} %bitcast.5), calls=%async_computation.2 | async-start | bytes 1048576 | tf_op jit(solution)/shard_map/all_to_all | solution.py:26
  129.9 42.0 %copy-start.1 = (bf16[8,32,1152]{2,1,0:T(8,128)(2,1)S(1)}, bf16[8,32,1152]{2,1,0:T(8,128)(2,1)}, u32[]{:S(2)}) copy-start(bf16[8,32,1152]{2,1,0:T(8,128)(2,1)} %copy-done) | copy-start | bytes 1769476
  129.9 42.0 %copy-start.3 = (bf16[8,32,1152]{2,1,0:T(8,128)(2,1)S(1)}, bf16[8,32,1152]{2,1,0:T(8,128)(2,1)}, u32[]{:S(2)}) copy-start(bf16[8,32,1152]{2,1,0:T(8,128)(2,1)} %copy-done.2) | copy-start | bytes 1769476
  131.2 13.1 %collective-permute-start.9 = (bf16[256,1024]{1,0:T(8,128)(2,1)S(1)}, bf16[256,1024]{1,0:T(8,128)(2,1)S(1)}, u32[]{:S(2)}, u32[]{:S(2)}) collective-permute-start(bf16[256,1024]{1,0:T(8,128)(2,1)S(1)} %fusion.3.refs_4_), channel_id=1, source_target_pairs={{0,2},{1,3},{2,0},{3,1},{4,6},{5,7},{6,4},{7,5},{8,10},{9,11},{10,... | collective-permute-start | bytes 1572872 | tf_op jit(solution)/shard_map/ppermute | solution.py:22
  131.8 0.8 copy-start.12
  146.5 25.4 %copy-start.5 = (bf16[8,32,1152]{2,1,0:T(8,128)(2,1)S(1)}, bf16[8,32,1152]{2,1,0:T(8,128)(2,1)}, u32[]{:S(2)}) copy-start(bf16[8,32,1152]{2,1,0:T(8,128)(2,1)} %copy-done.4) | copy-start | bytes 1769476
  146.5 41.0 %all-to-all-start.3 = ((bf16[8,32,1024]{2,1,0:T(8,128)(2,1)}), bf16[8,32,1024]{2,1,0:T(8,128)(2,1)S(1)}, u32[]{:S(2)}, u32[]{:S(2)}) async-start(bf16[8,32,1024]{2,1,0:T(8,128)(2,1)} %bitcast.8), calls=%async_computation.3 | async-start | bytes 1048576 | tf_op jit(solution)/shard_map/all_to_all | solution.py:26
  152.2 1.0 copy-start.7
  153.3 1.0 copy-start.9
  154.3 1.0 copy-start.11
  155.3 1.0 copy-start.13
  156.4 1.4 copy-start.15
  171.9 1.4 copy-start.17

commit v5 on v4

--- a/solution.py
+++ b/solution.py
@@ -14,6 +14,7 @@
 BF16 = jnp.bfloat16
 EXACT = lax.Precision.HIGHEST
 ANYWHERE = pl.BlockSpec(memory_space=pl.ANY)
+IN_HBM = pl.BlockSpec(memory_space=pltpu.HBM)
 DEPTH = 3
 
 
@@ -37,22 +38,6 @@
 
 def scatter_rows(value, rows):
     return jnp.sum(exchange_rows(value.reshape(-1, rows, value.shape[1])).astype(F32), axis=0)
-
-
-def scatter_chunks(even, odd):
-    size = lax.axis_size("tensor")
-    got = swap(odd, "tensor", 1)
-    parts = [even[i].astype(F32) + got[i].astype(F32) for i in range(size // 2)]
-    bit, passed = 2, ()
-    while bit < size:
-        kept = []
-        for i in range(len(parts) // 2):
-            sent = parts[2 * i + 1].astype(BF16)
-            passed = passed or (sent,)
-            kept.append(parts[2 * i] + swap(sent, "tensor", bit).astype(F32))
-        parts = kept
-        bit *= 2
-    return parts[0].astype(BF16), passed
 
 
 def dot(a, b, dims=((1,), (0,)), precision=None):
@@ -222,9 +207,9 @@
     for copy in copies(e):
         copy.wait()
     grad = sum(
-        dot(rows_ref[s, block(e, room), :], buffer[e % DEPTH, s], ((1,), (1,))) for s in range(n)
-    )
-    grad = (grad * slope_ref[...]).astype(BF16)
+        dot(buffer[e % DEPTH, s], rows_ref[s, block(e, room), :], ((1,), (1,))) for s in range(n)
+    )
+    grad = (grad.T * slope_ref[...]).astype(BF16)
     grad_ref[...] = grad
     spread_ref[...] = dot(to_row_ref[block(e, room), :], grad, ((0,), (0,))).astype(BF16)
 
@@ -260,8 +245,9 @@
 
 def back_kernel(steps, per, odd, me_ref, to_token_ref, grad_ref, w_ref, *refs):
     out_ref, rows_ref, buffer, sems = refs[-4:]
-    _, local, cols, _ = buffer.shape
-    room = rows_ref.shape[0] // local
+    _, local, cols, hid = buffer.shape
+    room = rows_ref.shape[1] // local
+    group = 2 if room % 128 and local % 2 == 0 else 1
     step = pl.program_id(0)
 
     def copies(step):
@@ -277,11 +263,23 @@
     stream(copies, step, steps)
     for copy in copies(step):
         copy.wait()
-    for e in range(local):
-        here = slice(e * room, (e + 1) * room)
-        part = dot(grad_ref[here, :], buffer[step % DEPTH, e], ((1,), (1,)))
-        rows_ref[here, :] = part.astype(BF16)
-    out_ref[0] = dot(to_token_ref[...], rows_ref[...]).astype(BF16)
+    for first in range(0, local, group):
+        part = 0.0
+        for i in range(group):
+            here = slice((first + i) * room, (first + i + 1) * room)
+            blank = [jnp.zeros((room, hid), BF16)] * group
+            blank[i] = grad_ref[here, :]
+            part = part + dot(
+                buffer[step % DEPTH, first + i], jnp.concatenate(blank, axis=0), ((1,), (1,))
+            )
+        rows_ref[:, first * room : (first + group) * room] = part.astype(BF16)
+    out_ref[0] = dot(to_token_ref[...], rows_ref[...], ((1,), (1,))).astype(BF16)
+
+
+def add_kernel(count, me_ref, *refs):
+    parts, out_ref = refs[:count], refs[-1]
+    total = sum(part[...].reshape(out_ref.shape).astype(F32) for part in parts)
+    out_ref[...] = total.astype(BF16)
 
 
 def drain(step, steps, out, buffer, sems):
@@ -308,10 +306,11 @@
 
 
 def d_out_kernel(n, steps, me_ref, act_ref, *refs):
-    ys, (out_ref, buffer, sems) = refs[:n], refs[-3:]
+    ys, (out_ref, done_ref, buffer, sems) = refs[:n], refs[-4:]
     e = pl.program_id(0)
     _, n, hid, width = buffer.shape
     act = act_ref[...].T
+    done_ref[...] = jnp.zeros_like(done_ref)
     outs = [out_ref.at[block(e, hid), block(me_ref[0] ^ s, width)] for s in range(n)]
 
     def values():
@@ -379,7 +378,7 @@
     me = jnp.stack([tensor_index, first])
     big = total > 256
     flops = 2 * slots * hid * width
-    limit = 56 if big else 36
+    limit = 56 if big else 20
     dense = jax.ShapeDtypeStruct((total, local * hid), BF16)
     packed = call(
         pack_kernel,
@@ -439,7 +438,7 @@
         ]
 
     chunk_specs = [once(groups, rows, quarter)] * n
-    loose = [ANYWHERE] * (n + 1)
+    loose = [ANYWHERE] * n + [IN_HBM]
     row_block = pl.BlockSpec((room, hid), lambda e, me: (e, 0))
     dense_block = pl.BlockSpec((total, hid), lambda e, me: (0, e))
     row_shape = jax.ShapeDtypeStruct((slots, hid), BF16)
@@ -448,7 +447,10 @@
         pltpu.VMEM((n, slots, quarter), BF16),
         pltpu.SemaphoreType.DMA((n,)),
     ]
-    flat_out = w_out.reshape(local * hid, width)
+    w_in = pltpu.with_memory_space_constraint(w_in, pltpu.HBM)
+    flat_out = pltpu.with_memory_space_constraint(
+        w_out.reshape(local * hid, width), pltpu.HBM
+    )
     act, act_dense, slope = call(
         functools.partial(preact_kernel, n, local),
         "preact",
@@ -472,19 +474,66 @@
             functools.partial(kernel, steps, per, odd),
             name,
             (steps,),
-            [once(total, slots), once(slots, hid), ANYWHERE],
+            [once(total, slots), once(slots, hid), IN_HBM],
             pl.BlockSpec((1, total, cols), lambda i, me: (i // per, 0, i % per)),
             jax.ShapeDtypeStruct((n // 2, total, quarter), BF16),
             (me, to_token, held, weights),
             flops // 2,
             limit,
-            [pltpu.VMEM((slots, cols), BF16)] + ring(*shape),
+            [pltpu.VMEM((slots, cols) if weights.ndim == 2 else (cols, slots), BF16)] + ring(*shape),
             after,
         )
 
-    mix_odd = parts(mix_kernel, "mix_odd", act, flat_out, 1)
+    def add(name, values, specs, after=()):
+        return call(
+            functools.partial(add_kernel, len(values)),
+            name,
+            (1,),
+            specs,
+            once(total, quarter),
+            jax.ShapeDtypeStruct((total, quarter), BF16),
+            (me, *values),
+            0,
+            56 if big else 8,
+            (),
+            after,
+        )
+
+    def one_of(index):
+        shape = (1, total, quarter)
+        return pl.BlockSpec(shape, lambda i, me: (index, 0, 0), pipeline_mode=pl.Buffered(1))
+
+    def pass_on(name, even, odd):
+        got = swap(odd, "tensor", 1)
+        return got, {
+            i: add(f"{name}_{i}", (even, got), [one_of(i), one_of(i)]) for i in range(1, n // 2)
+        }
+
+    def gather_sum(name, even, got, sent, after=()):
+        values, specs = [even, got], [one_of(0), one_of(0)]
+        count = n // 2
+        bit = n // 2
+        held = dict(sent)
+        while count > 1:
+            half = count // 2
+            for i in range(half, count):
+                received = swap(held[i], "tensor", bit)
+                if i == half:
+                    values.append(received)
+                    specs.append(once(total, quarter))
+                else:
+                    held[i - half] = add(
+                        f"{name}_{i - half}_{bit}",
+                        (held[i - half], received),
+                        [once(total, quarter)] * 2,
+                    )
+            count, bit = half, bit // 2
+        return add(f"{name}_sum", values, specs, after)
+
+    mix_odd = parts(mix_kernel, "mix_odd", act, flat_out, 1, (ys[n // 2],))
     mix_even = parts(mix_kernel, "mix_even", act, flat_out, 0, (mix_odd,))
-    mix_sum, mix_passed = scatter_chunks(mix_even, mix_odd)
+    mix_got, mix_sent = pass_on("mix", mix_even, mix_odd)
+    mix_sum = gather_sum("mix", mix_even, mix_got, mix_sent)
     mixed = scatter_rows(mix_sum, rows).astype(BF16)
 
     grad, grad_dense = call(
@@ -498,34 +547,35 @@
         flops,
         limit,
         gathered + ring(n, hid, quarter),
-        mix_passed,
-    )
-
-    back_odd = parts(back_kernel, "back_odd", grad, w_in, 1)
+        tuple(mix_sent.values()),
+    )
+
+    back_odd = parts(back_kernel, "back_odd", grad, w_in, 1, (mix_sum,))
     back_even = parts(back_kernel, "back_even", grad, w_in, 0, (back_odd,))
-    back_sum, back_passed = scatter_chunks(back_even, back_odd)
-    d_tokens = scatter_rows(back_sum, rows).astype(BF16)
+    back_got, back_sent = pass_on("back", back_even, back_odd)
 
     sems = pltpu.SemaphoreType.DMA((2, n))
-    d_w_out = call(
+    d_w_out, done = call(
         functools.partial(d_out_kernel, n, local),
         "d_w_out",
         (local,),
         [dense_block] + chunk_specs,
-        pl.BlockSpec(memory_space=pltpu.HBM),
-        placed(pltpu.HBM, (local * hid, width)),
+        [IN_HBM, once(8, 128)],
+        [placed(pltpu.HBM, (local * hid, width)), jax.ShapeDtypeStruct((8, 128), F32)],
         (me, act_dense, *ys),
         2 * total * local * hid * width,
         limit,
         [pltpu.VMEM((2, n, hid, quarter), BF16), sems],
-        (*back_passed, mix_sum),
-    )
+        tuple(back_sent.values()),
+    )
+    back_sum = gather_sum("back", back_even, back_got, back_sent, (done,))
+    d_tokens = scatter_rows(back_sum, rows).astype(BF16)
     d_w_in = call(
         functools.partial(d_in_kernel, n, local),
         "d_w_in",
         (local,),
         [dense_block] + chunk_specs,
-        pl.BlockSpec(memory_space=pltpu.HBM),
+        IN_HBM,
         placed(pltpu.HBM, w_in.shape),
         (me, grad_dense, *xs),
         2 * total * local * hid * width,

time: 189 us -> 158 us (0.84)
  waiting for transfers between devices: 40.9 us -> 13.2 us
  local copies, waits for them, and re-layouts: 12.8 us -> 7.86 us
  other arithmetic: 7.24 us -> 2.55 us
  starting transfers between devices: 17.5 us -> 20.9 us
  Pallas kernels: 85.2 us -> 88.5 us
    ppermute x10, waiting for transfers between devices: 37.1 us -> 13.2 us  [swap(): return lax.ppermute(value, axis, [(i, i ^ bits) for i in range(size)])]
    unnamed x46 -> x42, local copies, waits for them, and re-layouts: 12.8 us -> 7.86 us
    convert_element_type x4 -> x0, other arithmetic: 4.69 us -> none  [the longest x2 3.18 us: scatter_chunks(): return (parts[0].astype(BF16), passed)]
    all_to_all x3, waiting for transfers between devices: 3.82 us -> 0.01 us  [exchange_rows(): lax.all_to_all(blocks, 'expert', split_axis=0, concat_axis=0, tiled=True)]
    pallas_call x11 -> x15, Pallas kernels: 85.2 us -> 88.5 us  [call(): pl.pallas_call(kernel, grid_spec=pltpu.PrefetchScalarGridSpec(num_scalar_...]
  transfers between devices with their start and end apart: 13 -> 13, of which waited for: 5 -> 3; matrix products, arithmetic and copies ran while one was open for 3% -> 1% of each run, Pallas kernels for 24% -> 45%
where the time goes in v5:
time: 158 us
  Pallas kernels  88.5 us (56%)
  blocking collectives  23.6 us (15%)
  starting transfers between devices  20.9 us (13%)
  waiting for transfers between devices  13.2 us (8%)
  local copies, waits for them, and re-layouts  7.86 us (5%)
  other arithmetic  2.55 us (2%)
    pallas_call x15, Pallas kernels, call(): pl.pallas_call(kernel, grid_spec=pltpu.PrefetchScalarGridSpec(num_scalar_...  88.5 us
    all_to_all x1, blocking collectives, exchange_rows(): lax.all_to_all(blocks, 'expert', split_axis=0, concat_axis=0, tiled=True)  23.6 us
    all_to_all x3, starting transfers between devices, exchange_rows(): lax.all_to_all(blocks, 'expert', split_axis=0, concat_axis=0, tiled=True)  15 us
    ppermute x10, waiting for transfers between devices, swap(): return lax.ppermute(value, axis, [(i, i ^ bits) for i in range(size)])  13.2 us
    unnamed x42, local copies, waits for them, and re-layouts  7.86 us
    ppermute x10, starting transfers between devices, swap(): return lax.ppermute(value, axis, [(i, i ^ bits) for i in range(size)])  5.93 us
  transfers between devices with their start and end apart: 13, of which 3 were waited for; matrix products, arithmetic and copies ran while one was open for 1% of the time, Pallas kernels for 45%

profile of v5, /device:TPU:0, one launch (start us, length us, event | category | flops | bytes accessed | tf_op | source)
XLA Modules:
  0.0 157.6 jit_solution(10644631274128528361)
XLA Ops:
  0.6 0.8 copy.10.routing_ref
  1.4 0.8 copy.11.gates_ref
  2.2 0.1 pad_add_fusion.me_ref
  2.2 0.8 copy-done.16
  3.1 0.7 pack.1
  3.8 23.6 %all_to_all.20.packed_ref.refs_0_ = bf16[8,32,1152]{2,1,0:T(8,128)(2,1)S(1)} all-to-all(bf16[8,32,1152]{2,1,0:T(8,128)(2,1)S(1)} %pack.1), channel_id=1, replica_groups=mesh['expert'=8,'tensor'=4] {'expert'}, dimensions={0} | all-to-all | bytes 1179648 | tf_op jit(solution)/shard_map/all_to_all | solution.py:27
  27.4 0.8 copy-done.17
  28.2 1.4 repeat.1
  29.6 3.5 %all-to-all-start.1 = ((bf16[8,32,1024]{2,1,0:T(8,128)(2,1)}), bf16[8,32,1024]{2,1,0:T(8,128)(2,1)S(1)}, u32[]{:S(2)}, u32[]{:S(2)}) async-start(bf16[8,32,1024]{2,1,0:T(8,128)(2,1)} %repeat.1), calls=%async_computation.1 | async-start | bytes 1048576 | tf_op jit(solution)/shard_map/all_to_all | solution.py:27
  33.1 1.6 %collective-permute-start.1 = (bf16[8,32,1152]{2,1,0:T(8,128)(2,1)S(1)}, bf16[8,32,1152]{2,1,0:T(8,128)(2,1)S(1)}, u32[]{:S(2)}, u32[]{:S(2)}) collective-permute-start(bf16[8,32,1152]{2,1,0:T(8,128)(2,1)S(1)} %all_to_all.20.packed_ref.refs_0_), channel_id=1, source_target_pairs={{0,2},{1,3},{2,0},{3,1},{4,6},{5,7},{6,4},{7,5},{8,10},{9,11},{10,... | collective-permute-start | bytes 1769480 | tf_op jit(solution)/shard_map/ppermute | solution.py:23
  34.7 0.0 collective-permute-start
  34.7 12.5 %collective-permute-done.1.refs_2_ = bf16[8,32,1152]{2,1,0:T(8,128)(2,1)S(1)} collective-permute-done((bf16[8,32,1152]{2,1,0:T(8,128)(2,1)S(1)}, bf16[8,32,1152]{2,1,0:T(8,128)(2,1)S(1)}, u32[]{:S(2)}, u32[]{:S(2)}) %collective-permute-start.1) | collective-permute-done | bytes 589856 | tf_op jit(solution)/shard_map/ppermute | solution.py:23
  47.2 0.0 collective-permute-start.2
  47.2 0.0 all-to-all-done.1.refs_5_.refs_0_
  47.2 1.6 %collective-permute-start.3 = (bf16[8,32,1024]{2,1,0:T(8,128)(2,1)S(1)}, bf16[8,32,1024]{2,1,0:T(8,128)(2,1)S(1)}, u32[]{:S(2)}, u32[]{:S(2)}) collective-permute-start(bf16[8,32,1024]{2,1,0:T(8,128)(2,1)S(1)} %all-to-all-done.1.refs_5_.refs_0_), channel_id=1, source_target_pairs={{0,2},{1,3},{2,0},{3,1},{4,6},{5,7},{6,4},{7,5},{8,10},{9,11},{10,... | collective-permute-start | bytes 1572872 | tf_op jit(solution)/shard_map/ppermute | solution.py:23
  48.7 2.3 %plan.1 = (bf16[256,512]{1,0:T(8,128)(2,1)S(1)}, bf16[512,256]{1,0:T(8,128)(2,1)S(1)}, f32[512,1]{1,0:T(8,128)S(1)}) custom-call(s32[2]{0:T(128)S(1)} %pad_add_fusion.me_ref, bf16[8,32,1152]{2,1,0:T(8,128)(2,1)S(1)} %all_to_all.20.packed_ref.refs_0_), custom_call_target="tpu_custom_call" | custom-call | bytes 1116168 | tf_op jit(solution)/shard_map/plan/pallas_call | solution.py:347
  51.1 10.6 %preact.1 = (bf16[512,384]{1,0:T(8,128)(2,1)S(1)}, bf16[256,3072]{1,0:T(8,128)(2,1)S(1)}, f32[512,384]{1,0:T(8,128)S(1)}) custom-call(s32[2]{0:T(128)S(1)} %pad_add_fusion.me_ref, bf16[512,256]{1,0:T(8,128)(2,1)S(1)} %get-tuple-element.15.to_row_ref, f32[512,1]{1,0:T(8,128)S(1)} %get-tuple-element.16.gate_ref, ...), custom_call_target="tpu_custom_call" | custom-call | flops 1610612736 | bytes 30541832 | tf_op jit(solution)/shard_map/preact/pallas_call | solution.py:347
  61.7 0.0 copy-start.18
  61.7 1.1 copy-done.18
  62.8 6.6 %mix_odd.1.refs_0_ = bf16[2,256,1024]{2,1,0:T(8,128)(2,1)S(1)} custom-call(s32[2]{0:T(128)S(1)} %pad_add_fusion.me_ref, bf16[256,512]{1,0:T(8,128)(2,1)S(1)} %get-tuple-element.14.to_token_ref, bf16[512,384]{1,0:T(8,128)(2,1)S(1)} %get-tuple-element.17.act_ref, bf16[3072,4096]{1,0:T(8,128)(2,1)} %bitcast.6, ...), custom_call_target="tpu_custom_call" | custom-call | flops 805306368 | bytes 26869768 | tf_op jit(solution)/shard_map/mix_odd/pallas_call | solution.py:347
  69.5 0.2 collective-permute-start.4
  69.7 0.4 collective-permute-start.6
  70.1 0.2 collective-permute-start.7
  70.2 6.6 %mix_even.1.refs_0_ = bf16[2,256,1024]{2,1,0:T(8,128)(2,1)S(1)} custom-call(s32[2]{0:T(128)S(1)} %pad_add_fusion.me_ref, bf16[256,512]{1,0:T(8,128)(2,1)S(1)} %get-tuple-element.14.to_token_ref, bf16[512,384]{1,0:T(8,128)(2,1)S(1)} %get-tuple-element.17.act_ref, bf16[3072,4096]{1,0:T(8,128)(2,1)} %bitcast.7, bf16[2,256,1024]{2,1,0:T(8,128)(2,1)S(1)} %mix_odd.1.refs_0_), custom_call_target="tpu_custom_call" | custom-call | flops 805306368 | bytes 26869768 | tf_op jit(solution)/shard_map/mix_even/pallas_call | solution.py:347
  76.9 0.7 mix_1.1.refs_5_
  77.5 0.6 collective-permute-start.5
  78.1 0.0 collective-permute-done.6.refs_1_
  78.1 0.0 collective-permute-done.7.refs_3_
  78.2 13.3 %grad_preact.1 = (bf16[512,384]{1,0:T(8,128)(2,1)S(1)}, bf16[256,3072]{1,0:T(8,128)(2,1)S(1)}) custom-call(s32[2]{0:T(128)S(1)} %pad_add_fusion.me_ref, bf16[512,256]{1,0:T(8,128)(2,1)S(1)} %get-tuple-element.15.to_row_ref, f32[512,384]{1,0:T(8,128)S(1)} %get-tuple-element.18.slope_ref, bf16[8,32,1024]{2,1,0:T(8,128)(2,1)S(1)} %all-to-all-done.1.refs_5_.refs_0_, ...), custom_call_target="tpu_custom_call" | custom-call | flops 1610612736 | bytes 30277640 | tf_op jit(solution)/shard_map/grad_preact/pallas_call | solution.py:347
  91.5 0.3 collective-permute-done.5.refs_2_
  91.8 1.6 mix_sum.1.refs_0_
  93.4 7.9 %back_odd.1.refs_0_ = bf16[2,256,1024]{2,1,0:T(8,128)(2,1)S(1)} custom-call(s32[2]{0:T(128)S(1)} %pad_add_fusion.me_ref, bf16[256,512]{1,0:T(8,128)(2,1)S(1)} %get-tuple-element.14.to_token_ref, bf16[512,384]{1,0:T(8,128)(2,1)S(1)} %get-tuple-element.19.grad_ref, bf16[8,4096,384]{2,1,0:T(8,128)(2,1)} %w_ref.3, bf16[256,1024]{1,0:T(8,128)(2,1)} %mix_sum.1.refs_0_), custom_call_target="tpu_custom_call" | custom-call | flops 805306368 | bytes 26869768 | tf_op jit(solution)/shard_map/back_odd/pallas_call | solution.py:347
  101.3 0.1 collective-permute-start.8
  101.4 5.7 %all-to-all-start.2 = ((bf16[8,32,1024]{2,1,0:T(8,128)(2,1)}), bf16[8,32,1024]{2,1,0:T(8,128)(2,1)}, u32[]{:S(2)}, u32[]{:S(2)}) async-start(bf16[8,32,1024]{2,1,0:T(8,128)(2,1)} %bitcast.3), calls=%async_computation.2 | async-start | bytes 1048576 | tf_op jit(solution)/shard_map/all_to_all | solution.py:27
  107.1 1.0 copy-done.11
  108.1 8.2 %back_even.1.refs_0_ = bf16[2,256,1024]{2,1,0:T(8,128)(2,1)S(1)} custom-call(s32[2]{0:T(128)S(1)} %pad_add_fusion.me_ref, bf16[256,512]{1,0:T(8,128)(2,1)S(1)} %get-tuple-element.14.to_token_ref, bf16[512,384]{1,0:T(8,128)(2,1)S(1)} %copy-done.11, bf16[8,4096,384]{2,1,0:T(8,128)(2,1)} %w_ref.3, bf16[2,256,1024]{2,1,0:T(8,128)(2,1)S(1)} %back_odd.1.refs_0_), custom_call_target="tpu_custom_call" | custom-call | flops 805306368 | bytes 26869768 | tf_op jit(solution)/shard_map/back_even/pallas_call | solution.py:347
  116.4 0.7 back_1.1.refs_4_
  117.0 1.4 collective-permute-start.9
  118.4 12.3 %d_w_out.1 = (bf16[3072,4096]{1,0:T(8,128)(2,1)}, f32[8,128]{1,0:T(8,128)S(1)}) custom-call(s32[2]{0:T(128)S(1)} %pad_add_fusion.me_ref, bf16[256,3072]{1,0:T(8,128)(2,1)S(1)} %copy-done.19, bf16[8,32,1024]{2,1,0:T(8,128)(2,1)S(1)} %all-to-all-done.1.refs_5_.refs_0_, bf16[8,32,1024]{2,1,0:T(8,128)(2,1)S(1)} %copy-done.13, ...), custom_call_target="tpu_custom_call" | custom-call | flops 6442450944 | bytes 28839944 | tf_op jit(solution)/shard_map/d_w_out/pallas_call | solution.py:347
  130.7 0.4 collective-permute-done.9.refs_2_
  131.1 1.5 back_sum.1.refs_4_
  132.7 0.0 all-to-all-done.2
  132.7 5.7 %all-to-all-start.3 = ((bf16[8,32,1024]{2,1,0:T(8,128)(2,1)}), bf16[8,32,1024]{2,1,0:T(8,128)(2,1)S(1)}, u32[]{:S(2)}, u32[]{:S(2)}) async-start(bf16[8,32,1024]{2,1,0:T(8,128)(2,1)} %bitcast.4), calls=%async_computation.3 | async-start | bytes 1048576 | tf_op jit(solution)/shard_map/all_to_all | solution.py:27
  138.4 1.8 %reduce_sum.24 = bf16[32,1024]{1,0:T(8,128)(2,1)} reduce(bf16[8,32,1024]{2,1,0:T(8,128)(2,1)} %all-to-all-done.2, bf16[]{:T(256)} %constant.14.clone.1), dimensions={0}, to_apply=%region_0.0 | reduce | flops 229376 | bytes 589826 | tf_op jit(solution)/shard_map/reduce_sum | solution.py:40
  140.2 1.1 copy-done.5
  141.2 1.4 copy-done.9
  142.6 14.2 %d_w_in.1 = bf16[8,4096,384]{2,1,0:T(8,128)(2,1)} custom-call(s32[2]{0:T(128)S(1)} %pad_add_fusion.me_ref, bf16[256,3072]{1,0:T(8,128)(2,1)S(1)} %copy-done.9, bf16[8,32,1152]{2,1,0:T(8,128)(2,1)S(1)} %all_to_all.20.packed_ref.refs_0_, bf16[8,32,1152]{2,1,0:T(8,128)(2,1)S(1)} %copy-done.3, bf16[8,32,1152]{2,1,0:T(8,128)(2,1)S(1)} %copy-done.1, ...), custom_call_target="tpu_custom_call" | custom-call | flops 6442450944 | bytes 29097992 | tf_op jit(solution)/shard_map/d_w_in/pallas_call | solution.py:347
  156.9 0.7 reduce_sum.25
  (39 shorter events, 0.1 us)
Async XLA Ops:
  2.2 0.8 copy-start.16
  27.4 0.8 copy-start.17
  29.6 17.6 %all-to-all-start.1 = ((bf16[8,32,1024]{2,1,0:T(8,128)(2,1)}), bf16[8,32,1024]{2,1,0:T(8,128)(2,1)S(1)}, u32[]{:S(2)}, u32[]{:S(2)}) async-start(bf16[8,32,1024]{2,1,0:T(8,128)(2,1)} %repeat.1), calls=%async_computation.1 | async-start | bytes 1048576 | tf_op jit(solution)/shard_map/all_to_all | solution.py:27
  33.1 14.1 %collective-permute-start.1 = (bf16[8,32,1152]{2,1,0:T(8,128)(2,1)S(1)}, bf16[8,32,1152]{2,1,0:T(8,128)(2,1)S(1)}, u32[]{:S(2)}, u32[]{:S(2)}) collective-permute-start(bf16[8,32,1152]{2,1,0:T(8,128)(2,1)S(1)} %all_to_all.20.packed_ref.refs_0_), channel_id=1, source_target_pairs={{0,2},{1,3},{2,0},{3,1},{4,6},{5,7},{6,4},{7,5},{8,10},{9,11},{10,... | collective-permute-start | bytes 1769480 | tf_op jit(solution)/shard_map/ppermute | solution.py:23
  34.7 16.4 %collective-permute-start = (bf16[8,32,1152]{2,1,0:T(8,128)(2,1)S(1)}, bf16[8,32,1152]{2,1,0:T(8,128)(2,1)S(1)}, u32[]{:S(2)}, u32[]{:S(2)}) collective-permute-start(bf16[8,32,1152]{2,1,0:T(8,128)(2,1)S(1)} %all_to_all.20.packed_ref.refs_0_), channel_id=1, source_target_pairs={{0,1},{1,0},{2,3},{3,2},{4,5},{5,4},{6,7},{7,6},{8,9},{9,8},{10,11... | collective-permute-start | bytes 1769480 | tf_op jit(solution)/shard_map/ppermute | solution.py:23
  47.2 22.3 %copy-start = (bf16[8,32,1152]{2,1,0:T(8,128)(2,1)}, bf16[8,32,1152]{2,1,0:T(8,128)(2,1)S(1)}, u32[]{:S(2)}) copy-start(bf16[8,32,1152]{2,1,0:T(8,128)(2,1)S(1)} %collective-permute-done.1.refs_2_) | copy-start | bytes 1769476
  47.2 3.9 %collective-permute-start.2 = (bf16[8,32,1152]{2,1,0:T(8,128)(2,1)S(1)}, bf16[8,32,1152]{2,1,0:T(8,128)(2,1)S(1)}, u32[]{:S(2)}, u32[]{:S(2)}) collective-permute-start(bf16[8,32,1152]{2,1,0:T(8,128)(2,1)S(1)} %collective-permute-done.1.refs_2_), channel_id=1, source_target_pairs={{0,1},{1,0},{2,3},{3,2},{4,5},{5,4},{6,7},{7,6},{8,9},{9,8},{10,11... | collective-permute-start | bytes 1769480 | tf_op jit(solution)/shard_map/ppermute | solution.py:23
  47.2 15.7 %collective-permute-start.3 = (bf16[8,32,1024]{2,1,0:T(8,128)(2,1)S(1)}, bf16[8,32,1024]{2,1,0:T(8,128)(2,1)S(1)}, u32[]{:S(2)}, u32[]{:S(2)}) collective-permute-start(bf16[8,32,1024]{2,1,0:T(8,128)(2,1)S(1)} %all-to-all-done.1.refs_5_.refs_0_), channel_id=1, source_target_pairs={{0,2},{1,3},{2,0},{3,1},{4,6},{5,7},{6,4},{7,5},{8,10},{9,11},{10,... | collective-permute-start | bytes 1572872 | tf_op jit(solution)/shard_map/ppermute | solution.py:23
  51.0 18.5 %copy-start.2 = (bf16[8,32,1152]{2,1,0:T(8,128)(2,1)}, bf16[8,32,1152]{2,1,0:T(8,128)(2,1)S(1)}, u32[]{:S(2)}) copy-start(bf16[8,32,1152]{2,1,0:T(8,128)(2,1)S(1)} %collective-permute-done.refs_1_) | copy-start | bytes 1769476
  51.0 18.5 %copy-start.4 = (bf16[8,32,1152]{2,1,0:T(8,128)(2,1)}, bf16[8,32,1152]{2,1,0:T(8,128)(2,1)S(1)}, u32[]{:S(2)}) copy-start(bf16[8,32,1152]{2,1,0:T(8,128)(2,1)S(1)} %collective-permute-done.2.refs_3_) | copy-start | bytes 1769476
  61.7 1.1 copy-start.18
  62.8 15.3 %copy-start.6 = (bf16[8,32,1024]{2,1,0:T(8,128)(2,1)}, bf16[8,32,1024]{2,1,0:T(8,128)(2,1)S(1)}, u32[]{:S(2)}) copy-start(bf16[8,32,1024]{2,1,0:T(8,128)(2,1)S(1)} %collective-permute-done.3.refs_0_.refs_2_) | copy-start | bytes 1572868
  69.5 7.4 %collective-permute-start.4 = (bf16[2,256,1024]{2,1,0:T(8,128)(2,1)S(1)}, bf16[2,256,1024]{2,1,0:T(8,128)(2,1)S(1)}, u32[]{:S(2)}, u32[]{:S(2)}) collective-permute-start(bf16[2,256,1024]{2,1,0:T(8,128)(2,1)S(1)} %mix_odd.1.refs_0_), channel_id=1, source_target_pairs={{0,1},{1,0},{2,3},{3,2},{4,5},{5,4},{6,7},{7,6},{8,9},{9,8},{10,11... | collective-permute-start | bytes 3145736 | tf_op jit(solution)/shard_map/ppermute | solution.py:23
  69.7 8.4 %collective-permute-start.6 = (bf16[8,32,1024]{2,1,0:T(8,128)(2,1)S(1)}, bf16[8,32,1024]{2,1,0:T(8,128)(2,1)S(1)}, u32[]{:S(2)}, u32[]{:S(2)}) collective-permute-start(bf16[8,32,1024]{2,1,0:T(8,128)(2,1)S(1)} %all-to-all-done.1.refs_5_.refs_0_), channel_id=1, source_target_pairs={{0,1},{1,0},{2,3},{3,2},{4,5},{5,4},{6,7},{7,6},{8,9},{9,8},{10,11... | collective-permute-start | bytes 1572872 | tf_op jit(solution)/shard_map/ppermute | solution.py:23
  70.1 8.1 %collective-permute-start.7 = (bf16[8,32,1024]{2,1,0:T(8,128)(2,1)S(1)}, bf16[8,32,1024]{2,1,0:T(8,128)(2,1)S(1)}, u32[]{:S(2)}, u32[]{:S(2)}) collective-permute-start(bf16[8,32,1024]{2,1,0:T(8,128)(2,1)S(1)} %collective-permute-done.3.refs_0_.refs_2_), channel_id=1, source_target_pairs={{0,1},{1,0},{2,3},{3,2},{4,5},{5,4},{6,7},{7,6},{8,9},{9,8},{10,11... | collective-permute-start | bytes 1572872 | tf_op jit(solution)/shard_map/ppermute | solution.py:23
  77.5 14.3 %collective-permute-start.5 = (bf16[256,1024]{1,0:T(8,128)(2,1)S(1)}, bf16[256,1024]{1,0:T(8,128)(2,1)S(1)}, u32[]{:S(2)}, u32[]{:S(2)}) collective-permute-start(bf16[256,1024]{1,0:T(8,128)(2,1)S(1)} %mix_1.1.refs_5_), channel_id=1, source_target_pairs={{0,2},{1,3},{2,0},{3,1},{4,6},{5,7},{6,4},{7,5},{8,10},{9,11},{10,... | collective-permute-start | bytes 1572872 | tf_op jit(solution)/shard_map/ppermute | solution.py:23
  78.1 23.2 %copy-start.12 = (bf16[8,32,1024]{2,1,0:T(8,128)(2,1)}, bf16[8,32,1024]{2,1,0:T(8,128)(2,1)S(1)}, u32[]{:S(2)}) copy-start(bf16[8,32,1024]{2,1,0:T(8,128)(2,1)S(1)} %collective-permute-done.6.refs_1_) | copy-start | bytes 1572868
  78.1 23.2 %copy-start.14 = (bf16[8,32,1024]{2,1,0:T(8,128)(2,1)}, bf16[8,32,1024]{2,1,0:T(8,128)(2,1)S(1)}, u32[]{:S(2)}) copy-start(bf16[8,32,1024]{2,1,0:T(8,128)(2,1)S(1)} %collective-permute-done.7.refs_3_) | copy-start | bytes 1572868
  91.5 1.9 %copy-start.8 = (bf16[256,3072]{1,0:T(8,128)(2,1)}, bf16[256,3072]{1,0:T(8,128)(2,1)S(1)}, u32[]{:S(2)}) copy-start(bf16[256,3072]{1,0:T(8,128)(2,1)S(1)} %get-tuple-element.22.grad_ref) | copy-start | bytes 4718596
  91.5 9.8 %copy-start.10 = (bf16[512,384]{1,0:T(8,128)(2,1)}, bf16[512,384]{1,0:T(8,128)(2,1)S(1)}, u32[]{:S(2)}) copy-start(bf16[512,384]{1,0:T(8,128)(2,1)S(1)} %get-tuple-element.19.grad_ref) | copy-start | bytes 1179652
  101.3 15.0 %collective-permute-start.8 = (bf16[2,256,1024]{2,1,0:T(8,128)(2,1)S(1)}, bf16[2,256,1024]{2,1,0:T(8,128)(2,1)S(1)}, u32[]{:S(2)}, u32[]{:S(2)}) collective-permute-start(bf16[2,256,1024]{2,1,0:T(8,128)(2,1)S(1)} %back_odd.1.refs_0_), channel_id=1, source_target_pairs={{0,1},{1,0},{2,3},{3,2},{4,5},{5,4},{6,7},{7,6},{8,9},{9,8},{10,11... | collective-permute-start | bytes 3145736 | tf_op jit(solution)/shard_map/ppermute | solution.py:23
  101.4 31.3 %all-to-all-start.2 = ((bf16[8,32,1024]{2,1,0:T(8,128)(2,1)}), bf16[8,32,1024]{2,1,0:T(8,128)(2,1)}, u32[]{:S(2)}, u32[]{:S(2)}) async-start(bf16[8,32,1024]{2,1,0:T(8,128)(2,1)} %bitcast.3), calls=%async_computation.2 | async-start | bytes 1048576 | tf_op jit(solution)/shard_map/all_to_all | solution.py:27
  107.1 1.0 copy-start.11
  108.1 10.3 %copy-start.7 = (bf16[8,32,1024]{2,1,0:T(8,128)(2,1)S(1)}, bf16[8,32,1024]{2,1,0:T(8,128)(2,1)}, u32[]{:S(2)}) copy-start(bf16[8,32,1024]{2,1,0:T(8,128)(2,1)} %copy-done.6) | copy-start | bytes 1572868
  108.1 10.3 %copy-start.13 = (bf16[8,32,1024]{2,1,0:T(8,128)(2,1)S(1)}, bf16[8,32,1024]{2,1,0:T(8,128)(2,1)}, u32[]{:S(2)}) copy-start(bf16[8,32,1024]{2,1,0:T(8,128)(2,1)} %copy-done.12) | copy-start | bytes 1572868
  108.1 10.3 %copy-start.15 = (bf16[8,32,1024]{2,1,0:T(8,128)(2,1)S(1)}, bf16[8,32,1024]{2,1,0:T(8,128)(2,1)}, u32[]{:S(2)}) copy-start(bf16[8,32,1024]{2,1,0:T(8,128)(2,1)} %copy-done.14) | copy-start | bytes 1572868
  108.1 10.3 %copy-start.19 = (bf16[256,3072]{1,0:T(8,128)(2,1)S(1)}, bf16[256,3072]{1,0:T(8,128)(2,1)}, u32[]{:S(2)}) copy-start(bf16[256,3072]{1,0:T(8,128)(2,1)} %copy-done.18) | copy-start | bytes 4718596
  116.4 23.8 %copy-start.1 = (bf16[8,32,1152]{2,1,0:T(8,128)(2,1)S(1)}, bf16[8,32,1152]{2,1,0:T(8,128)(2,1)}, u32[]{:S(2)}) copy-start(bf16[8,32,1152]{2,1,0:T(8,128)(2,1)} %copy-done) | copy-start | bytes 1769476
  116.4 23.8 %copy-start.3 = (bf16[8,32,1152]{2,1,0:T(8,128)(2,1)S(1)}, bf16[8,32,1152]{2,1,0:T(8,128)(2,1)}, u32[]{:S(2)}) copy-start(bf16[8,32,1152]{2,1,0:T(8,128)(2,1)} %copy-done.2) | copy-start | bytes 1769476
  117.0 14.1 %collective-permute-start.9 = (bf16[256,1024]{1,0:T(8,128)(2,1)S(1)}, bf16[256,1024]{1,0:T(8,128)(2,1)S(1)}, u32[]{:S(2)}, u32[]{:S(2)}) collective-permute-start(bf16[256,1024]{1,0:T(8,128)(2,1)S(1)} %back_1.1.refs_4_), channel_id=1, source_target_pairs={{0,2},{1,3},{2,0},{3,1},{4,6},{5,7},{6,4},{7,5},{8,10},{9,11},{10,... | collective-permute-start | bytes 1572872 | tf_op jit(solution)/shard_map/ppermute | solution.py:23
  132.7 24.2 %all-to-all-start.3 = ((bf16[8,32,1024]{2,1,0:T(8,128)(2,1)}), bf16[8,32,1024]{2,1,0:T(8,128)(2,1)S(1)}, u32[]{:S(2)}, u32[]{:S(2)}) async-start(bf16[8,32,1024]{2,1,0:T(8,128)(2,1)} %bitcast.4), calls=%async_computation.3 | async-start | bytes 1048576 | tf_op jit(solution)/shard_map/all_to_all | solution.py:27
  140.2 1.1 copy-start.5
  141.2 1.4 copy-start.9

commit v6 on v5

--- a/solution.py
+++ b/solution.py
@@ -62,25 +62,24 @@
     return space(shape, dtype)
 
 
-def stream(copies, step, steps):
+def stream(copies, step, steps, depth):
     @pl.when(step == 0)
     def _():
-        for ahead in range(min(DEPTH - 1, steps)):
+        for ahead in range(min(depth - 1, steps)):
             for copy in copies(ahead):
                 copy.start()
 
-    @pl.when(step + DEPTH - 1 < steps)
-    def _():
-        for copy in copies(step + DEPTH - 1):
+    @pl.when(step + depth - 1 < steps)
+    def _():
+        for copy in copies(step + depth - 1):
             copy.start()
 
 
 def gather(to_row_ref, sources, held_ref, rows_ref, sems):
+    width = held_ref.shape[3]
     copies = [
-        pltpu.make_async_copy(
-            source.at[:, :, pl.ds(0, held_ref.shape[3])], held_ref.at[s], sems.at[s]
-        )
-        for s, source in enumerate(sources)
+        pltpu.make_async_copy(source.at[:, :, pl.ds(start, width)], held_ref.at[s], sems.at[s])
+        for s, (source, start) in enumerate(sources)
     ]
     for copy in copies:
         copy.start()
@@ -107,10 +106,12 @@
         out_ref[group, :, width:] = packed
 
 
-def repeat_kernel(me_ref, token_ref, *refs):
-    out_ref = refs[-1]
-    for group in range(out_ref.shape[0]):
-        out_ref[group] = token_ref[...]
+def repeat_kernel(count, me_ref, *refs):
+    parts, out_ref = refs[:count], refs[-1]
+    width = parts[0].shape[1]
+    for i, part in enumerate(parts):
+        for group in range(out_ref.shape[0]):
+            out_ref[group, :, i * width : (i + 1) * width] = part[...]
 
 
 def plan_kernel(top, local, me_ref, packed_ref, to_token_ref, to_row_ref, gate_ref):
@@ -151,11 +152,11 @@
 def preact_kernel(n, steps, me_ref, to_row_ref, gate_ref, *refs):
     xs, w_ref = refs[:n], refs[n]
     act_ref, spread_ref, slope_ref, held_ref, rows_ref, x_sems, buffer, sems = refs[-8:]
-    room, width = act_ref.shape[0], rows_ref.shape[2]
+    room, width, depth = act_ref.shape[0], rows_ref.shape[2], buffer.shape[0]
     e = pl.program_id(0)
 
     def copies(step):
-        slot = step % DEPTH
+        slot = step % depth
         return [
             pltpu.make_async_copy(
                 w_ref.at[step, block(me_ref[0] ^ s, width), :], buffer.at[slot, s], sems.at[slot, s]
@@ -163,15 +164,15 @@
             for s in range(n)
         ]
 
-    stream(copies, e, steps)
+    stream(copies, e, steps, depth)
 
     @pl.when(e == 0)
     def _():
-        gather(to_row_ref, xs, held_ref, rows_ref, x_sems)
+        gather(to_row_ref, [(x, 0) for x in xs], held_ref, rows_ref, x_sems)
 
     for copy in copies(e):
         copy.wait()
-    pre = sum(dot(rows_ref[s, block(e, room), :], buffer[e % DEPTH, s]) for s in range(n))
+    pre = sum(dot(rows_ref[s, block(e, room), :], buffer[e % depth, s]) for s in range(n))
     sig = jax.nn.sigmoid(pre)
     gate = gate_ref[...]
     act = (gate * (pre * sig)).astype(BF16)
@@ -180,15 +181,16 @@
     slope_ref[...] = gate * (sig * (1.0 + pre * (1.0 - sig)))
 
 
-def slope_kernel(n, steps, me_ref, to_row_ref, slope_ref, *refs):
-    ys, w_ref = refs[:n], refs[n]
-    grad_ref, spread_ref, held_ref, rows_ref, y_sems, buffer, sems = refs[-7:]
+def middle_kernel(n, steps, me_ref, to_token_ref, to_row_ref, slope_ref, act_ref, *refs):
+    ys, w_ref = refs[:2], refs[2]
+    sums, (grad_ref, spread_ref) = refs[3:5], refs[5:7]
+    held_ref, rows_ref, y_sems, out_rows_ref, buffer, sems = refs[7:]
     room, hid = grad_ref.shape
-    width = rows_ref.shape[2]
+    width, depth = rows_ref.shape[2], buffer.shape[0]
     e = pl.program_id(0)
 
     def copies(step):
-        slot = step % DEPTH
+        slot = step % depth
         return [
             pltpu.make_async_copy(
                 w_ref.at[block(step, hid), block(me_ref[0] ^ s, width)],
@@ -198,81 +200,66 @@
             for s in range(n)
         ]
 
-    stream(copies, e, steps)
+    stream(copies, e, steps, depth)
 
     @pl.when(e == 0)
     def _():
-        gather(to_row_ref, ys, held_ref, rows_ref, y_sems)
+        sources = [(ys[s % 2], s // 2 * width) for s in range(n)]
+        gather(to_row_ref, sources, held_ref, rows_ref, y_sems)
 
     for copy in copies(e):
         copy.wait()
-    grad = sum(
-        dot(buffer[e % DEPTH, s], rows_ref[s, block(e, room), :], ((1,), (1,))) for s in range(n)
-    )
+    here = block(e, room)
+    grad = 0.0
+    for s in range(n):
+        weights = buffer[e % depth, s]
+        out_rows_ref[s, here, :] = dot(act_ref[...], weights).astype(BF16)
+        grad = grad + dot(weights, rows_ref[s, here, :], ((1,), (1,)))
     grad = (grad.T * slope_ref[...]).astype(BF16)
     grad_ref[...] = grad
-    spread_ref[...] = dot(to_row_ref[block(e, room), :], grad, ((0,), (0,))).astype(BF16)
-
-
-def column_block(me_ref, step, per, odd):
-    return (me_ref[0] ^ (2 * (step // per) + odd)) * per + step % per
-
-
-def mix_kernel(steps, per, odd, me_ref, to_token_ref, act_ref, w_ref, *refs):
+    spread_ref[...] = dot(to_row_ref[here, :], grad, ((0,), (0,))).astype(BF16)
+
+    @pl.when(e == steps - 1)
+    def _():
+        for s in range(n):
+            total = dot(to_token_ref[...], out_rows_ref[s])
+            sums[s % 2][s // 2] = total.astype(BF16)
+
+
+def back_kernel(steps, per, odd, me_ref, to_token_ref, grad_ref, w_ref, *refs):
     out_ref, rows_ref, buffer, sems = refs[-4:]
-    _, local, hid, cols = buffer.shape
-    room = rows_ref.shape[0] // local
+    depth, pairs, cols, wide = buffer.shape
+    hid = grad_ref.shape[1]
+    group = wide // hid
+    room = rows_ref.shape[1] // (pairs * group)
     step = pl.program_id(0)
 
     def copies(step):
-        slot = step % DEPTH
-        columns = block(column_block(me_ref, step, per, odd), cols)
+        slot = step % depth
+        column = (me_ref[0] ^ (2 * (step // per) + odd)) * per + step % per
         return [
             pltpu.make_async_copy(
-                w_ref.at[pl.ds(e * hid, hid), columns], buffer.at[slot, e], sems.at[slot, e]
+                w_ref.at[p * group + i, block(column, cols), :],
+                buffer.at[slot, p, :, pl.ds(i * hid, hid)],
+                sems.at[slot, p * group + i],
             )
-            for e in range(local)
+            for p in range(pairs)
+            for i in range(group)
         ]
 
-    stream(copies, step, steps)
+    stream(copies, step, steps, depth)
     for copy in copies(step):
         copy.wait()
-    for e in range(local):
-        here = slice(e * room, (e + 1) * room)
-        rows_ref[here, :] = dot(act_ref[here, :], buffer[step % DEPTH, e]).astype(BF16)
-    out_ref[0] = dot(to_token_ref[...], rows_ref[...]).astype(BF16)
-
-
-def back_kernel(steps, per, odd, me_ref, to_token_ref, grad_ref, w_ref, *refs):
-    out_ref, rows_ref, buffer, sems = refs[-4:]
-    _, local, cols, hid = buffer.shape
-    room = rows_ref.shape[1] // local
-    group = 2 if room % 128 and local % 2 == 0 else 1
-    step = pl.program_id(0)
-
-    def copies(step):
-        slot = step % DEPTH
-        columns = block(column_block(me_ref, step, per, odd), cols)
-        return [
-            pltpu.make_async_copy(
-                w_ref.at[e, columns, :], buffer.at[slot, e], sems.at[slot, e]
-            )
-            for e in range(local)
-        ]
-
-    stream(copies, step, steps)
-    for copy in copies(step):
-        copy.wait()
-    for first in range(0, local, group):
-        part = 0.0
+    for p in range(pairs):
+        corners = []
         for i in range(group):
-            here = slice((first + i) * room, (first + i + 1) * room)
+            start = (p * group + i) * room
             blank = [jnp.zeros((room, hid), BF16)] * group
-            blank[i] = grad_ref[here, :]
-            part = part + dot(
-                buffer[step % DEPTH, first + i], jnp.concatenate(blank, axis=0), ((1,), (1,))
-            )
-        rows_ref[:, first * room : (first + group) * room] = part.astype(BF16)
+            blank[i] = grad_ref[start : start + room, :]
+            corners.append(jnp.concatenate(blank, axis=1) if group > 1 else blank[0])
+        corner = jnp.concatenate(corners, axis=0) if group > 1 else corners[0]
+        part = dot(buffer[step % depth, p], corner, ((1,), (1,)))
+        rows_ref[:, p * group * room : (p + 1) * group * room] = part.astype(BF16)
     out_ref[0] = dot(to_token_ref[...], rows_ref[...], ((1,), (1,))).astype(BF16)
 
 
@@ -306,7 +293,7 @@
 
 
 def d_out_kernel(n, steps, me_ref, act_ref, *refs):
-    ys, (out_ref, done_ref, buffer, sems) = refs[:n], refs[-4:]
+    ys, (out_ref, done_ref, buffer, sems) = refs[:2], refs[-4:]
     e = pl.program_id(0)
     _, n, hid, width = buffer.shape
     act = act_ref[...].T
@@ -315,29 +302,50 @@
 
     def values():
         for s in range(n):
-            yield dot(act, flat_rows(ys[s][...]))
+            start = s // 2 * width
+            yield dot(act, flat_rows(ys[s % 2][:, :, start : start + width]))
 
     write_step(e, steps, values, outs, buffer, sems)
 
 
-def d_in_kernel(n, steps, me_ref, grad_ref, *refs):
+def d_in_kernel(n, pairs, me_ref, grad_ref, *refs):
     xs, (out_ref, flipped, buffer, sems) = refs[:n], refs[-4:]
-    e = pl.program_id(0)
-    _, n, width, hid = buffer.shape
-
-    @pl.when(e == 0)
-    def _():
-        for s in range(n):
-            flipped[s] = flat_rows(xs[s][...]).T
-
-    grad = grad_ref[...]
-    outs = [out_ref.at[e, block(me_ref[0] ^ s, width), :] for s in range(n)]
-
-    def values():
-        for s in range(n):
-            yield dot(flipped[s], grad)
-
-    write_step(e, steps, values, outs, buffer, sems)
+    p, s = pl.program_id(0), pl.program_id(1)
+    slots, group, width, hid = buffer.shape
+    step, steps = p * n + s, pairs * n
+    slot = step % slots
+
+    for i in range(n):
+
+        @pl.when((p == 0) & (s == i))
+        def _():
+            flipped[i] = flat_rows(xs[i][...]).T
+
+    def copies(slot):
+        return [
+            pltpu.make_async_copy(
+                buffer.at[slot, i],
+                out_ref.at[p * group + i, block(me_ref[0] ^ s, width), :],
+                sems.at[slot, i],
+            )
+            for i in range(group)
+        ]
+
+    @pl.when(step >= slots)
+    def _():
+        for copy in copies(slot):
+            copy.wait()
+
+    value = dot(flipped[s], grad_ref[...]).astype(BF16)
+    for i, copy in enumerate(copies(slot)):
+        buffer[slot, i] = value[:, i * hid : (i + 1) * hid]
+        copy.start()
+
+    @pl.when(step == steps - 1)
+    def _():
+        for last in range(min(slots, steps)):
+            for copy in copies(last):
+                copy.wait()
 
 
 def call(kernel, name, grid, in_specs, out_specs, out_shape, args, flops, limit, scratch=(), after=()):
@@ -393,22 +401,29 @@
     )
     left = exchange_rows(packed)
     xs = gather_chunks(left)
-    whole = exchange_rows(
+    raw = {0: cotangent}
+    bit = n // 2
+    while bit > 1:
+        raw.update({k | bit: swap(c, "tensor", bit) for k, c in list(raw.items())})
+        bit //= 2
+    raw = [raw[k] for k in sorted(raw)]
+    wide = len(raw) * quarter
+    even_y = exchange_rows(
         call(
-            repeat_kernel,
+            functools.partial(repeat_kernel, len(raw)),
             "repeat",
             (1,),
-            [once(rows, quarter)],
-            once(groups, rows, quarter),
-            jax.ShapeDtypeStruct((groups, rows, quarter), BF16),
-            (me, cotangent),
+            [once(rows, quarter)] * len(raw),
+            once(groups, rows, wide),
+            jax.ShapeDtypeStruct((groups, rows, wide), BF16),
+            (me, *raw),
             0,
-            24 if big else 4,
+            24 if big else 6,
             (),
-            (left,),
+            (xs[1],),
         )
     )
-    ys = gather_chunks(whole)
+    ys = (even_y, swap(even_y, "tensor", 1))
     to_token, to_row, gate = call(
         functools.partial(plan_kernel, top, local),
         "plan",
@@ -431,10 +446,12 @@
         48 if big else 6,
     )
 
+    depth = min(DEPTH, local)
+
     def ring(*shape):
         return [
-            pltpu.VMEM((DEPTH, *shape), BF16),
-            pltpu.SemaphoreType.DMA((DEPTH, shape[0])),
+            pltpu.VMEM((depth, *shape), BF16),
+            pltpu.SemaphoreType.DMA((depth, shape[0])),
         ]
 
     chunk_specs = [once(groups, rows, quarter)] * n
@@ -462,25 +479,45 @@
         flops,
         limit,
         gathered + ring(n, quarter, hid),
-        (whole,),
+        (even_y,),
     )
     cols = min(512, quarter)
     per = quarter // cols
     steps = n // 2 * per
-
-    def parts(kernel, name, held, weights, odd, after=()):
-        shape = (local, hid, cols) if weights.ndim == 2 else (local, cols, hid)
+    group = 2 if local % 2 == 0 else 1
+    sum_spec = once(n // 2, total, quarter)
+    sum_shape = jax.ShapeDtypeStruct((n // 2, total, quarter), BF16)
+    mix_even, mix_odd, grad, grad_dense = call(
+        functools.partial(middle_kernel, n, local),
+        "middle",
+        (local,),
+        [once(total, slots), once(slots, total), row_block, row_block]
+        + [ANYWHERE] * 2
+        + [IN_HBM],
+        [sum_spec, sum_spec, row_block, dense_block],
+        [sum_shape, sum_shape, row_shape, dense],
+        (me, to_token, to_row, slope, act, *ys, flat_out),
+        2 * flops,
+        56 if big else 30,
+        gathered + [pltpu.VMEM((n, slots, quarter), BF16)] + ring(n, hid, quarter),
+    )
+
+    def back(name, odd, after=()):
         return call(
-            functools.partial(kernel, steps, per, odd),
+            functools.partial(back_kernel, steps, per, odd),
             name,
             (steps,),
             [once(total, slots), once(slots, hid), IN_HBM],
             pl.BlockSpec((1, total, cols), lambda i, me: (i // per, 0, i % per)),
-            jax.ShapeDtypeStruct((n // 2, total, quarter), BF16),
-            (me, to_token, held, weights),
+            sum_shape,
+            (me, to_token, grad, w_in),
             flops // 2,
             limit,
-            [pltpu.VMEM((slots, cols) if weights.ndim == 2 else (cols, slots), BF16)] + ring(*shape),
+            [pltpu.VMEM((cols, slots), BF16)]
+            + [
+                pltpu.VMEM((DEPTH, local // group, cols, group * hid), BF16),
+                pltpu.SemaphoreType.DMA((DEPTH, local)),
+            ],
             after,
         )
 
@@ -503,10 +540,11 @@
         shape = (1, total, quarter)
         return pl.BlockSpec(shape, lambda i, me: (index, 0, 0), pipeline_mode=pl.Buffered(1))
 
-    def pass_on(name, even, odd):
+    def pass_on(name, even, odd, after=()):
         got = swap(odd, "tensor", 1)
         return got, {
-            i: add(f"{name}_{i}", (even, got), [one_of(i), one_of(i)]) for i in range(1, n // 2)
+            i: add(f"{name}_{i}", (even, got), [one_of(i), one_of(i)], after)
+            for i in range(1, n // 2)
         }
 
     def gather_sum(name, even, got, sent, after=()):
@@ -530,28 +568,9 @@
             count, bit = half, bit // 2
         return add(f"{name}_sum", values, specs, after)
 
-    mix_odd = parts(mix_kernel, "mix_odd", act, flat_out, 1, (ys[n // 2],))
-    mix_even = parts(mix_kernel, "mix_even", act, flat_out, 0, (mix_odd,))
-    mix_got, mix_sent = pass_on("mix", mix_even, mix_odd)
-    mix_sum = gather_sum("mix", mix_even, mix_got, mix_sent)
-    mixed = scatter_rows(mix_sum, rows).astype(BF16)
-
-    grad, grad_dense = call(
-        functools.partial(slope_kernel, n, local),
-        "grad_preact",
-        (local,),
-        [once(slots, total), row_block] + loose,
-        [row_block, dense_block],
-        [row_shape, dense],
-        (me, to_row, slope, *ys, flat_out),
-        flops,
-        limit,
-        gathered + ring(n, hid, quarter),
-        tuple(mix_sent.values()),
-    )
-
-    back_odd = parts(back_kernel, "back_odd", grad, w_in, 1, (mix_sum,))
-    back_even = parts(back_kernel, "back_even", grad, w_in, 0, (back_odd,))
+    back_odd = back("back_odd", 1)
+    mix_got, mix_sent = pass_on("mix", mix_even, mix_odd, (back_odd,))
+    back_even = back("back_even", 0, tuple(mix_sent.values()))
     back_got, back_sent = pass_on("back", back_even, back_odd)
 
     sems = pltpu.SemaphoreType.DMA((2, n))
@@ -559,7 +578,7 @@
         functools.partial(d_out_kernel, n, local),
         "d_w_out",
         (local,),
-        [dense_block] + chunk_specs,
+        [dense_block] + [once(groups, rows, wide)] * 2,
         [IN_HBM, once(8, 128)],
         [placed(pltpu.HBM, (local * hid, width)), jax.ShapeDtypeStruct((8, 128), F32)],
         (me, act_dense, *ys),
@@ -568,13 +587,15 @@
         [pltpu.VMEM((2, n, hid, quarter), BF16), sems],
         tuple(back_sent.values()),
     )
-    back_sum = gather_sum("back", back_even, back_got, back_sent, (done,))
+    mix_sum = gather_sum("mix", mix_even, mix_got, mix_sent, (done,))
+    mixed = scatter_rows(mix_sum, rows).astype(BF16)
+    back_sum = gather_sum("back", back_even, back_got, back_sent, (mix_sum,))
     d_tokens = scatter_rows(back_sum, rows).astype(BF16)
     d_w_in = call(
-        functools.partial(d_in_kernel, n, local),
+        functools.partial(d_in_kernel, n, local // group),
         "d_w_in",
-        (local,),
-        [dense_block] + chunk_specs,
+        (local // group, n),
+        [pl.BlockSpec((total, group * hid), lambda p, s, me: (0, p))] + chunk_specs,
         IN_HBM,
         placed(pltpu.HBM, w_in.shape),
         (me, grad_dense, *xs),
@@ -582,8 +603,8 @@
         limit,
         [
             pltpu.VMEM((n, quarter, total), BF16),
-            pltpu.VMEM((2, n, quarter, hid), BF16),
-            sems,
+            pltpu.VMEM((4, group, quarter, hid), BF16),
+            pltpu.SemaphoreType.DMA((4, group)),
         ],
         (back_sum,),
     )

time: 158 us -> 176 us (1.11)
  waiting for transfers between devices: 13.2 us -> 41.5 us
  Pallas kernels: 88.5 us -> 80.2 us
  starting transfers between devices: 20.9 us -> 19.1 us
    all_to_all x3, waiting for transfers between devices: 0.01 us -> 24.3 us  [exchange_rows(): lax.all_to_all(blocks, 'expert', split_axis=0, concat_axis=0, tiled=True)]
    pallas_call x15 -> x13, Pallas kernels: 88.5 us -> 80.2 us  [call(): pl.pallas_call(kernel, grid_spec=pltpu.PrefetchScalarGridSpec(num_scalar_...]
    ppermute x10 -> x9, waiting for transfers between devices: 13.2 us -> 17.3 us  [swap(): return lax.ppermute(value, axis, [(i, i ^ bits) for i in range(size)])]
    all_to_all x3, starting transfers between devices: 15 us -> 12.7 us  [exchange_rows(): lax.all_to_all(blocks, 'expert', split_axis=0, concat_axis=0, tiled=True)]
    unnamed x42 -> x24, local copies, waits for them, and re-layouts: 7.86 us -> 8.96 us
    ppermute x10 -> x9, starting transfers between devices: 5.93 us -> 6.36 us  [swap(): return lax.ppermute(value, axis, [(i, i ^ bits) for i in range(size)])]
  transfers between devices with their start and end apart: 13 -> 12, of which waited for: 3 -> 4; matrix products, arithmetic and copies ran while one was open for 1% -> 0% of each run, Pallas kernels for 45% -> 33%
where the time goes in v6:
time: 176 us
  Pallas kernels  80.2 us (46%)
  waiting for transfers between devices  41.5 us (24%)
  blocking collectives  23.6 us (13%)
  starting transfers between devices  19.1 us (11%)
  local copies, waits for them, and re-layouts  8.96 us (5%)
    pallas_call x13, Pallas kernels, call(): pl.pallas_call(kernel, grid_spec=pltpu.PrefetchScalarGridSpec(num_scalar_...  80.2 us
    all_to_all x3, waiting for transfers between devices, exchange_rows(): lax.all_to_all(blocks, 'expert', split_axis=0, concat_axis=0, tiled=True)  24.3 us
    all_to_all x1, blocking collectives, exchange_rows(): lax.all_to_all(blocks, 'expert', split_axis=0, concat_axis=0, tiled=True)  23.6 us
    ppermute x9, waiting for transfers between devices, swap(): return lax.ppermute(value, axis, [(i, i ^ bits) for i in range(size)])  17.3 us
    all_to_all x3, starting transfers between devices, exchange_rows(): lax.all_to_all(blocks, 'expert', split_axis=0, concat_axis=0, tiled=True)  12.7 us
    unnamed x24, local copies, waits for them, and re-layouts  8.96 us
    ppermute x9, starting transfers between devices, swap(): return lax.ppermute(value, axis, [(i, i ^ bits) for i in range(size)])  6.36 us
  transfers between devices with their start and end apart: 12, of which 4 were waited for; matrix products, arithmetic and copies ran while one was open for 0% of the time, Pallas kernels for 33%

profile of v6, /device:TPU:0, one launch (start us, length us, event | category | flops | bytes accessed | tf_op | source)
XLA Modules:
  0.0 175.7 jit_solution(5660632207769097770)
XLA Ops:
  0.6 0.8 copy.10.routing_ref
  1.4 0.8 copy.11.gates_ref
  2.2 0.1 pad_add_fusion.me_ref
  2.2 0.8 copy-done.9
  3.1 0.7 pack.1
  3.8 23.6 %all_to_all.20.packed_ref.refs_0_ = bf16[8,32,1152]{2,1,0:T(8,128)(2,1)S(1)} all-to-all(bf16[8,32,1152]{2,1,0:T(8,128)(2,1)S(1)} %pack.1), channel_id=1, replica_groups=mesh['expert'=8,'tensor'=4] {'expert'}, dimensions={0} | all-to-all | bytes 1179648 | tf_op jit(solution)/shard_map/all_to_all | solution.py:27
  27.4 0.0 collective-permute-start
  27.4 1.5 collective-permute-start.3
  28.9 3.2 %collective-permute-done.3.refs_1_ = bf16[32,1024]{1,0:T(8,128)(2,1)S(1)} collective-permute-done((bf16[32,1024]{1,0:T(8,128)(2,1)}, bf16[32,1024]{1,0:T(8,128)(2,1)S(1)}, u32[]{:S(2)}, u32[]{:S(2)}) %collective-permute-start.3) | collective-permute-done | bytes 65568 | tf_op jit(solution)/shard_map/ppermute | solution.py:23
  32.1 0.0 collective-permute-done.refs_2_.refs_1_
  32.1 0.8 copy-done.10
  32.9 1.6 repeat.1
  34.5 3.6 %all-to-all-start.1 = ((bf16[8,32,2048]{2,1,0:T(8,128)(2,1)}), bf16[8,32,2048]{2,1,0:T(8,128)(2,1)S(1)}, u32[]{:S(2)}, u32[]{:S(2)}) async-start(bf16[8,32,2048]{2,1,0:T(8,128)(2,1)} %repeat.1), calls=%async_computation.1 | async-start | bytes 2097152 | tf_op jit(solution)/shard_map/all_to_all | solution.py:27
  38.1 1.6 collective-permute-start.1
  39.7 24.3 %all-to-all-done.1.refs_5_.refs_0_ = bf16[8,32,2048]{2,1,0:T(8,128)(2,1)S(1)} async-done(((bf16[8,32,2048]{2,1,0:T(8,128)(2,1)}), bf16[8,32,2048]{2,1,0:T(8,128)(2,1)S(1)}, u32[]{:S(2)}, u32[]{:S(2)}) %all-to-all-start.1) | async-done | bytes 1048608 | tf_op jit(solution)/shard_map/all_to_all | solution.py:27
  63.9 0.0 collective-permute-start.4
  63.9 0.0 collective-permute-done.1.refs_2_
  63.9 0.5 collective-permute-start.2
  64.5 2.3 %plan.1 = (bf16[256,512]{1,0:T(8,128)(2,1)S(1)}, bf16[512,256]{1,0:T(8,128)(2,1)S(1)}, f32[512,1]{1,0:T(8,128)S(1)}) custom-call(s32[2]{0:T(128)S(1)} %pad_add_fusion.me_ref, bf16[8,32,1152]{2,1,0:T(8,128)(2,1)S(1)} %all_to_all.20.packed_ref.refs_0_), custom_call_target="tpu_custom_call" | custom-call | bytes 1116168 | tf_op jit(solution)/shard_map/plan/pallas_call | solution.py:355
  66.7 0.7 collective-permute-done.2.refs_3_
  67.4 10.6 %preact.1 = (bf16[512,384]{1,0:T(8,128)(2,1)S(1)}, bf16[256,3072]{1,0:T(8,128)(2,1)S(1)}, f32[512,384]{1,0:T(8,128)S(1)}) custom-call(s32[2]{0:T(128)S(1)} %pad_add_fusion.me_ref, bf16[512,256]{1,0:T(8,128)(2,1)S(1)} %get-tuple-element.17.to_row_ref, f32[512,1]{1,0:T(8,128)S(1)} %get-tuple-element.18.gate_ref, ...), custom_call_target="tpu_custom_call" | custom-call | flops 1610612736 | bytes 30541832 | tf_op jit(solution)/shard_map/preact/pallas_call | solution.py:355
  78.1 18.6 %middle.1 = (bf16[2,256,1024]{2,1,0:T(8,128)(2,1)S(1)}, bf16[2,256,1024]{2,1,0:T(8,128)(2,1)S(1)}, bf16[512,384]{1,0:T(8,128)(2,1)S(1)}, bf16[256,3072]{1,0:T(8,128)(2,1)S(1)}) custom-call(s32[2]{0:T(128)S(1)} %pad_add_fusion.me_ref, bf16[256,512]{1,0:T(8,128)(2,1)S(1)} %get-tuple-element.16.to_token_ref, bf16[512,256]{1,0:T(8,128)(2,1)S(1)} %get-tuple-element.17.to_row_ref, ...), custom_call_target="tpu_custom_call" | custom-call | flops 3221225472 | bytes 33030152 | tf_op jit(solution)/shard_map/middle/pallas_call | solution.py:355
  96.8 0.0 copy-start.6
  96.8 0.2 collective-permute-start.5
  97.0 7.8 %back_odd.1.refs_2_ = bf16[2,256,1024]{2,1,0:T(8,128)(2,1)S(1)} custom-call(s32[2]{0:T(128)S(1)} %pad_add_fusion.me_ref, bf16[256,512]{1,0:T(8,128)(2,1)S(1)} %get-tuple-element.16.to_token_ref, bf16[512,384]{1,0:T(8,128)(2,1)S(1)} %get-tuple-element.23.grad_ref, bf16[8,4096,384]{2,1,0:T(8,128)(2,1)} %w_ref.3), custom_call_target="tpu_custom_call" | custom-call | flops 805306368 | bytes 26869768 | tf_op jit(solution)/shard_map/back_odd/pallas_call | solution.py:355
  104.8 0.4 collective-permute-start.7
  105.2 0.0 collective-permute-done.5.refs_1_
  105.2 0.7 mix_1.1.refs_0_
  105.9 1.6 collective-permute-start.6
  107.5 7.8 %back_even.1.refs_0_ = bf16[2,256,1024]{2,1,0:T(8,128)(2,1)S(1)} custom-call(s32[2]{0:T(128)S(1)} %pad_add_fusion.me_ref, bf16[256,512]{1,0:T(8,128)(2,1)S(1)} %get-tuple-element.16.to_token_ref, bf16[512,384]{1,0:T(8,128)(2,1)S(1)} %get-tuple-element.23.grad_ref, bf16[8,4096,384]{2,1,0:T(8,128)(2,1)} %w_ref.3, bf16[256,1024]{1,0:T(8,128)(2,1)S(1)} %mix_1.1.refs_0_), custom_call_target="tpu_custom_call" | custom-call | flops 805306368 | bytes 26869768 | tf_op jit(solution)/shard_map/back_even/pallas_call | solution.py:355
  115.3 0.0 collective-permute-done.7.refs_1_
  115.3 0.7 back_1.1.refs_2_
  115.9 1.0 copy-done
  116.9 12.3 %d_w_out.1 = (bf16[3072,4096]{1,0:T(8,128)(2,1)}, f32[8,128]{1,0:T(8,128)S(1)}) custom-call(s32[2]{0:T(128)S(1)} %pad_add_fusion.me_ref, bf16[256,3072]{1,0:T(8,128)(2,1)S(1)} %get-tuple-element.24.act_ref, bf16[8,32,2048]{2,1,0:T(8,128)(2,1)S(1)} %all-to-all-done.1.refs_5_.refs_0_, bf16[8,32,2048]{2,1,0:T(8,128)(2,1)S(1)} %collective-permute-done.4.refs_1_, ...), custom_call_target="tpu_custom_call" | custom-call | flops 6442450944 | bytes 28839944 | tf_op jit(solution)/shard_map/d_w_out/pallas_call | solution.py:355
  129.2 0.0 collective-permute-done.6.refs_2_
  129.2 1.5 mix_sum.1.refs_3_
  130.8 3.6 %all-to-all-start.2 = ((bf16[8,32,1024]{2,1,0:T(8,128)(2,1)}), bf16[8,32,1024]{2,1,0:T(8,128)(2,1)S(1)}, u32[]{:S(2)}, u32[]{:S(2)}) async-start(bf16[8,32,1024]{2,1,0:T(8,128)(2,1)} %bitcast.3), calls=%async_computation.2 | async-start | bytes 1048576 | tf_op jit(solution)/shard_map/all_to_all | solution.py:27
  134.4 0.5 collective-permute-start.8
  134.9 13.3 %collective-permute-done.8.refs_2_ = bf16[256,1024]{1,0:T(8,128)(2,1)S(1)} collective-permute-done((bf16[256,1024]{1,0:T(8,128)(2,1)}, bf16[256,1024]{1,0:T(8,128)(2,1)S(1)}, u32[]{:S(2)}, u32[]{:S(2)}) %collective-permute-start.8) | collective-permute-done | bytes 524320 | tf_op jit(solution)/shard_map/ppermute | solution.py:23
  148.2 1.2 copy-done.1
  149.5 1.6 back_sum.1.refs_4_
  151.0 5.6 %all-to-all-start.3 = ((bf16[8,32,1024]{2,1,0:T(8,128)(2,1)}), bf16[8,32,1024]{2,1,0:T(8,128)(2,1)S(1)}, u32[]{:S(2)}, u32[]{:S(2)}) async-start(bf16[8,32,1024]{2,1,0:T(8,128)(2,1)} %bitcast.4), calls=%async_computation.3 | async-start | bytes 1048576 | tf_op jit(solution)/shard_map/all_to_all | solution.py:27
  156.6 1.1 copy-done.3
  157.7 1.1 copy-done.5
  158.7 1.4 copy-done.7
  160.2 14.1 %d_w_in.1 = bf16[8,4096,384]{2,1,0:T(8,128)(2,1)} custom-call(s32[2]{0:T(128)S(1)} %pad_add_fusion.me_ref, bf16[256,3072]{1,0:T(8,128)(2,1)S(1)} %copy-done.7, bf16[8,32,1152]{2,1,0:T(8,128)(2,1)S(1)} %all_to_all.20.packed_ref.refs_0_, bf16[8,32,1152]{2,1,0:T(8,128)(2,1)S(1)} %collective-permute-done.refs_2_.refs_1_, bf16[8,32,1152]{2,1,0:T(8,128)(2,1)S(1)} %copy-done.3, ...), custom_call_target="tpu_custom_call" | custom-call | flops 6442450944 | bytes 29097992 | tf_op jit(solution)/shard_map/d_w_in/pallas_call | solution.py:355
  174.3 0.7 reduce_sum.24
  175.0 0.7 reduce_sum.25
  (17 shorter events, 0.0 us)
Async XLA Ops:
  2.2 0.8 copy-start.9
  27.4 4.7 %collective-permute-start = (bf16[8,32,1152]{2,1,0:T(8,128)(2,1)S(1)}, bf16[8,32,1152]{2,1,0:T(8,128)(2,1)S(1)}, u32[]{:S(2)}, u32[]{:S(2)}) collective-permute-start(bf16[8,32,1152]{2,1,0:T(8,128)(2,1)S(1)} %all_to_all.20.packed_ref.refs_0_), channel_id=1, source_target_pairs={{0,1},{1,0},{2,3},{3,2},{4,5},{5,4},{6,7},{7,6},{8,9},{9,8},{10,11... | collective-permute-start | bytes 1769480 | tf_op jit(solution)/shard_map/ppermute | solution.py:23
  27.4 4.7 %collective-permute-start.3 = (bf16[32,1024]{1,0:T(8,128)(2,1)}, bf16[32,1024]{1,0:T(8,128)(2,1)S(1)}, u32[]{:S(2)}, u32[]{:S(2)}) collective-permute-start(bf16[32,1024]{1,0:T(8,128)(2,1)} %refs_0_.1), channel_id=1, source_target_pairs={{0,2},{1,3},{2,0},{3,1},{4,6},{5,7},{6,4},{7,5},{8,10},{9,11},{10,... | collective-permute-start | bytes 196616 | tf_op jit(solution)/shard_map/ppermute | solution.py:23
  32.1 0.8 copy-start.10
  34.5 29.4 %all-to-all-start.1 = ((bf16[8,32,2048]{2,1,0:T(8,128)(2,1)}), bf16[8,32,2048]{2,1,0:T(8,128)(2,1)S(1)}, u32[]{:S(2)}, u32[]{:S(2)}) async-start(bf16[8,32,2048]{2,1,0:T(8,128)(2,1)} %repeat.1), calls=%async_computation.1 | async-start | bytes 2097152 | tf_op jit(solution)/shard_map/all_to_all | solution.py:27
  38.1 25.9 %collective-permute-start.1 = (bf16[8,32,1152]{2,1,0:T(8,128)(2,1)S(1)}, bf16[8,32,1152]{2,1,0:T(8,128)(2,1)S(1)}, u32[]{:S(2)}, u32[]{:S(2)}) collective-permute-start(bf16[8,32,1152]{2,1,0:T(8,128)(2,1)S(1)} %all_to_all.20.packed_ref.refs_0_), channel_id=1, source_target_pairs={{0,2},{1,3},{2,0},{3,1},{4,6},{5,7},{6,4},{7,5},{8,10},{9,11},{10,... | collective-permute-start | bytes 1769480 | tf_op jit(solution)/shard_map/ppermute | solution.py:23
  63.9 14.1 %collective-permute-start.4 = (bf16[8,32,2048]{2,1,0:T(8,128)(2,1)S(1)}, bf16[8,32,2048]{2,1,0:T(8,128)(2,1)S(1)}, u32[]{:S(2)}, u32[]{:S(2)}) collective-permute-start(bf16[8,32,2048]{2,1,0:T(8,128)(2,1)S(1)} %all-to-all-done.1.refs_5_.refs_0_), channel_id=1, source_target_pairs={{0,1},{1,0},{2,3},{3,2},{4,5},{5,4},{6,7},{7,6},{8,9},{9,8},{10,11... | collective-permute-start | bytes 3145736 | tf_op jit(solution)/shard_map/ppermute | solution.py:23
  63.9 32.8 %copy-start.2 = (bf16[8,32,1152]{2,1,0:T(8,128)(2,1)}, bf16[8,32,1152]{2,1,0:T(8,128)(2,1)S(1)}, u32[]{:S(2)}) copy-start(bf16[8,32,1152]{2,1,0:T(8,128)(2,1)S(1)} %collective-permute-done.1.refs_2_) | copy-start | bytes 1769476
  63.9 3.5 %collective-permute-start.2 = (bf16[8,32,1152]{2,1,0:T(8,128)(2,1)S(1)}, bf16[8,32,1152]{2,1,0:T(8,128)(2,1)S(1)}, u32[]{:S(2)}, u32[]{:S(2)}) collective-permute-start(bf16[8,32,1152]{2,1,0:T(8,128)(2,1)S(1)} %collective-permute-done.1.refs_2_), channel_id=1, source_target_pairs={{0,1},{1,0},{2,3},{3,2},{4,5},{5,4},{6,7},{7,6},{8,9},{9,8},{10,11... | collective-permute-start | bytes 1769480 | tf_op jit(solution)/shard_map/ppermute | solution.py:23
  67.4 10.6 %copy-start.4 = (bf16[8,32,1152]{2,1,0:T(8,128)(2,1)}, bf16[8,32,1152]{2,1,0:T(8,128)(2,1)S(1)}, u32[]{:S(2)}) copy-start(bf16[8,32,1152]{2,1,0:T(8,128)(2,1)S(1)} %collective-permute-done.2.refs_3_) | copy-start | bytes 1769476
  96.8 18.5 %copy-start.6 = (bf16[256,3072]{1,0:T(8,128)(2,1)}, bf16[256,3072]{1,0:T(8,128)(2,1)S(1)}, u32[]{:S(2)}) copy-start(bf16[256,3072]{1,0:T(8,128)(2,1)S(1)} %get-tuple-element.26.grad_ref) | copy-start | bytes 4718596
  96.8 8.4 %collective-permute-start.5 = (bf16[2,256,1024]{2,1,0:T(8,128)(2,1)S(1)}, bf16[2,256,1024]{2,1,0:T(8,128)(2,1)S(1)}, u32[]{:S(2)}, u32[]{:S(2)}) collective-permute-start(bf16[2,256,1024]{2,1,0:T(8,128)(2,1)S(1)} %get-tuple-element.22), channel_id=1, source_target_pairs={{0,1},{1,0},{2,3},{3,2},{4,5},{5,4},{6,7},{7,6},{8,9},{9,8},{10,11... | collective-permute-start | bytes 3145736 | tf_op jit(solution)/shard_map/ppermute | solution.py:23
  104.8 10.5 %collective-permute-start.7 = (bf16[2,256,1024]{2,1,0:T(8,128)(2,1)S(1)}, bf16[2,256,1024]{2,1,0:T(8,128)(2,1)S(1)}, u32[]{:S(2)}, u32[]{:S(2)}) collective-permute-start(bf16[2,256,1024]{2,1,0:T(8,128)(2,1)S(1)} %back_odd.1.refs_2_), channel_id=1, source_target_pairs={{0,1},{1,0},{2,3},{3,2},{4,5},{5,4},{6,7},{7,6},{8,9},{9,8},{10,11... | collective-permute-start | bytes 3145736 | tf_op jit(solution)/shard_map/ppermute | solution.py:23
  105.9 23.3 %collective-permute-start.6 = (bf16[256,1024]{1,0:T(8,128)(2,1)S(1)}, bf16[256,1024]{1,0:T(8,128)(2,1)S(1)}, u32[]{:S(2)}, u32[]{:S(2)}) collective-permute-start(bf16[256,1024]{1,0:T(8,128)(2,1)S(1)} %mix_1.1.refs_0_), channel_id=1, source_target_pairs={{0,2},{1,3},{2,0},{3,1},{4,6},{5,7},{6,4},{7,5},{8,10},{9,11},{10,... | collective-permute-start | bytes 1572872 | tf_op jit(solution)/shard_map/ppermute | solution.py:23
  115.9 1.0 copy-start
  116.9 13.8 %copy-start.8 = (bf16[256,1024]{1,0:T(8,128)(2,1)}, bf16[256,1024]{1,0:T(8,128)(2,1)S(1)}, u32[]{:S(2)}) copy-start(bf16[256,1024]{1,0:T(8,128)(2,1)S(1)} %back_1.1.refs_2_) | copy-start | bytes 1572868
  130.8 20.3 %all-to-all-start.2 = ((bf16[8,32,1024]{2,1,0:T(8,128)(2,1)}), bf16[8,32,1024]{2,1,0:T(8,128)(2,1)S(1)}, u32[]{:S(2)}, u32[]{:S(2)}) async-start(bf16[8,32,1024]{2,1,0:T(8,128)(2,1)} %bitcast.3), calls=%async_computation.2 | async-start | bytes 1048576 | tf_op jit(solution)/shard_map/all_to_all | solution.py:27
  134.4 13.9 %collective-permute-start.8 = (bf16[256,1024]{1,0:T(8,128)(2,1)}, bf16[256,1024]{1,0:T(8,128)(2,1)S(1)}, u32[]{:S(2)}, u32[]{:S(2)}) collective-permute-start(bf16[256,1024]{1,0:T(8,128)(2,1)} %copy-done.8), channel_id=1, source_target_pairs={{0,2},{1,3},{2,0},{3,1},{4,6},{5,7},{6,4},{7,5},{8,10},{9,11},{10,... | collective-permute-start | bytes 1572872 | tf_op jit(solution)/shard_map/ppermute | solution.py:23
  148.2 1.2 copy-start.1
  151.0 24.0 %all-to-all-start.3 = ((bf16[8,32,1024]{2,1,0:T(8,128)(2,1)}), bf16[8,32,1024]{2,1,0:T(8,128)(2,1)S(1)}, u32[]{:S(2)}, u32[]{:S(2)}) async-start(bf16[8,32,1024]{2,1,0:T(8,128)(2,1)} %bitcast.4), calls=%async_computation.3 | async-start | bytes 1048576 | tf_op jit(solution)/shard_map/all_to_all | solution.py:27
  156.6 1.1 copy-start.3
  157.7 1.1 copy-start.5
  158.7 1.4 copy-start.7

commit v7 on v6

--- a/solution.py
+++ b/solution.py
@@ -27,13 +27,17 @@
     return lax.all_to_all(blocks, "expert", split_axis=0, concat_axis=0, tiled=True)
 
 
-def gather_chunks(value):
+def far_chunks(value):
     chunks = {0: value}
     bit = lax.axis_size("tensor") // 2
-    while bit:
+    while bit > 1:
         chunks.update({s | bit: swap(c, "tensor", bit) for s, c in list(chunks.items())})
         bit //= 2
-    return [chunks[s] for s in range(len(chunks))]
+    return [chunks[s] for s in sorted(chunks)]
+
+
+def with_pairs(chunks):
+    return [part for chunk in chunks for part in (chunk, swap(chunk, "tensor", 1))]
 
 
 def scatter_rows(value, rows):
@@ -88,7 +92,7 @@
         rows_ref[s] = dot(to_row_ref[...], flat_rows(held_ref[s])).astype(BF16)
 
 
-def pack_kernel(me_ref, token_ref, routing_ref, gates_ref, out_ref):
+def pack_kernel(me_ref, token_ref, cot_ref, routing_ref, gates_ref, out_ref):
     _, width = token_ref.shape
     top = routing_ref.shape[1]
     gates = gates_ref[...]
@@ -103,15 +107,8 @@
     ).astype(BF16)
     for group in range(out_ref.shape[0]):
         out_ref[group, :, :width] = token_ref[...]
-        out_ref[group, :, width:] = packed
-
-
-def repeat_kernel(count, me_ref, *refs):
-    parts, out_ref = refs[:count], refs[-1]
-    width = parts[0].shape[1]
-    for i, part in enumerate(parts):
-        for group in range(out_ref.shape[0]):
-            out_ref[group, :, i * width : (i + 1) * width] = part[...]
+        out_ref[group, :, width : 2 * width] = cot_ref[...]
+        out_ref[group, :, 2 * width :] = packed
 
 
 def plan_kernel(top, local, me_ref, packed_ref, to_token_ref, to_row_ref, gate_ref):
@@ -149,10 +146,10 @@
     gate_ref[...] = jnp.sum(jnp.where(own, gates, 0.0), axis=1, keepdims=True)
 
 
-def preact_kernel(n, steps, me_ref, to_row_ref, gate_ref, *refs):
-    xs, w_ref = refs[:n], refs[n]
-    act_ref, spread_ref, slope_ref, held_ref, rows_ref, x_sems, buffer, sems = refs[-8:]
-    room, width, depth = act_ref.shape[0], rows_ref.shape[2], buffer.shape[0]
+def early_kernel(count, steps, me_ref, to_row_ref, *refs):
+    xs, w_ref = refs[:count], refs[count]
+    part_ref, held_ref, rows_ref, x_sems, buffer, sems = refs[count + 1 :]
+    room, width, depth = part_ref.shape[0], rows_ref.shape[2], buffer.shape[0]
     e = pl.program_id(0)
 
     def copies(step):
@@ -161,7 +158,7 @@
             pltpu.make_async_copy(
                 w_ref.at[step, block(me_ref[0] ^ s, width), :], buffer.at[slot, s], sems.at[slot, s]
             )
-            for s in range(n)
+            for s in range(count)
         ]
 
     stream(copies, e, steps, depth)
@@ -172,19 +169,78 @@
 
     for copy in copies(e):
         copy.wait()
-    pre = sum(dot(rows_ref[s, block(e, room), :], buffer[e % depth, s]) for s in range(n))
+    part_ref[...] = sum(
+        dot(rows_ref[s, block(e, room), :], buffer[e % depth, s]) for s in range(count)
+    )
+
+
+def front_kernel(
+    n, begin, steps, me_ref, to_token_ref, to_row_ref, gate_ref, part_ref, *refs
+):
+    count = n - begin
+    xs, w_in_ref, w_out_ref = refs[:count], refs[count], refs[count + 1]
+    act_ref, spread_ref, slope_ref = refs[count + 2 : count + 5]
+    sums = refs[count + 5 : count + 7]
+    held_ref, rows_ref, x_sems, out_rows_ref = refs[count + 7 : count + 11]
+    in_buffer, in_sems, out_buffer, out_sems = refs[count + 11 :]
+    room, hid = act_ref.shape
+    width, depth = rows_ref.shape[2], in_buffer.shape[0]
+    e = pl.program_id(0)
+
+    def in_copies(step):
+        slot = step % depth
+        return [
+            pltpu.make_async_copy(
+                w_in_ref.at[step, block(me_ref[0] ^ (begin + i), width), :],
+                in_buffer.at[slot, i],
+                in_sems.at[slot, i],
+            )
+            for i in range(count)
+        ]
+
+    def out_copies(step):
+        slot = step % depth
+        return [
+            pltpu.make_async_copy(
+                w_out_ref.at[block(step, hid), block(me_ref[0] ^ s, width)],
+                out_buffer.at[slot, s],
+                out_sems.at[slot, s],
+            )
+            for s in range(n)
+        ]
+
+    stream(lambda step: in_copies(step) + out_copies(step), e, steps, depth)
+
+    @pl.when(e == 0)
+    def _():
+        gather(to_row_ref, [(x, 0) for x in xs], held_ref, rows_ref, x_sems)
+
+    here = block(e, room)
+    for copy in in_copies(e):
+        copy.wait()
+    pre = part_ref[...]
+    for i in range(count):
+        pre = pre + dot(rows_ref[i, here, :], in_buffer[e % depth, i])
     sig = jax.nn.sigmoid(pre)
     gate = gate_ref[...]
     act = (gate * (pre * sig)).astype(BF16)
     act_ref[...] = act
-    spread_ref[...] = dot(to_row_ref[block(e, room), :], act, ((0,), (0,))).astype(BF16)
+    spread_ref[...] = dot(to_row_ref[here, :], act, ((0,), (0,))).astype(BF16)
     slope_ref[...] = gate * (sig * (1.0 + pre * (1.0 - sig)))
-
-
-def middle_kernel(n, steps, me_ref, to_token_ref, to_row_ref, slope_ref, act_ref, *refs):
-    ys, w_ref = refs[:2], refs[2]
-    sums, (grad_ref, spread_ref) = refs[3:5], refs[5:7]
-    held_ref, rows_ref, y_sems, out_rows_ref, buffer, sems = refs[7:]
+    for s, copy in enumerate(out_copies(e)):
+        copy.wait()
+        out_rows_ref[s, here, :] = dot(act, out_buffer[e % depth, s]).astype(BF16)
+
+    @pl.when(e == steps - 1)
+    def _():
+        for s in range(n):
+            total = dot(to_token_ref[...], out_rows_ref[s])
+            sums[s % 2][s // 2] = total.astype(BF16)
+
+
+def slope_kernel(n, steps, me_ref, to_row_ref, slope_ref, *refs):
+    ys, w_ref = refs[:n], refs[n]
+    grad_ref, spread_ref, held_ref, rows_ref, y_sems, buffer, sems = refs[-7:]
     room, hid = grad_ref.shape
     width, depth = rows_ref.shape[2], buffer.shape[0]
     e = pl.program_id(0)
@@ -204,39 +260,32 @@
 
     @pl.when(e == 0)
     def _():
-        sources = [(ys[s % 2], s // 2 * width) for s in range(n)]
-        gather(to_row_ref, sources, held_ref, rows_ref, y_sems)
-
-    for copy in copies(e):
-        copy.wait()
+        gather(to_row_ref, [(y, 0) for y in ys], held_ref, rows_ref, y_sems)
+
     here = block(e, room)
     grad = 0.0
-    for s in range(n):
-        weights = buffer[e % depth, s]
-        out_rows_ref[s, here, :] = dot(act_ref[...], weights).astype(BF16)
-        grad = grad + dot(weights, rows_ref[s, here, :], ((1,), (1,)))
+    for s, copy in enumerate(copies(e)):
+        copy.wait()
+        grad = grad + dot(buffer[e % depth, s], rows_ref[s, here, :], ((1,), (1,)))
     grad = (grad.T * slope_ref[...]).astype(BF16)
     grad_ref[...] = grad
     spread_ref[...] = dot(to_row_ref[here, :], grad, ((0,), (0,))).astype(BF16)
 
-    @pl.when(e == steps - 1)
-    def _():
-        for s in range(n):
-            total = dot(to_token_ref[...], out_rows_ref[s])
-            sums[s % 2][s // 2] = total.astype(BF16)
-
-
-def back_kernel(steps, per, odd, me_ref, to_token_ref, grad_ref, w_ref, *refs):
-    out_ref, rows_ref, buffer, sems = refs[-4:]
+
+def back_kernel(steps, per, me_ref, to_token_ref, grad_ref, w_ref, *refs):
+    odd_ref, even_ref, rows_ref, buffer, sems = refs[-5:]
     depth, pairs, cols, wide = buffer.shape
     hid = grad_ref.shape[1]
     group = wide // hid
     room = rows_ref.shape[1] // (pairs * group)
     step = pl.program_id(0)
+    half = steps // 2
 
     def copies(step):
         slot = step % depth
-        column = (me_ref[0] ^ (2 * (step // per) + odd)) * per + step % per
+        late = (step >= half).astype(jnp.int32) if not isinstance(step, int) else int(step >= half)
+        inside = step - late * half
+        column = (me_ref[0] ^ (2 * (inside // per) + 1 - late)) * per + inside % per
         return [
             pltpu.make_async_copy(
                 w_ref.at[p * group + i, block(column, cols), :],
@@ -260,7 +309,15 @@
         corner = jnp.concatenate(corners, axis=0) if group > 1 else corners[0]
         part = dot(buffer[step % depth, p], corner, ((1,), (1,)))
         rows_ref[:, p * group * room : (p + 1) * group * room] = part.astype(BF16)
-    out_ref[0] = dot(to_token_ref[...], rows_ref[...], ((1,), (1,))).astype(BF16)
+    total = dot(to_token_ref[...], rows_ref[...], ((1,), (1,))).astype(BF16)
+
+    @pl.when(step < half)
+    def _():
+        odd_ref[0] = total
+
+    @pl.when(step >= half)
+    def _():
+        even_ref[0] = total
 
 
 def add_kernel(count, me_ref, *refs):
@@ -293,7 +350,7 @@
 
 
 def d_out_kernel(n, steps, me_ref, act_ref, *refs):
-    ys, (out_ref, done_ref, buffer, sems) = refs[:2], refs[-4:]
+    ys, (out_ref, done_ref, buffer, sems) = refs[:n], refs[-4:]
     e = pl.program_id(0)
     _, n, hid, width = buffer.shape
     act = act_ref[...].T
@@ -302,8 +359,7 @@
 
     def values():
         for s in range(n):
-            start = s // 2 * width
-            yield dot(act, flat_rows(ys[s % 2][:, :, start : start + width]))
+            yield dot(act, flat_rows(ys[s][...]))
 
     write_step(e, steps, values, outs, buffer, sems)
 
@@ -392,38 +448,17 @@
         pack_kernel,
         "pack",
         (1,),
-        [once(rows, quarter), once(rows, top), once(rows, top)],
-        once(groups, rows, quarter + LANES),
-        jax.ShapeDtypeStruct((groups, rows, quarter + LANES), BF16),
-        (me, tokens, routing, gates),
+        [once(rows, quarter)] * 2 + [once(rows, top)] * 2,
+        once(groups, rows, 2 * quarter + LANES),
+        jax.ShapeDtypeStruct((groups, rows, 2 * quarter + LANES), BF16),
+        (me, tokens, cotangent, routing, gates),
         0,
-        24 if big else 4,
+        32 if big else 6,
     )
     left = exchange_rows(packed)
-    xs = gather_chunks(left)
-    raw = {0: cotangent}
-    bit = n // 2
-    while bit > 1:
-        raw.update({k | bit: swap(c, "tensor", bit) for k, c in list(raw.items())})
-        bit //= 2
-    raw = [raw[k] for k in sorted(raw)]
-    wide = len(raw) * quarter
-    even_y = exchange_rows(
-        call(
-            functools.partial(repeat_kernel, len(raw)),
-            "repeat",
-            (1,),
-            [once(rows, quarter)] * len(raw),
-            once(groups, rows, wide),
-            jax.ShapeDtypeStruct((groups, rows, wide), BF16),
-            (me, *raw),
-            0,
-            24 if big else 6,
-            (),
-            (xs[1],),
-        )
-    )
-    ys = (even_y, swap(even_y, "tensor", 1))
+    x_far = far_chunks(left[:, :, :quarter])
+    x_near = [x_far[0], swap(x_far[0], "tensor", 1)]
+    ys = with_pairs(far_chunks(left[:, :, quarter : 2 * quarter]))
     to_token, to_row, gate = call(
         functools.partial(plan_kernel, top, local),
         "plan",
@@ -431,7 +466,7 @@
         [
             pl.BlockSpec(
                 (groups, rows, LANES),
-                lambda i, me: (0, 0, quarter // LANES),
+                lambda i, me: (0, 0, 2 * quarter // LANES),
                 pipeline_mode=pl.Buffered(1),
             )
         ],
@@ -455,63 +490,96 @@
         ]
 
     chunk_specs = [once(groups, rows, quarter)] * n
-    loose = [ANYWHERE] * n + [IN_HBM]
     row_block = pl.BlockSpec((room, hid), lambda e, me: (e, 0))
     dense_block = pl.BlockSpec((total, hid), lambda e, me: (0, e))
     row_shape = jax.ShapeDtypeStruct((slots, hid), BF16)
-    gathered = [
-        pltpu.VMEM((n, groups, rows, quarter), BF16),
-        pltpu.VMEM((n, slots, quarter), BF16),
-        pltpu.SemaphoreType.DMA((n,)),
-    ]
+
+    def gathered(count):
+        return [
+            pltpu.VMEM((count, groups, rows, quarter), BF16),
+            pltpu.VMEM((count, slots, quarter), BF16),
+            pltpu.SemaphoreType.DMA((count,)),
+        ]
+
     w_in = pltpu.with_memory_space_constraint(w_in, pltpu.HBM)
     flat_out = pltpu.with_memory_space_constraint(
         w_out.reshape(local * hid, width), pltpu.HBM
     )
-    act, act_dense, slope = call(
-        functools.partial(preact_kernel, n, local),
-        "preact",
+    begin = len(x_near)
+    part = call(
+        functools.partial(early_kernel, begin, local),
+        "preact_early",
         (local,),
-        [once(slots, total), pl.BlockSpec((room, 1), lambda e, me: (e, 0))] + loose,
-        [row_block, dense_block, row_block],
-        [row_shape, dense, jax.ShapeDtypeStruct((slots, hid), F32)],
-        (me, to_row, gate, *xs, w_in),
+        [once(slots, total)] + [ANYWHERE] * begin + [IN_HBM],
+        row_block,
+        jax.ShapeDtypeStruct((slots, hid), F32),
+        (me, to_row, *x_near, w_in),
+        flops // 2,
+        limit,
+        gathered(begin) + ring(begin, quarter, hid),
+    )
+    *x_far, part = lax.optimization_barrier((*x_far[1:], part))
+    xs = x_near + with_pairs(x_far)
+    sum_spec = once(n // 2, total, quarter)
+    sum_shape = jax.ShapeDtypeStruct((n // 2, total, quarter), BF16)
+    act, act_dense, slope, mix_even, mix_odd = call(
+        functools.partial(front_kernel, n, begin, local),
+        "front",
+        (local,),
+        [
+            once(total, slots),
+            once(slots, total),
+            pl.BlockSpec((room, 1), lambda e, me: (e, 0)),
+            row_block,
+        ]
+        + [ANYWHERE] * (n - begin)
+        + [IN_HBM] * 2,
+        [row_block, dense_block, row_block, sum_spec, sum_spec],
+        [row_shape, dense, jax.ShapeDtypeStruct((slots, hid), F32), sum_shape, sum_shape],
+        (me, to_token, to_row, gate, part, *xs[begin:], w_in, flat_out),
+        2 * flops,
+        56 if big else 30,
+        gathered(n - begin)
+        + [pltpu.VMEM((n, slots, quarter), BF16)]
+        + ring(n - begin, quarter, hid)
+        + ring(n, hid, quarter),
+    )
+    grad, grad_dense = call(
+        functools.partial(slope_kernel, n, local),
+        "grad_preact",
+        (local,),
+        [once(slots, total), row_block] + [ANYWHERE] * n + [IN_HBM],
+        [row_block, dense_block],
+        [row_shape, dense],
+        (me, to_row, slope, *ys, flat_out),
         flops,
         limit,
-        gathered + ring(n, quarter, hid),
-        (even_y,),
+        gathered(n) + ring(n, hid, quarter),
     )
     cols = min(512, quarter)
     per = quarter // cols
-    steps = n // 2 * per
+    steps = n * per
+    half = steps // 2
     group = 2 if local % 2 == 0 else 1
-    sum_spec = once(n // 2, total, quarter)
-    sum_shape = jax.ShapeDtypeStruct((n // 2, total, quarter), BF16)
-    mix_even, mix_odd, grad, grad_dense = call(
-        functools.partial(middle_kernel, n, local),
-        "middle",
-        (local,),
-        [once(total, slots), once(slots, total), row_block, row_block]
-        + [ANYWHERE] * 2
-        + [IN_HBM],
-        [sum_spec, sum_spec, row_block, dense_block],
-        [sum_shape, sum_shape, row_shape, dense],
-        (me, to_token, to_row, slope, act, *ys, flat_out),
-        2 * flops,
-        56 if big else 30,
-        gathered + [pltpu.VMEM((n, slots, quarter), BF16)] + ring(n, hid, quarter),
-    )
-
-    def back(name, odd, after=()):
+
+    def odd_block(i, me):
+        i = jnp.minimum(i, half - 1)
+        return i // per, 0, i % per
+
+    def even_block(i, me):
+        i = jnp.maximum(i - half, 0)
+        return i // per, 0, i % per
+
+    def back(after):
         return call(
-            functools.partial(back_kernel, steps, per, odd),
-            name,
+            functools.partial(back_kernel, steps, per),
+            "back",
             (steps,),
             [once(total, slots), once(slots, hid), IN_HBM],
-            pl.BlockSpec((1, total, cols), lambda i, me: (i // per, 0, i % per)),
-            sum_shape,
+            [pl.BlockSpec((1, total, cols), odd_block), pl.BlockSpec((1, total, cols), even_block)],
+            [sum_shape, sum_shape],
             (me, to_token, grad, w_in),
-            flops // 2,
+            flops,
             limit,
             [pltpu.VMEM((cols, slots), BF16)]
             + [
@@ -568,17 +636,18 @@
             count, bit = half, bit // 2
         return add(f"{name}_sum", values, specs, after)
 
-    back_odd = back("back_odd", 1)
-    mix_got, mix_sent = pass_on("mix", mix_even, mix_odd, (back_odd,))
-    back_even = back("back_even", 0, tuple(mix_sent.values()))
-    back_got, back_sent = pass_on("back", back_even, back_odd)
+    mix_got, mix_sent = pass_on("mix", mix_even, mix_odd, (grad,))
+    back_odd, back_even = back(tuple(mix_sent.values()))
+    mix_sum = gather_sum("mix", mix_even, mix_got, mix_sent, (back_odd,))
+    mixed = scatter_rows(mix_sum, rows).astype(BF16)
+    back_got, back_sent = pass_on("back", back_even, back_odd, (mix_sum,))
 
     sems = pltpu.SemaphoreType.DMA((2, n))
     d_w_out, done = call(
         functools.partial(d_out_kernel, n, local),
         "d_w_out",
         (local,),
-        [dense_block] + [once(groups, rows, wide)] * 2,
+        [dense_block] + chunk_specs,
         [IN_HBM, once(8, 128)],
         [placed(pltpu.HBM, (local * hid, width)), jax.ShapeDtypeStruct((8, 128), F32)],
         (me, act_dense, *ys),
@@ -587,9 +656,7 @@
         [pltpu.VMEM((2, n, hid, quarter), BF16), sems],
         tuple(back_sent.values()),
     )
-    mix_sum = gather_sum("mix", mix_even, mix_got, mix_sent, (done,))
-    mixed = scatter_rows(mix_sum, rows).astype(BF16)
-    back_sum = gather_sum("back", back_even, back_got, back_sent, (mix_sum,))
+    back_sum = gather_sum("back", back_even, back_got, back_sent, (done,))
     d_tokens = scatter_rows(back_sum, rows).astype(BF16)
     d_w_in = call(
         functools.partial(d_in_kernel, n, local // group),

time: 176 us -> 177 us (level)
  waiting for transfers between devices: 41.5 us -> 20.4 us
  Pallas kernels: 80.2 us -> 94.6 us
  blocking collectives: 23.6 us -> 34.9 us
  local copies, waits for them, and re-layouts: 8.96 us -> 6.15 us
    all_to_all x3 -> x2, waiting for transfers between devices: 24.3 us -> 0.01 us  [exchange_rows(): lax.all_to_all(blocks, 'expert', split_axis=0, concat_axis=0, tiled=True)]
    pallas_call x13 -> x12, Pallas kernels: 80.2 us -> 94.6 us  [call(): pl.pallas_call(kernel, grid_spec=pltpu.PrefetchScalarGridSpec(num_scalar_...]
    all_to_all x1, blocking collectives: 23.6 us -> 34.9 us  [exchange_rows(): lax.all_to_all(blocks, 'expert', split_axis=0, concat_axis=0, tiled=True)]
    ppermute x9 -> x10, waiting for transfers between devices: 17.3 us -> 20.4 us  [swap(): return lax.ppermute(value, axis, [(i, i ^ bits) for i in range(size)])]
    unnamed x24 -> x38, local copies, waits for them, and re-layouts: 8.96 us -> 6.07 us
    all_to_all x3 -> x2, starting transfers between devices: 12.7 us -> 10.2 us  [exchange_rows(): lax.all_to_all(blocks, 'expert', split_axis=0, concat_axis=0, tiled=True)]
    ppermute x9 -> x10, starting transfers between devices: 6.36 us -> 7.21 us  [swap(): return lax.ppermute(value, axis, [(i, i ^ bits) for i in range(size)])]
  transfers between devices with their start and end apart: 12 -> 12, of which waited for: 4 -> 5; matrix products, arithmetic and copies ran while one was open for 0% -> 1% of each run, Pallas kernels for 33% -> 45%
where the time goes in v7:
time: 177 us
  Pallas kernels  94.6 us (53%)
  blocking collectives  34.9 us (20%)
  waiting for transfers between devices  20.4 us (12%)
  starting transfers between devices  17.4 us (10%)
  local copies, waits for them, and re-layouts  6.15 us (3%)
  other arithmetic  2.55 us (1%)
    pallas_call x12, Pallas kernels, call(): pl.pallas_call(kernel, grid_spec=pltpu.PrefetchScalarGridSpec(num_scalar_...  94.6 us
    all_to_all x1, blocking collectives, exchange_rows(): lax.all_to_all(blocks, 'expert', split_axis=0, concat_axis=0, tiled=True)  34.9 us
    ppermute x10, waiting for transfers between devices, swap(): return lax.ppermute(value, axis, [(i, i ^ bits) for i in range(size)])  20.4 us
    all_to_all x2, starting transfers between devices, exchange_rows(): lax.all_to_all(blocks, 'expert', split_axis=0, concat_axis=0, tiled=True)  10.2 us
    ppermute x10, starting transfers between devices, swap(): return lax.ppermute(value, axis, [(i, i ^ bits) for i in range(size)])  7.21 us
    unnamed x38, local copies, waits for them, and re-layouts  6.07 us
  transfers between devices with their start and end apart: 12, of which 5 were waited for; matrix products, arithmetic and copies ran while one was open for 1% of the time, Pallas kernels for 45%

profile of v7, /device:TPU:0, one launch (start us, length us, event | category | flops | bytes accessed | tf_op | source)
XLA Modules:
  0.0 176.8 jit_solution(10711703184279493959)
XLA Ops:
  0.6 0.8 copy.10.routing_ref
  1.4 0.8 copy.11.gates_ref
  2.2 0.1 pad_add_fusion.me_ref
  2.2 0.8 copy-done.14
  3.1 0.8 copy-done.15
  3.9 0.7 pack.1
  4.6 34.9 %all_to_all.15.packed_ref = bf16[8,32,2176]{2,1,0:T(8,128)(2,1)S(1)} all-to-all(bf16[8,32,2176]{2,1,0:T(8,128)(2,1)S(1)} %pack.1), channel_id=1, replica_groups=mesh['expert'=8,'tensor'=4] {'expert'}, dimensions={0} | all-to-all | bytes 2228224 | tf_op jit(solution)/shard_map/all_to_all | solution.py:27
  39.5 0.1 fusion
  39.5 0.1 collective-permute-start.1
  39.6 1.6 collective-permute-start
  41.2 2.3 %plan.1 = (bf16[256,512]{1,0:T(8,128)(2,1)S(1)}, bf16[512,256]{1,0:T(8,128)(2,1)S(1)}, f32[512,1]{1,0:T(8,128)S(1)}) custom-call(s32[2]{0:T(128)S(1)} %pad_add_fusion.me_ref, bf16[8,32,2176]{2,1,0:T(8,128)(2,1)S(1)} %all_to_all.15.packed_ref), custom_call_target="tpu_custom_call" | custom-call | bytes 1640456 | tf_op jit(solution)/shard_map/plan/pallas_call | solution.py:411
  43.5 0.0 collective-permute-done.1.refs_1_
  43.5 6.7 %preact_early.1.part_ref = f32[512,384]{1,0:T(8,128)S(1)} custom-call(s32[2]{0:T(128)S(1)} %pad_add_fusion.me_ref, bf16[512,256]{1,0:T(8,128)(2,1)S(1)} %get-tuple-element.20.to_row_ref, bf16[8,32,1024]{2,1,0:T(8,128)(2,1)S(1)} %get-tuple-element.35.refs_0_, bf16[8,32,1024]{2,1,0:T(8,128)(2,1)S(1)} %collective-permute-done.1.refs_1_, bf16[8,4096,384]{2,1,0:T(8,128)(2,1)} %w_ref.1), custom_call_target="tpu_custom_call" | custom-call | flops 805306368 | bytes 27262984 | tf_op jit(solution)/shard_map/preact_early/pallas_call | solution.py:411
  50.2 3.8 %collective-permute-done.refs_0_.refs_2_ = bf16[8,32,1024]{2,1,0:T(8,128)(2,1)S(1)} collective-permute-done((bf16[8,32,1024]{2,1,0:T(8,128)(2,1)S(1)}, bf16[8,32,1024]{2,1,0:T(8,128)(2,1)S(1)}, u32[]{:S(2)}, u32[]{:S(2)}) %collective-permute-start) | collective-permute-done | bytes 524320 | tf_op jit(solution)/shard_map/ppermute | solution.py:23
  54.0 0.0 collective-permute-start.2
  54.0 1.5 collective-permute-start.5
  55.5 0.4 collective-permute-done.2.refs_1_.refs_3_
  55.9 20.1 %front.1 = (bf16[512,384]{1,0:T(8,128)(2,1)}, bf16[256,3072]{1,0:T(8,128)(2,1)S(1)}, f32[512,384]{1,0:T(8,128)S(1)}, bf16[2,256,1024]{2,1,0:T(8,128)(2,1)S(1)}, bf16[2,256,1024]{2,1,0:T(8,128)(2,1)S(1)}) custom-call(s32[2]{0:T(128)S(1)} %pad_add_fusion.me_ref, bf16[256,512]{1,0:T(8,128)(2,1)S(1)} %get-tuple-element.19.to_token_ref, ...), custom_call_target="tpu_custom_call" | custom-call | flops 3221225472 | bytes 57542664 | tf_op jit(solution)/shard_map/front/pallas_call | solution.py:411
  76.0 0.0 copy-start.16
  76.0 0.2 collective-permute-start.3
  76.2 0.4 collective-permute-start.4
  76.6 0.0 collective-permute-done.5.refs_2_
  76.6 0.1 collective-permute-start.6
  76.7 2.8 %collective-permute-done.4.refs_1_ = bf16[8,32,1024]{2,1,0:T(8,128)(2,1)S(1)} collective-permute-done((bf16[8,32,1024]{2,1,0:T(8,128)(2,1)S(1)}, bf16[8,32,1024]{2,1,0:T(8,128)(2,1)S(1)}, u32[]{:S(2)}, u32[]{:S(2)}) %collective-permute-start.4) | collective-permute-done | bytes 524320 | tf_op jit(solution)/shard_map/ppermute | solution.py:23
  79.5 0.7 collective-permute-done.6.refs_3_
  80.2 20.5 %grad_preact.1 = (bf16[512,384]{1,0:T(8,128)(2,1)S(1)}, bf16[256,3072]{1,0:T(8,128)(2,1)S(1)}) custom-call(s32[2]{0:T(128)S(1)} %pad_add_fusion.me_ref, bf16[512,256]{1,0:T(8,128)(2,1)S(1)} %get-tuple-element.20.to_row_ref, f32[512,384]{1,0:T(8,128)S(1)} %get-tuple-element.26.slope_ref, bf16[8,32,1024]{2,1,0:T(8,128)(2,1)S(1)} %get-tuple-element.34.refs_0_, ...), custom_call_target="tpu_custom_call" | custom-call | flops 1610612736 | bytes 30277640 | tf_op jit(solution)/shard_map/grad_preact/pallas_call | solution.py:411
  100.7 0.0 collective-permute-done.3.refs_1_
  100.8 0.7 mix_1.1.refs_0_
  101.4 14.1 %back.1 = (bf16[2,256,1024]{2,1,0:T(8,128)(2,1)}, bf16[2,256,1024]{2,1,0:T(8,128)(2,1)S(1)}) custom-call(s32[2]{0:T(128)S(1)} %pad_add_fusion.me_ref, bf16[256,512]{1,0:T(8,128)(2,1)S(1)} %get-tuple-element.19.to_token_ref, bf16[512,384]{1,0:T(8,128)(2,1)S(1)} %get-tuple-element.27.refs_2_.grad_ref, bf16[8,4096,384]{2,1,0:T(8,128)(2,1)} %w_ref.1, ...), custom_call_target="tpu_custom_call" | custom-call | flops 1610612736 | bytes 27918344 | tf_op jit(solution)/shard_map/back/pallas_call | solution.py:411
  115.5 0.2 collective-permute-start.8
  115.7 1.5 collective-permute-start.7
  117.3 12.7 %collective-permute-done.7.refs_2_ = bf16[256,1024]{1,0:T(8,128)(2,1)S(1)} collective-permute-done((bf16[256,1024]{1,0:T(8,128)(2,1)S(1)}, bf16[256,1024]{1,0:T(8,128)(2,1)S(1)}, u32[]{:S(2)}, u32[]{:S(2)}) %collective-permute-start.7) | collective-permute-done | bytes 524320 | tf_op jit(solution)/shard_map/ppermute | solution.py:23
  129.9 1.5 mix_sum.1.refs_2_
  131.5 4.3 %all-to-all-start.1 = ((bf16[8,32,1024]{2,1,0:T(8,128)(2,1)}), bf16[8,32,1024]{2,1,0:T(8,128)(2,1)}, u32[]{:S(2)}, u32[]{:S(2)}) async-start(bf16[8,32,1024]{2,1,0:T(8,128)(2,1)} %bitcast.3), calls=%async_computation.1 | async-start | bytes 1048576 | tf_op jit(solution)/shard_map/all_to_all | solution.py:27
  135.8 0.0 collective-permute-done.8.refs_1_
  135.9 0.7 back_1.1.refs_4_
  136.5 1.6 collective-permute-start.9
  138.1 0.0 copy-start.17
  138.1 1.4 copy-done.17
  139.5 12.3 %d_w_out.1 = (bf16[3072,4096]{1,0:T(8,128)(2,1)}, f32[8,128]{1,0:T(8,128)S(1)}) custom-call(s32[2]{0:T(128)S(1)} %pad_add_fusion.me_ref, bf16[256,3072]{1,0:T(8,128)(2,1)S(1)} %copy-done.17, bf16[8,32,1024]{2,1,0:T(8,128)(2,1)S(1)} %copy-done.5, bf16[8,32,1024]{2,1,0:T(8,128)(2,1)S(1)} %copy-done.11, bf16[8,32,1024]{2,1,0:T(8,128)(2,1)S(1)} %copy-done.9, ...), custom_call_target="tpu_custom_call" | custom-call | flops 6442450944 | bytes 28839944 | tf_op jit(solution)/shard_map/d_w_out/pallas_call | solution.py:411
  151.8 0.0 collective-permute-done.9.refs_2_
  151.8 1.5 back_sum.1.refs_4_
  153.4 0.0 all-to-all-done.1
  153.4 5.8 %all-to-all-start.2 = ((bf16[8,32,1024]{2,1,0:T(8,128)(2,1)}), bf16[8,32,1024]{2,1,0:T(8,128)(2,1)S(1)}, u32[]{:S(2)}, u32[]{:S(2)}) async-start(bf16[8,32,1024]{2,1,0:T(8,128)(2,1)} %bitcast.4), calls=%async_computation.2 | async-start | bytes 1048576 | tf_op jit(solution)/shard_map/all_to_all | solution.py:27
  159.2 1.8 reduce_sum.24
  161.0 1.4 copy-done.7
  162.4 13.7 %d_w_in.1 = bf16[8,4096,384]{2,1,0:T(8,128)(2,1)} custom-call(s32[2]{0:T(128)S(1)} %pad_add_fusion.me_ref, bf16[256,3072]{1,0:T(8,128)(2,1)S(1)} %copy-done.7, bf16[8,32,1024]{2,1,0:T(8,128)(2,1)S(1)} %get-tuple-element.35.refs_0_, bf16[8,32,1024]{2,1,0:T(8,128)(2,1)S(1)} %copy-done.3, bf16[8,32,1024]{2,1,0:T(8,128)(2,1)S(1)} %collective-permute-done.refs_0_.refs_2_, ...), custom_call_target="tpu_custom_call" | custom-call | flops 6442450944 | bytes 28835848 | tf_op jit(solution)/shard_map/d_w_in/pallas_call | solution.py:411
  176.1 0.7 reduce_sum.25
  (31 shorter events, 0.1 us)
Async XLA Ops:
  2.2 0.8 copy-start.14
  3.1 0.8 copy-start.15
  39.5 40.7 %copy-start.4 = (bf16[8,32,1024]{2,1,0:T(8,128)(2,1)}, bf16[8,32,1024]{2,1,0:T(8,128)(2,1)S(1)}, u32[]{:S(2)}) copy-start(bf16[8,32,1024]{2,1,0:T(8,128)(2,1)S(1)} %get-tuple-element.34.refs_0_) | copy-start | bytes 1572868
  39.5 3.9 %collective-permute-start.1 = (bf16[8,32,1024]{2,1,0:T(8,128)(2,1)S(1)}, bf16[8,32,1024]{2,1,0:T(8,128)(2,1)S(1)}, u32[]{:S(2)}, u32[]{:S(2)}) collective-permute-start(bf16[8,32,1024]{2,1,0:T(8,128)(2,1)S(1)} %get-tuple-element.35.refs_0_), channel_id=1, source_target_pairs={{0,1},{1,0},{2,3},{3,2},{4,5},{5,4},{6,7},{7,6},{8,9},{9,8},{10,11... | collective-permute-start | bytes 1572872 | tf_op jit(solution)/shard_map/ppermute | solution.py:23
  39.6 14.3 %collective-permute-start = (bf16[8,32,1024]{2,1,0:T(8,128)(2,1)S(1)}, bf16[8,32,1024]{2,1,0:T(8,128)(2,1)S(1)}, u32[]{:S(2)}, u32[]{:S(2)}) collective-permute-start(bf16[8,32,1024]{2,1,0:T(8,128)(2,1)S(1)} %get-tuple-element.35.refs_0_), channel_id=1, source_target_pairs={{0,2},{1,3},{2,0},{3,1},{4,6},{5,7},{6,4},{7,5},{8,10},{9,11},{10,... | collective-permute-start | bytes 1572872 | tf_op jit(solution)/shard_map/ppermute | solution.py:23
  43.5 6.7 %copy-start.2 = (bf16[8,32,1024]{2,1,0:T(8,128)(2,1)}, bf16[8,32,1024]{2,1,0:T(8,128)(2,1)S(1)}, u32[]{:S(2)}) copy-start(bf16[8,32,1024]{2,1,0:T(8,128)(2,1)S(1)} %collective-permute-done.1.refs_1_) | copy-start | bytes 1572868
  54.0 1.9 %collective-permute-start.2 = (bf16[8,32,1024]{2,1,0:T(8,128)(2,1)S(1)}, bf16[8,32,1024]{2,1,0:T(8,128)(2,1)S(1)}, u32[]{:S(2)}, u32[]{:S(2)}) collective-permute-start(bf16[8,32,1024]{2,1,0:T(8,128)(2,1)S(1)} %collective-permute-done.refs_0_.refs_2_), channel_id=1, source_target_pairs={{0,1},{1,0},{2,3},{3,2},{4,5},{5,4},{6,7},{7,6},{8,9},{9,8},{10,11... | collective-permute-start | bytes 1572872 | tf_op jit(solution)/shard_map/ppermute | solution.py:23
  54.0 22.6 %collective-permute-start.5 = (bf16[8,32,1024]{2,1,0:T(8,128)(2,1)S(1)}, bf16[8,32,1024]{2,1,0:T(8,128)(2,1)S(1)}, u32[]{:S(2)}, u32[]{:S(2)}) collective-permute-start(bf16[8,32,1024]{2,1,0:T(8,128)(2,1)S(1)} %get-tuple-element.34.refs_0_), channel_id=1, source_target_pairs={{0,2},{1,3},{2,0},{3,1},{4,6},{5,7},{6,4},{7,5},{8,10},{9,11},{10,... | collective-permute-start | bytes 1572872 | tf_op jit(solution)/shard_map/ppermute | solution.py:23
  55.9 20.1 %copy-start = (bf16[8,32,1024]{2,1,0:T(8,128)(2,1)}, bf16[8,32,1024]{2,1,0:T(8,128)(2,1)S(1)}, u32[]{:S(2)}) copy-start(bf16[8,32,1024]{2,1,0:T(8,128)(2,1)S(1)} %collective-permute-done.2.refs_1_.refs_3_) | copy-start | bytes 1572868
  76.0 24.7 %copy-start.16 = (bf16[256,3072]{1,0:T(8,128)(2,1)}, bf16[256,3072]{1,0:T(8,128)(2,1)S(1)}, u32[]{:S(2)}) copy-start(bf16[256,3072]{1,0:T(8,128)(2,1)S(1)} %get-tuple-element.30.act_ref) | copy-start | bytes 4718596
  76.0 24.8 %collective-permute-start.3 = (bf16[2,256,1024]{2,1,0:T(8,128)(2,1)S(1)}, bf16[2,256,1024]{2,1,0:T(8,128)(2,1)S(1)}, u32[]{:S(2)}, u32[]{:S(2)}) collective-permute-start(bf16[2,256,1024]{2,1,0:T(8,128)(2,1)S(1)} %get-tuple-element.25), channel_id=1, source_target_pairs={{0,1},{1,0},{2,3},{3,2},{4,5},{5,4},{6,7},{7,6},{8,9},{9,8},{10,11... | collective-permute-start | bytes 3145736 | tf_op jit(solution)/shard_map/ppermute | solution.py:23
  76.2 3.3 %collective-permute-start.4 = (bf16[8,32,1024]{2,1,0:T(8,128)(2,1)S(1)}, bf16[8,32,1024]{2,1,0:T(8,128)(2,1)S(1)}, u32[]{:S(2)}, u32[]{:S(2)}) collective-permute-start(bf16[8,32,1024]{2,1,0:T(8,128)(2,1)S(1)} %get-tuple-element.34.refs_0_), channel_id=1, source_target_pairs={{0,1},{1,0},{2,3},{3,2},{4,5},{5,4},{6,7},{7,6},{8,9},{9,8},{10,11... | collective-permute-start | bytes 1572872 | tf_op jit(solution)/shard_map/ppermute | solution.py:23
  76.6 24.1 %copy-start.8 = (bf16[8,32,1024]{2,1,0:T(8,128)(2,1)}, bf16[8,32,1024]{2,1,0:T(8,128)(2,1)S(1)}, u32[]{:S(2)}) copy-start(bf16[8,32,1024]{2,1,0:T(8,128)(2,1)S(1)} %collective-permute-done.5.refs_2_) | copy-start | bytes 1572868
  76.6 3.6 %collective-permute-start.6 = (bf16[8,32,1024]{2,1,0:T(8,128)(2,1)S(1)}, bf16[8,32,1024]{2,1,0:T(8,128)(2,1)S(1)}, u32[]{:S(2)}, u32[]{:S(2)}) collective-permute-start(bf16[8,32,1024]{2,1,0:T(8,128)(2,1)S(1)} %collective-permute-done.5.refs_2_), channel_id=1, source_target_pairs={{0,1},{1,0},{2,3},{3,2},{4,5},{5,4},{6,7},{7,6},{8,9},{9,8},{10,11... | collective-permute-start | bytes 1572872 | tf_op jit(solution)/shard_map/ppermute | solution.py:23
  79.5 21.2 %copy-start.10 = (bf16[8,32,1024]{2,1,0:T(8,128)(2,1)}, bf16[8,32,1024]{2,1,0:T(8,128)(2,1)S(1)}, u32[]{:S(2)}) copy-start(bf16[8,32,1024]{2,1,0:T(8,128)(2,1)S(1)} %collective-permute-done.4.refs_1_) | copy-start | bytes 1572868
  80.2 20.5 %copy-start.12 = (bf16[8,32,1024]{2,1,0:T(8,128)(2,1)}, bf16[8,32,1024]{2,1,0:T(8,128)(2,1)S(1)}, u32[]{:S(2)}) copy-start(bf16[8,32,1024]{2,1,0:T(8,128)(2,1)S(1)} %collective-permute-done.6.refs_3_) | copy-start | bytes 1572868
  100.7 14.8 %copy-start.6 = (bf16[256,3072]{1,0:T(8,128)(2,1)}, bf16[256,3072]{1,0:T(8,128)(2,1)S(1)}, u32[]{:S(2)}) copy-start(bf16[256,3072]{1,0:T(8,128)(2,1)S(1)} %get-tuple-element.32.grad_ref) | copy-start | bytes 4718596
  115.5 20.3 %collective-permute-start.8 = (bf16[2,256,1024]{2,1,0:T(8,128)(2,1)}, bf16[2,256,1024]{2,1,0:T(8,128)(2,1)S(1)}, u32[]{:S(2)}, u32[]{:S(2)}) collective-permute-start(bf16[2,256,1024]{2,1,0:T(8,128)(2,1)} %get-tuple-element.28.refs_3_), channel_id=1, source_target_pairs={{0,1},{1,0},{2,3},{3,2},{4,5},{5,4},{6,7},{7,6},{8,9},{9,8},{10,11... | collective-permute-start | bytes 3145736 | tf_op jit(solution)/shard_map/ppermute | solution.py:23
  115.7 14.2 %collective-permute-start.7 = (bf16[256,1024]{1,0:T(8,128)(2,1)S(1)}, bf16[256,1024]{1,0:T(8,128)(2,1)S(1)}, u32[]{:S(2)}, u32[]{:S(2)}) collective-permute-start(bf16[256,1024]{1,0:T(8,128)(2,1)S(1)} %mix_1.1.refs_0_), channel_id=1, source_target_pairs={{0,2},{1,3},{2,0},{3,1},{4,6},{5,7},{6,4},{7,5},{8,10},{9,11},{10,... | collective-permute-start | bytes 1572872 | tf_op jit(solution)/shard_map/ppermute | solution.py:23
  131.5 21.9 %all-to-all-start.1 = ((bf16[8,32,1024]{2,1,0:T(8,128)(2,1)}), bf16[8,32,1024]{2,1,0:T(8,128)(2,1)}, u32[]{:S(2)}, u32[]{:S(2)}) async-start(bf16[8,32,1024]{2,1,0:T(8,128)(2,1)} %bitcast.3), calls=%async_computation.1 | async-start | bytes 1048576 | tf_op jit(solution)/shard_map/all_to_all | solution.py:27
  135.8 2.3 %copy-start.5 = (bf16[8,32,1024]{2,1,0:T(8,128)(2,1)S(1)}, bf16[8,32,1024]{2,1,0:T(8,128)(2,1)}, u32[]{:S(2)}) copy-start(bf16[8,32,1024]{2,1,0:T(8,128)(2,1)} %copy-done.4) | copy-start | bytes 1572868
  135.8 2.3 %copy-start.9 = (bf16[8,32,1024]{2,1,0:T(8,128)(2,1)S(1)}, bf16[8,32,1024]{2,1,0:T(8,128)(2,1)}, u32[]{:S(2)}) copy-start(bf16[8,32,1024]{2,1,0:T(8,128)(2,1)} %copy-done.8) | copy-start | bytes 1572868
  135.8 2.3 %copy-start.11 = (bf16[8,32,1024]{2,1,0:T(8,128)(2,1)S(1)}, bf16[8,32,1024]{2,1,0:T(8,128)(2,1)}, u32[]{:S(2)}) copy-start(bf16[8,32,1024]{2,1,0:T(8,128)(2,1)} %copy-done.10) | copy-start | bytes 1572868
  135.8 2.3 %copy-start.13 = (bf16[8,32,1024]{2,1,0:T(8,128)(2,1)S(1)}, bf16[8,32,1024]{2,1,0:T(8,128)(2,1)}, u32[]{:S(2)}) copy-start(bf16[8,32,1024]{2,1,0:T(8,128)(2,1)} %copy-done.12) | copy-start | bytes 1572868
  136.5 15.3 %collective-permute-start.9 = (bf16[256,1024]{1,0:T(8,128)(2,1)S(1)}, bf16[256,1024]{1,0:T(8,128)(2,1)S(1)}, u32[]{:S(2)}, u32[]{:S(2)}) collective-permute-start(bf16[256,1024]{1,0:T(8,128)(2,1)S(1)} %back_1.1.refs_4_), channel_id=1, source_target_pairs={{0,2},{1,3},{2,0},{3,1},{4,6},{5,7},{6,4},{7,5},{8,10},{9,11},{10,... | collective-permute-start | bytes 1572872 | tf_op jit(solution)/shard_map/ppermute | solution.py:23
  138.1 1.4 copy-start.17
  153.4 7.6 %copy-start.1 = (bf16[8,32,1024]{2,1,0:T(8,128)(2,1)S(1)}, bf16[8,32,1024]{2,1,0:T(8,128)(2,1)}, u32[]{:S(2)}) copy-start(bf16[8,32,1024]{2,1,0:T(8,128)(2,1)} %copy-done) | copy-start | bytes 1572868
  153.4 7.6 %copy-start.3 = (bf16[8,32,1024]{2,1,0:T(8,128)(2,1)S(1)}, bf16[8,32,1024]{2,1,0:T(8,128)(2,1)}, u32[]{:S(2)}) copy-start(bf16[8,32,1024]{2,1,0:T(8,128)(2,1)} %copy-done.2) | copy-start | bytes 1572868
  153.4 22.8 %all-to-all-start.2 = ((bf16[8,32,1024]{2,1,0:T(8,128)(2,1)}), bf16[8,32,1024]{2,1,0:T(8,128)(2,1)S(1)}, u32[]{:S(2)}, u32[]{:S(2)}) async-start(bf16[8,32,1024]{2,1,0:T(8,128)(2,1)} %bitcast.4), calls=%async_computation.2 | async-start | bytes 1048576 | tf_op jit(solution)/shard_map/all_to_all | solution.py:27
  161.0 1.4 copy-start.7

commit v8 on v6

--- a/solution.py
+++ b/solution.py
@@ -34,6 +34,15 @@
         chunks.update({s | bit: swap(c, "tensor", bit) for s, c in list(chunks.items())})
         bit //= 2
     return [chunks[s] for s in range(len(chunks))]
+
+
+def far_chunks(value):
+    chunks = {0: value}
+    bit = lax.axis_size("tensor") // 2
+    while bit > 1:
+        chunks.update({s | bit: swap(c, "tensor", bit) for s, c in list(chunks.items())})
+        bit //= 2
+    return [chunks[s] for s in sorted(chunks)]
 
 
 def scatter_rows(value, rows):
@@ -106,12 +115,10 @@
         out_ref[group, :, width:] = packed
 
 
-def repeat_kernel(count, me_ref, *refs):
-    parts, out_ref = refs[:count], refs[-1]
-    width = parts[0].shape[1]
-    for i, part in enumerate(parts):
-        for group in range(out_ref.shape[0]):
-            out_ref[group, :, i * width : (i + 1) * width] = part[...]
+def repeat_kernel(me_ref, token_ref, *refs):
+    out_ref = refs[-1]
+    for group in range(out_ref.shape[0]):
+        out_ref[group] = token_ref[...]
 
 
 def plan_kernel(top, local, me_ref, packed_ref, to_token_ref, to_row_ref, gate_ref):
@@ -182,9 +189,9 @@
 
 
 def middle_kernel(n, steps, me_ref, to_token_ref, to_row_ref, slope_ref, act_ref, *refs):
-    ys, w_ref = refs[:2], refs[2]
-    sums, (grad_ref, spread_ref) = refs[3:5], refs[5:7]
-    held_ref, rows_ref, y_sems, out_rows_ref, buffer, sems = refs[7:]
+    ys, w_ref = refs[:n], refs[n]
+    sums, (grad_ref, spread_ref) = refs[n + 1 : n + 3], refs[n + 3 : n + 5]
+    held_ref, rows_ref, y_sems, out_rows_ref, buffer, sems = refs[n + 5 :]
     room, hid = grad_ref.shape
     width, depth = rows_ref.shape[2], buffer.shape[0]
     e = pl.program_id(0)
@@ -204,8 +211,7 @@
 
     @pl.when(e == 0)
     def _():
-        sources = [(ys[s % 2], s // 2 * width) for s in range(n)]
-        gather(to_row_ref, sources, held_ref, rows_ref, y_sems)
+        gather(to_row_ref, [(y, 0) for y in ys], held_ref, rows_ref, y_sems)
 
     for copy in copies(e):
         copy.wait()
@@ -293,7 +299,7 @@
 
 
 def d_out_kernel(n, steps, me_ref, act_ref, *refs):
-    ys, (out_ref, done_ref, buffer, sems) = refs[:2], refs[-4:]
+    ys, (out_ref, done_ref, buffer, sems) = refs[:n], refs[-4:]
     e = pl.program_id(0)
     _, n, hid, width = buffer.shape
     act = act_ref[...].T
@@ -302,8 +308,7 @@
 
     def values():
         for s in range(n):
-            start = s // 2 * width
-            yield dot(act, flat_rows(ys[s % 2][:, :, start : start + width]))
+            yield dot(act, flat_rows(ys[s][...]))
 
     write_step(e, steps, values, outs, buffer, sems)
 
@@ -401,29 +406,22 @@
     )
     left = exchange_rows(packed)
     xs = gather_chunks(left)
-    raw = {0: cotangent}
-    bit = n // 2
-    while bit > 1:
-        raw.update({k | bit: swap(c, "tensor", bit) for k, c in list(raw.items())})
-        bit //= 2
-    raw = [raw[k] for k in sorted(raw)]
-    wide = len(raw) * quarter
-    even_y = exchange_rows(
+    whole = exchange_rows(
         call(
-            functools.partial(repeat_kernel, len(raw)),
+            repeat_kernel,
             "repeat",
             (1,),
-            [once(rows, quarter)] * len(raw),
-            once(groups, rows, wide),
-            jax.ShapeDtypeStruct((groups, rows, wide), BF16),
-            (me, *raw),
+            [once(rows, quarter)],
+            once(groups, rows, quarter),
+            jax.ShapeDtypeStruct((groups, rows, quarter), BF16),
+            (me, cotangent),
             0,
-            24 if big else 6,
+            24 if big else 4,
             (),
-            (xs[1],),
+            (left,),
         )
     )
-    ys = (even_y, swap(even_y, "tensor", 1))
+    far = far_chunks(whole)
     to_token, to_row, gate = call(
         functools.partial(plan_kernel, top, local),
         "plan",
@@ -479,8 +477,13 @@
         flops,
         limit,
         gathered + ring(n, quarter, hid),
-        (even_y,),
-    )
+        (whole,),
+    )
+    near = swap(whole, "tensor", 1)
+    *far, act = lax.optimization_barrier((*far[1:], act))
+    ys = [whole, near]
+    for chunk in far:
+        ys += [chunk, swap(chunk, "tensor", 1)]
     cols = min(512, quarter)
     per = quarter // cols
     steps = n // 2 * per
@@ -492,7 +495,7 @@
         "middle",
         (local,),
         [once(total, slots), once(slots, total), row_block, row_block]
-        + [ANYWHERE] * 2
+        + [ANYWHERE] * n
         + [IN_HBM],
         [sum_spec, sum_spec, row_block, dense_block],
         [sum_shape, sum_shape, row_shape, dense],
@@ -578,7 +581,7 @@
         functools.partial(d_out_kernel, n, local),
         "d_w_out",
         (local,),
-        [dense_block] + [once(groups, rows, wide)] * 2,
+        [dense_block] + chunk_specs,
         [IN_HBM, once(8, 128)],
         [placed(pltpu.HBM, (local * hid, width)), jax.ShapeDtypeStruct((8, 128), F32)],
         (me, act_dense, *ys),
@@ -589,7 +592,7 @@
     )
     mix_sum = gather_sum("mix", mix_even, mix_got, mix_sent, (done,))
     mixed = scatter_rows(mix_sum, rows).astype(BF16)
-    back_sum = gather_sum("back", back_even, back_got, back_sent, (mix_sum,))
+    back_sum = gather_sum("back", back_even, back_got, back_sent, (done,))
     d_tokens = scatter_rows(back_sum, rows).astype(BF16)
     d_w_in = call(
         functools.partial(d_in_kernel, n, local // group),
@@ -606,7 +609,7 @@
             pltpu.VMEM((4, group, quarter, hid), BF16),
             pltpu.SemaphoreType.DMA((4, group)),
         ],
-        (back_sum,),
+        (back_sum, mix_sum),
     )
     return mixed, d_tokens, d_w_in, d_w_out.reshape(w_out.shape)
 

time: 176 us -> 163 us (0.926)
  waiting for transfers between devices: 41.5 us -> 27.5 us
  starting transfers between devices: 19.1 us -> 21.2 us
    all_to_all x3, waiting for transfers between devices: 24.3 us -> 0.01 us  [exchange_rows(): lax.all_to_all(blocks, 'expert', split_axis=0, concat_axis=0, tiled=True)]
    ppermute x9 -> x10, waiting for transfers between devices: 17.3 us -> 27.5 us  [swap(): return lax.ppermute(value, axis, [(i, i ^ bits) for i in range(size)])]
    all_to_all x3, starting transfers between devices: 12.7 us -> 14.9 us  [exchange_rows(): lax.all_to_all(blocks, 'expert', split_axis=0, concat_axis=0, tiled=True)]
    ppermute x9 -> x10, starting transfers between devices: 6.36 us -> 6.29 us  [swap(): return lax.ppermute(value, axis, [(i, i ^ bits) for i in range(size)])]
  transfers between devices with their start and end apart: 12 -> 13, of which waited for: 4 -> 4; matrix products, arithmetic and copies ran while one was open for 0% -> 0% of each run, Pallas kernels for 33% -> 35%
where the time goes in v8:
time: 163 us; the launch traced here: 162 us
  Pallas kernels  79.9 us (49%)
  waiting for transfers between devices  27.5 us (17%)
  blocking collectives  23.6 us (14%)
  starting transfers between devices  21.2 us (13%)
  local copies, waits for them, and re-layouts  7.82 us (5%)
    pallas_call x13, Pallas kernels, call(): pl.pallas_call(kernel, grid_spec=pltpu.PrefetchScalarGridSpec(num_scalar_...  79.9 us
    ppermute x10, waiting for transfers between devices, swap(): return lax.ppermute(value, axis, [(i, i ^ bits) for i in range(size)])  27.5 us
    all_to_all x1, blocking collectives, exchange_rows(): lax.all_to_all(blocks, 'expert', split_axis=0, concat_axis=0, tiled=True)  23.6 us
    all_to_all x3, starting transfers between devices, exchange_rows(): lax.all_to_all(blocks, 'expert', split_axis=0, concat_axis=0, tiled=True)  14.9 us
    unnamed x24, local copies, waits for them, and re-layouts  7.82 us
    ppermute x10, starting transfers between devices, swap(): return lax.ppermute(value, axis, [(i, i ^ bits) for i in range(size)])  6.29 us
  transfers between devices with their start and end apart: 13, of which 4 were waited for; matrix products, arithmetic and copies ran while one was open for 0% of the time, Pallas kernels for 35%

profile of v8, /device:TPU:0, one launch (start us, length us, event | category | flops | bytes accessed | tf_op | source)
XLA Modules:
  0.0 162.3 jit_solution(10480387967530462180)
XLA Ops:
  0.6 0.8 copy.10.routing_ref
  1.4 0.8 copy.11.gates_ref
  2.2 0.1 pad_add_fusion.me_ref
  2.2 0.8 copy-done.9
  3.1 0.7 pack.1
  3.8 23.6 %all_to_all.20.packed_ref.refs_0_ = bf16[8,32,1152]{2,1,0:T(8,128)(2,1)S(1)} all-to-all(bf16[8,32,1152]{2,1,0:T(8,128)(2,1)S(1)} %pack.1), channel_id=1, replica_groups=mesh['expert'=8,'tensor'=4] {'expert'}, dimensions={0} | all-to-all | bytes 1179648 | tf_op jit(solution)/shard_map/all_to_all | solution.py:27
  27.4 0.8 copy-done.10
  28.2 1.4 repeat.1
  29.6 3.5 %all-to-all-start.1 = ((bf16[8,32,1024]{2,1,0:T(8,128)(2,1)}), bf16[8,32,1024]{2,1,0:T(8,128)(2,1)S(1)}, u32[]{:S(2)}, u32[]{:S(2)}) async-start(bf16[8,32,1024]{2,1,0:T(8,128)(2,1)} %repeat.1), calls=%async_computation.1 | async-start | bytes 1048576 | tf_op jit(solution)/shard_map/all_to_all | solution.py:27
  33.1 1.6 collective-permute-start.1
  34.7 0.0 collective-permute-start
  34.7 12.5 %collective-permute-done.1.refs_2_ = bf16[8,32,1152]{2,1,0:T(8,128)(2,1)S(1)} collective-permute-done((bf16[8,32,1152]{2,1,0:T(8,128)(2,1)S(1)}, bf16[8,32,1152]{2,1,0:T(8,128)(2,1)S(1)}, u32[]{:S(2)}, u32[]{:S(2)}) %collective-permute-start.1) | collective-permute-done | bytes 589856 | tf_op jit(solution)/shard_map/ppermute | solution.py:23
  47.2 0.0 collective-permute-start.2
  47.2 0.0 all-to-all-done.1.refs_5_.refs_0_
  47.2 1.6 collective-permute-start.3
  48.7 2.3 %plan.1 = (bf16[256,512]{1,0:T(8,128)(2,1)S(1)}, bf16[512,256]{1,0:T(8,128)(2,1)S(1)}, f32[512,1]{1,0:T(8,128)S(1)}) custom-call(s32[2]{0:T(128)S(1)} %pad_add_fusion.me_ref, bf16[8,32,1152]{2,1,0:T(8,128)(2,1)S(1)} %all_to_all.20.packed_ref.refs_0_), custom_call_target="tpu_custom_call" | custom-call | bytes 1116168 | tf_op jit(solution)/shard_map/plan/pallas_call | solution.py:360
  51.0 0.2 collective-permute-start.4
  51.2 0.0 collective-permute-done.refs_1_
  51.3 10.6 %preact.1 = (bf16[512,384]{1,0:T(8,128)(2,1)S(1)}, bf16[256,3072]{1,0:T(8,128)(2,1)S(1)}, f32[512,384]{1,0:T(8,128)S(1)}) custom-call(s32[2]{0:T(128)S(1)} %pad_add_fusion.me_ref, bf16[512,256]{1,0:T(8,128)(2,1)S(1)} %get-tuple-element.19.to_row_ref, f32[512,1]{1,0:T(8,128)S(1)} %get-tuple-element.20.gate_ref, ...), custom_call_target="tpu_custom_call" | custom-call | flops 1610612736 | bytes 30541832 | tf_op jit(solution)/shard_map/preact/pallas_call | solution.py:360
  61.9 0.0 collective-permute-done.3.refs_2_
  61.9 0.4 collective-permute-start.5
  62.3 0.0 collective-permute-done.4.refs_1_
  62.3 1.5 collective-permute-done.5.refs_3_
  63.9 18.6 %middle.1 = (bf16[2,256,1024]{2,1,0:T(8,128)(2,1)S(1)}, bf16[2,256,1024]{2,1,0:T(8,128)(2,1)S(1)}, bf16[512,384]{1,0:T(8,128)(2,1)S(1)}, bf16[256,3072]{1,0:T(8,128)(2,1)S(1)}) custom-call(s32[2]{0:T(128)S(1)} %pad_add_fusion.me_ref, bf16[256,512]{1,0:T(8,128)(2,1)S(1)} %get-tuple-element.18.to_token_ref, bf16[512,256]{1,0:T(8,128)(2,1)S(1)} %get-tuple-element.19.to_row_ref, ...), custom_call_target="tpu_custom_call" | custom-call | flops 3221225472 | bytes 33030152 | tf_op jit(solution)/shard_map/middle/pallas_call | solution.py:360
  82.5 0.0 copy-start.7
  82.5 0.4 collective-permute-start.6
  83.0 7.8 %back_odd.1.refs_2_ = bf16[2,256,1024]{2,1,0:T(8,128)(2,1)S(1)} custom-call(s32[2]{0:T(128)S(1)} %pad_add_fusion.me_ref, bf16[256,512]{1,0:T(8,128)(2,1)S(1)} %get-tuple-element.18.to_token_ref, bf16[512,384]{1,0:T(8,128)(2,1)S(1)} %get-tuple-element.27.grad_ref, bf16[8,4096,384]{2,1,0:T(8,128)(2,1)} %w_ref.3), custom_call_target="tpu_custom_call" | custom-call | flops 805306368 | bytes 26869768 | tf_op jit(solution)/shard_map/back_odd/pallas_call | solution.py:360
  90.8 0.2 collective-permute-start.8
  91.0 0.7 mix_1.1.refs_0_
  91.6 7.8 %back_even.1.refs_0_ = bf16[2,256,1024]{2,1,0:T(8,128)(2,1)S(1)} custom-call(s32[2]{0:T(128)S(1)} %pad_add_fusion.me_ref, bf16[256,512]{1,0:T(8,128)(2,1)S(1)} %get-tuple-element.18.to_token_ref, bf16[512,384]{1,0:T(8,128)(2,1)S(1)} %get-tuple-element.27.grad_ref, bf16[8,4096,384]{2,1,0:T(8,128)(2,1)} %w_ref.3, bf16[256,1024]{1,0:T(8,128)(2,1)S(1)} %mix_1.1.refs_0_), custom_call_target="tpu_custom_call" | custom-call | flops 805306368 | bytes 26869768 | tf_op jit(solution)/shard_map/back_even/pallas_call | solution.py:360
  99.4 0.7 back_1.1.refs_4_
  100.1 1.1 collective-permute-start.9
  101.2 12.3 %d_w_out.1 = (bf16[3072,4096]{1,0:T(8,128)(2,1)}, f32[8,128]{1,0:T(8,128)S(1)}) custom-call(s32[2]{0:T(128)S(1)} %pad_add_fusion.me_ref, bf16[256,3072]{1,0:T(8,128)(2,1)S(1)} %get-tuple-element.28.act_ref, bf16[8,32,1024]{2,1,0:T(8,128)(2,1)S(1)} %all-to-all-done.1.refs_5_.refs_0_, bf16[8,32,1024]{2,1,0:T(8,128)(2,1)S(1)} %collective-permute-done.4.refs_1_, ...), custom_call_target="tpu_custom_call" | custom-call | flops 6442450944 | bytes 28839944 | tf_op jit(solution)/shard_map/d_w_out/pallas_call | solution.py:360
  113.5 0.9 collective-permute-done.9.refs_2_
  114.4 1.5 back_sum.1.refs_4_
  115.9 5.7 %all-to-all-start.3 = ((bf16[8,32,1024]{2,1,0:T(8,128)(2,1)}), bf16[8,32,1024]{2,1,0:T(8,128)(2,1)S(1)}, u32[]{:S(2)}, u32[]{:S(2)}) async-start(bf16[8,32,1024]{2,1,0:T(8,128)(2,1)} %bitcast.4), calls=%async_computation.3 | async-start | bytes 1048576 | tf_op jit(solution)/shard_map/all_to_all | solution.py:27
  121.6 0.7 collective-permute-start.7
  122.3 12.6 %collective-permute-done.7.refs_2_ = bf16[256,1024]{1,0:T(8,128)(2,1)S(1)} collective-permute-done((bf16[256,1024]{1,0:T(8,128)(2,1)}, bf16[256,1024]{1,0:T(8,128)(2,1)S(1)}, u32[]{:S(2)}, u32[]{:S(2)}) %collective-permute-start.7) | collective-permute-done | bytes 524320 | tf_op jit(solution)/shard_map/ppermute | solution.py:23
  134.9 1.5 mix_sum.1.refs_5_
  136.5 5.7 %all-to-all-start.2 = ((bf16[8,32,1024]{2,1,0:T(8,128)(2,1)}), bf16[8,32,1024]{2,1,0:T(8,128)(2,1)S(1)}, u32[]{:S(2)}, u32[]{:S(2)}) async-start(bf16[8,32,1024]{2,1,0:T(8,128)(2,1)} %bitcast.3), calls=%async_computation.2 | async-start | bytes 1048576 | tf_op jit(solution)/shard_map/all_to_all | solution.py:27
  142.2 1.1 copy-done.1
  143.2 1.1 copy-done.3
  144.3 1.1 copy-done.5
  145.4 1.4 copy-done.8
  146.8 14.1 %d_w_in.1 = bf16[8,4096,384]{2,1,0:T(8,128)(2,1)} custom-call(s32[2]{0:T(128)S(1)} %pad_add_fusion.me_ref, bf16[256,3072]{1,0:T(8,128)(2,1)S(1)} %copy-done.8, bf16[8,32,1152]{2,1,0:T(8,128)(2,1)S(1)} %all_to_all.20.packed_ref.refs_0_, bf16[8,32,1152]{2,1,0:T(8,128)(2,1)S(1)} %copy-done.3, bf16[8,32,1152]{2,1,0:T(8,128)(2,1)S(1)} %copy-done.1, ...), custom_call_target="tpu_custom_call" | custom-call | flops 6442450944 | bytes 29097992 | tf_op jit(solution)/shard_map/d_w_in/pallas_call | solution.py:360
  160.9 0.7 reduce_sum.25
  161.6 0.0 all-to-all-done.2
  161.6 0.7 reduce_sum.24
  (19 shorter events, 0.0 us)
Async XLA Ops:
  2.2 0.8 copy-start.9
  27.4 0.8 copy-start.10
  29.6 17.6 %all-to-all-start.1 = ((bf16[8,32,1024]{2,1,0:T(8,128)(2,1)}), bf16[8,32,1024]{2,1,0:T(8,128)(2,1)S(1)}, u32[]{:S(2)}, u32[]{:S(2)}) async-start(bf16[8,32,1024]{2,1,0:T(8,128)(2,1)} %repeat.1), calls=%async_computation.1 | async-start | bytes 1048576 | tf_op jit(solution)/shard_map/all_to_all | solution.py:27
  33.1 14.1 %collective-permute-start.1 = (bf16[8,32,1152]{2,1,0:T(8,128)(2,1)S(1)}, bf16[8,32,1152]{2,1,0:T(8,128)(2,1)S(1)}, u32[]{:S(2)}, u32[]{:S(2)}) collective-permute-start(bf16[8,32,1152]{2,1,0:T(8,128)(2,1)S(1)} %all_to_all.20.packed_ref.refs_0_), channel_id=1, source_target_pairs={{0,2},{1,3},{2,0},{3,1},{4,6},{5,7},{6,4},{7,5},{8,10},{9,11},{10,... | collective-permute-start | bytes 1769480 | tf_op jit(solution)/shard_map/ppermute | solution.py:23
  34.7 16.6 %collective-permute-start = (bf16[8,32,1152]{2,1,0:T(8,128)(2,1)S(1)}, bf16[8,32,1152]{2,1,0:T(8,128)(2,1)S(1)}, u32[]{:S(2)}, u32[]{:S(2)}) collective-permute-start(bf16[8,32,1152]{2,1,0:T(8,128)(2,1)S(1)} %all_to_all.20.packed_ref.refs_0_), channel_id=1, source_target_pairs={{0,1},{1,0},{2,3},{3,2},{4,5},{5,4},{6,7},{7,6},{8,9},{9,8},{10,11... | collective-permute-start | bytes 1769480 | tf_op jit(solution)/shard_map/ppermute | solution.py:23
  47.2 16.7 %copy-start = (bf16[8,32,1152]{2,1,0:T(8,128)(2,1)}, bf16[8,32,1152]{2,1,0:T(8,128)(2,1)S(1)}, u32[]{:S(2)}) copy-start(bf16[8,32,1152]{2,1,0:T(8,128)(2,1)S(1)} %collective-permute-done.1.refs_2_) | copy-start | bytes 1769476
  47.2 4.1 %collective-permute-start.2 = (bf16[8,32,1152]{2,1,0:T(8,128)(2,1)S(1)}, bf16[8,32,1152]{2,1,0:T(8,128)(2,1)S(1)}, u32[]{:S(2)}, u32[]{:S(2)}) collective-permute-start(bf16[8,32,1152]{2,1,0:T(8,128)(2,1)S(1)} %collective-permute-done.1.refs_2_), channel_id=1, source_target_pairs={{0,1},{1,0},{2,3},{3,2},{4,5},{5,4},{6,7},{7,6},{8,9},{9,8},{10,11... | collective-permute-start | bytes 1769480 | tf_op jit(solution)/shard_map/ppermute | solution.py:23
  47.2 14.7 %collective-permute-start.3 = (bf16[8,32,1024]{2,1,0:T(8,128)(2,1)S(1)}, bf16[8,32,1024]{2,1,0:T(8,128)(2,1)S(1)}, u32[]{:S(2)}, u32[]{:S(2)}) collective-permute-start(bf16[8,32,1024]{2,1,0:T(8,128)(2,1)S(1)} %all-to-all-done.1.refs_5_.refs_0_), channel_id=1, source_target_pairs={{0,2},{1,3},{2,0},{3,1},{4,6},{5,7},{6,4},{7,5},{8,10},{9,11},{10,... | collective-permute-start | bytes 1572872 | tf_op jit(solution)/shard_map/ppermute | solution.py:23
  51.0 11.3 %collective-permute-start.4 = (bf16[8,32,1024]{2,1,0:T(8,128)(2,1)S(1)}, bf16[8,32,1024]{2,1,0:T(8,128)(2,1)S(1)}, u32[]{:S(2)}, u32[]{:S(2)}) collective-permute-start(bf16[8,32,1024]{2,1,0:T(8,128)(2,1)S(1)} %all-to-all-done.1.refs_5_.refs_0_), channel_id=1, source_target_pairs={{0,1},{1,0},{2,3},{3,2},{4,5},{5,4},{6,7},{7,6},{8,9},{9,8},{10,11... | collective-permute-start | bytes 1572872 | tf_op jit(solution)/shard_map/ppermute | solution.py:23
  51.2 12.6 %copy-start.2 = (bf16[8,32,1152]{2,1,0:T(8,128)(2,1)}, bf16[8,32,1152]{2,1,0:T(8,128)(2,1)S(1)}, u32[]{:S(2)}) copy-start(bf16[8,32,1152]{2,1,0:T(8,128)(2,1)S(1)} %collective-permute-done.refs_1_) | copy-start | bytes 1769476
  51.3 31.2 %copy-start.4 = (bf16[8,32,1152]{2,1,0:T(8,128)(2,1)}, bf16[8,32,1152]{2,1,0:T(8,128)(2,1)S(1)}, u32[]{:S(2)}) copy-start(bf16[8,32,1152]{2,1,0:T(8,128)(2,1)S(1)} %collective-permute-done.2.refs_3_) | copy-start | bytes 1769476
  61.9 2.0 %collective-permute-start.5 = (bf16[8,32,1024]{2,1,0:T(8,128)(2,1)S(1)}, bf16[8,32,1024]{2,1,0:T(8,128)(2,1)S(1)}, u32[]{:S(2)}, u32[]{:S(2)}) collective-permute-start(bf16[8,32,1024]{2,1,0:T(8,128)(2,1)S(1)} %collective-permute-done.3.refs_2_), channel_id=1, source_target_pairs={{0,1},{1,0},{2,3},{3,2},{4,5},{5,4},{6,7},{7,6},{8,9},{9,8},{10,11... | collective-permute-start | bytes 1572872 | tf_op jit(solution)/shard_map/ppermute | solution.py:23
  82.5 16.9 %copy-start.7 = (bf16[256,3072]{1,0:T(8,128)(2,1)}, bf16[256,3072]{1,0:T(8,128)(2,1)S(1)}, u32[]{:S(2)}) copy-start(bf16[256,3072]{1,0:T(8,128)(2,1)S(1)} %get-tuple-element.30.grad_ref) | copy-start | bytes 4718596
  82.5 8.4 %collective-permute-start.6 = (bf16[2,256,1024]{2,1,0:T(8,128)(2,1)S(1)}, bf16[2,256,1024]{2,1,0:T(8,128)(2,1)S(1)}, u32[]{:S(2)}, u32[]{:S(2)}) collective-permute-start(bf16[2,256,1024]{2,1,0:T(8,128)(2,1)S(1)} %get-tuple-element.26), channel_id=1, source_target_pairs={{0,1},{1,0},{2,3},{3,2},{4,5},{5,4},{6,7},{7,6},{8,9},{9,8},{10,11... | collective-permute-start | bytes 3145736 | tf_op jit(solution)/shard_map/ppermute | solution.py:23
  90.8 8.7 %collective-permute-start.8 = (bf16[2,256,1024]{2,1,0:T(8,128)(2,1)S(1)}, bf16[2,256,1024]{2,1,0:T(8,128)(2,1)S(1)}, u32[]{:S(2)}, u32[]{:S(2)}) collective-permute-start(bf16[2,256,1024]{2,1,0:T(8,128)(2,1)S(1)} %back_odd.1.refs_2_), channel_id=1, source_target_pairs={{0,1},{1,0},{2,3},{3,2},{4,5},{5,4},{6,7},{7,6},{8,9},{9,8},{10,11... | collective-permute-start | bytes 3145736 | tf_op jit(solution)/shard_map/ppermute | solution.py:23
  91.6 7.8 %copy-start.6 = (bf16[256,1024]{1,0:T(8,128)(2,1)}, bf16[256,1024]{1,0:T(8,128)(2,1)S(1)}, u32[]{:S(2)}) copy-start(bf16[256,1024]{1,0:T(8,128)(2,1)S(1)} %mix_1.1.refs_0_) | copy-start | bytes 1572868
  100.1 14.3 %collective-permute-start.9 = (bf16[256,1024]{1,0:T(8,128)(2,1)S(1)}, bf16[256,1024]{1,0:T(8,128)(2,1)S(1)}, u32[]{:S(2)}, u32[]{:S(2)}) collective-permute-start(bf16[256,1024]{1,0:T(8,128)(2,1)S(1)} %back_1.1.refs_4_), channel_id=1, source_target_pairs={{0,2},{1,3},{2,0},{3,1},{4,6},{5,7},{6,4},{7,5},{8,10},{9,11},{10,... | collective-permute-start | bytes 1572872 | tf_op jit(solution)/shard_map/ppermute | solution.py:23
  115.9 20.6 %all-to-all-start.3 = ((bf16[8,32,1024]{2,1,0:T(8,128)(2,1)}), bf16[8,32,1024]{2,1,0:T(8,128)(2,1)S(1)}, u32[]{:S(2)}, u32[]{:S(2)}) async-start(bf16[8,32,1024]{2,1,0:T(8,128)(2,1)} %bitcast.4), calls=%async_computation.3 | async-start | bytes 1048576 | tf_op jit(solution)/shard_map/all_to_all | solution.py:27
  121.6 13.3 %collective-permute-start.7 = (bf16[256,1024]{1,0:T(8,128)(2,1)}, bf16[256,1024]{1,0:T(8,128)(2,1)S(1)}, u32[]{:S(2)}, u32[]{:S(2)}) collective-permute-start(bf16[256,1024]{1,0:T(8,128)(2,1)} %copy-done.6), channel_id=1, source_target_pairs={{0,2},{1,3},{2,0},{3,1},{4,6},{5,7},{6,4},{7,5},{8,10},{9,11},{10,... | collective-permute-start | bytes 1572872 | tf_op jit(solution)/shard_map/ppermute | solution.py:23
  136.5 25.2 %all-to-all-start.2 = ((bf16[8,32,1024]{2,1,0:T(8,128)(2,1)}), bf16[8,32,1024]{2,1,0:T(8,128)(2,1)S(1)}, u32[]{:S(2)}, u32[]{:S(2)}) async-start(bf16[8,32,1024]{2,1,0:T(8,128)(2,1)} %bitcast.3), calls=%async_computation.2 | async-start | bytes 1048576 | tf_op jit(solution)/shard_map/all_to_all | solution.py:27
  142.2 1.1 copy-start.1
  143.2 1.1 copy-start.3
  144.3 1.1 copy-start.5
  145.4 1.4 copy-start.8

commit v9 on v8

--- a/solution.py
+++ b/solution.py
@@ -498,7 +498,7 @@
         + [ANYWHERE] * n
         + [IN_HBM],
         [sum_spec, sum_spec, row_block, dense_block],
-        [sum_shape, sum_shape, row_shape, dense],
+        [sum_shape, sum_shape, row_shape, placed(pltpu.HBM, dense.shape)],
         (me, to_token, to_row, slope, act, *ys, flat_out),
         2 * flops,
         56 if big else 30,
@@ -574,6 +574,8 @@
     back_odd = back("back_odd", 1)
     mix_got, mix_sent = pass_on("mix", mix_even, mix_odd, (back_odd,))
     back_even = back("back_even", 0, tuple(mix_sent.values()))
+    mix_sum = gather_sum("mix", mix_even, mix_got, mix_sent)
+    mixed = scatter_rows(mix_sum, rows).astype(BF16)
     back_got, back_sent = pass_on("back", back_even, back_odd)
 
     sems = pltpu.SemaphoreType.DMA((2, n))
@@ -588,10 +590,8 @@
         2 * total * local * hid * width,
         limit,
         [pltpu.VMEM((2, n, hid, quarter), BF16), sems],
-        tuple(back_sent.values()),
-    )
-    mix_sum = gather_sum("mix", mix_even, mix_got, mix_sent, (done,))
-    mixed = scatter_rows(mix_sum, rows).astype(BF16)
+        (*back_sent.values(), mix_sum),
+    )
     back_sum = gather_sum("back", back_even, back_got, back_sent, (done,))
     d_tokens = scatter_rows(back_sum, rows).astype(BF16)
     d_w_in = call(
@@ -601,7 +601,7 @@
         [pl.BlockSpec((total, group * hid), lambda p, s, me: (0, p))] + chunk_specs,
         IN_HBM,
         placed(pltpu.HBM, w_in.shape),
-        (me, grad_dense, *xs),
+        (me, grad_dense, *[pltpu.with_memory_space_constraint(x, pltpu.HBM) for x in xs]),
         2 * total * local * hid * width,
         limit,
         [
@@ -609,7 +609,7 @@
             pltpu.VMEM((4, group, quarter, hid), BF16),
             pltpu.SemaphoreType.DMA((4, group)),
         ],
-        (back_sum, mix_sum),
+        (back_sum,),
     )
     return mixed, d_tokens, d_w_in, d_w_out.reshape(w_out.shape)
 

time: 163 us -> 164 us (level)
  local copies, waits for them, and re-layouts: 7.82 us -> 6.17 us
    unnamed x24 -> x40, local copies, waits for them, and re-layouts: 7.82 us -> 6.17 us
  transfers between devices with their start and end apart: 13 -> 13, of which waited for: 4 -> 4; matrix products, arithmetic and copies ran while one was open for 0% -> 1% of each run, Pallas kernels for 35% -> 37%
where the time goes in v9:
time: 164 us; the launch traced here: 163 us
  Pallas kernels  81.2 us (50%)
  waiting for transfers between devices  28.1 us (17%)
  blocking collectives  23.6 us (14%)
  starting transfers between devices  20.4 us (12%)
  local copies, waits for them, and re-layouts  6.17 us (4%)
  other arithmetic  2.55 us (2%)
    pallas_call x13, Pallas kernels, call(): pl.pallas_call(kernel, grid_spec=pltpu.PrefetchScalarGridSpec(num_scalar_...  81.2 us
    ppermute x10, waiting for transfers between devices, swap(): return lax.ppermute(value, axis, [(i, i ^ bits) for i in range(size)])  28.1 us
    all_to_all x1, blocking collectives, exchange_rows(): lax.all_to_all(blocks, 'expert', split_axis=0, concat_axis=0, tiled=True)  23.6 us
    all_to_all x3, starting transfers between devices, exchange_rows(): lax.all_to_all(blocks, 'expert', split_axis=0, concat_axis=0, tiled=True)  14.9 us
    unnamed x40, local copies, waits for them, and re-layouts  6.17 us
    ppermute x10, starting transfers between devices, swap(): return lax.ppermute(value, axis, [(i, i ^ bits) for i in range(size)])  5.48 us
  transfers between devices with their start and end apart: 13, of which 4 were waited for; matrix products, arithmetic and copies ran while one was open for 1% of the time, Pallas kernels for 37%

profile of v9, /device:TPU:0, one launch (start us, length us, event | category | flops | bytes accessed | tf_op | source)
XLA Modules:
  0.0 163.0 jit_solution(16874692437285500423)
XLA Ops:
  0.6 0.8 copy.10.routing_ref
  1.4 0.8 copy.11.gates_ref
  2.2 0.1 pad_add_fusion.me_ref
  2.2 0.8 copy-done.15
  3.1 0.7 pack.1
  3.8 23.6 %all_to_all.20.packed_ref.refs_0_ = bf16[8,32,1152]{2,1,0:T(8,128)(2,1)S(1)} all-to-all(bf16[8,32,1152]{2,1,0:T(8,128)(2,1)S(1)} %pack.1), channel_id=1, replica_groups=mesh['expert'=8,'tensor'=4] {'expert'}, dimensions={0} | all-to-all | bytes 1179648 | tf_op jit(solution)/shard_map/all_to_all | solution.py:27
  27.4 0.8 copy-done.16
  28.2 1.4 repeat.1
  29.6 3.5 %all-to-all-start.1 = ((bf16[8,32,1024]{2,1,0:T(8,128)(2,1)}), bf16[8,32,1024]{2,1,0:T(8,128)(2,1)S(1)}, u32[]{:S(2)}, u32[]{:S(2)}) async-start(bf16[8,32,1024]{2,1,0:T(8,128)(2,1)} %repeat.1), calls=%async_computation.1 | async-start | bytes 1048576 | tf_op jit(solution)/shard_map/all_to_all | solution.py:27
  33.1 1.6 collective-permute-start.1
  34.7 12.5 %collective-permute-done.1.refs_2_ = bf16[8,32,1152]{2,1,0:T(8,128)(2,1)S(1)} collective-permute-done((bf16[8,32,1152]{2,1,0:T(8,128)(2,1)S(1)}, bf16[8,32,1152]{2,1,0:T(8,128)(2,1)S(1)}, u32[]{:S(2)}, u32[]{:S(2)}) %collective-permute-start.1) | collective-permute-done | bytes 589856 | tf_op jit(solution)/shard_map/ppermute | solution.py:23
  47.2 0.0 collective-permute-start.2
  47.2 1.6 collective-permute-start.3
  48.8 2.3 %plan.1 = (bf16[256,512]{1,0:T(8,128)(2,1)S(1)}, bf16[512,256]{1,0:T(8,128)(2,1)S(1)}, f32[512,1]{1,0:T(8,128)S(1)}) custom-call(s32[2]{0:T(128)S(1)} %pad_add_fusion.me_ref, bf16[8,32,1152]{2,1,0:T(8,128)(2,1)S(1)} %all_to_all.20.packed_ref.refs_0_), custom_call_target="tpu_custom_call" | custom-call | bytes 1116168 | tf_op jit(solution)/shard_map/plan/pallas_call | solution.py:360
  51.0 0.2 collective-permute-start.4
  51.3 0.0 collective-permute-done.refs_1_
  51.3 0.0 collective-permute-done.2.refs_3_
  51.3 10.6 %preact.1 = (bf16[512,384]{1,0:T(8,128)(2,1)S(1)}, bf16[256,3072]{1,0:T(8,128)(2,1)S(1)}, f32[512,384]{1,0:T(8,128)S(1)}) custom-call(s32[2]{0:T(128)S(1)} %pad_add_fusion.me_ref, bf16[512,256]{1,0:T(8,128)(2,1)S(1)} %get-tuple-element.19.to_row_ref, f32[512,1]{1,0:T(8,128)S(1)} %get-tuple-element.20.gate_ref, ...), custom_call_target="tpu_custom_call" | custom-call | flops 1610612736 | bytes 30541832 | tf_op jit(solution)/shard_map/preact/pallas_call | solution.py:360
  61.9 0.0 copy-start.17
  61.9 1.1 copy-done.17
  63.1 0.0 collective-permute-done.3.refs_2_
  63.1 0.3 collective-permute-start.5
  63.4 1.6 collective-permute-done.5.refs_3_
  65.0 19.1 %middle.1 = (bf16[2,256,1024]{2,1,0:T(8,128)(2,1)S(1)}, bf16[2,256,1024]{2,1,0:T(8,128)(2,1)S(1)}, bf16[512,384]{1,0:T(8,128)(2,1)S(1)}, bf16[256,3072]{1,0:T(8,128)(2,1)}) custom-call(s32[2]{0:T(128)S(1)} %pad_add_fusion.me_ref, bf16[256,512]{1,0:T(8,128)(2,1)S(1)} %get-tuple-element.18.to_token_ref, bf16[512,256]{1,0:T(8,128)(2,1)S(1)} %get-tuple-element.19.to_row_ref, ...), custom_call_target="tpu_custom_call" | custom-call | flops 3221225472 | bytes 33030152 | tf_op jit(solution)/shard_map/middle/pallas_call | solution.py:360
  84.2 0.4 collective-permute-start.6
  84.6 7.8 %back_odd.1.refs_2_ = bf16[2,256,1024]{2,1,0:T(8,128)(2,1)S(1)} custom-call(s32[2]{0:T(128)S(1)} %pad_add_fusion.me_ref, bf16[256,512]{1,0:T(8,128)(2,1)S(1)} %get-tuple-element.18.to_token_ref, bf16[512,384]{1,0:T(8,128)(2,1)S(1)} %get-tuple-element.27.grad_ref, bf16[8,4096,384]{2,1,0:T(8,128)(2,1)} %w_ref.3), custom_call_target="tpu_custom_call" | custom-call | flops 805306368 | bytes 26869768 | tf_op jit(solution)/shard_map/back_odd/pallas_call | solution.py:360
  92.4 0.3 collective-permute-start.8
  92.6 0.0 collective-permute-done.6.refs_1_
  92.6 0.7 mix_1.1.refs_0_
  93.3 0.5 collective-permute-start.7
  93.9 13.7 %collective-permute-done.7.refs_2_ = bf16[256,1024]{1,0:T(8,128)(2,1)S(1)} collective-permute-done((bf16[256,1024]{1,0:T(8,128)(2,1)S(1)}, bf16[256,1024]{1,0:T(8,128)(2,1)S(1)}, u32[]{:S(2)}, u32[]{:S(2)}) %collective-permute-start.7) | collective-permute-done | bytes 524320 | tf_op jit(solution)/shard_map/ppermute | solution.py:23
  107.5 0.7 mix_sum.1.refs_5_
  108.3 0.8 copy-done.4
  109.1 5.7 %all-to-all-start.2 = ((bf16[8,32,1024]{2,1,0:T(8,128)(2,1)}), bf16[8,32,1024]{2,1,0:T(8,128)(2,1)}, u32[]{:S(2)}, u32[]{:S(2)}) async-start(bf16[8,32,1024]{2,1,0:T(8,128)(2,1)} %bitcast.6), calls=%async_computation.2 | async-start | bytes 1048576 | tf_op jit(solution)/shard_map/all_to_all | solution.py:27
  114.8 1.0 copy-done.8
  115.8 0.0 copy-start.18
  115.8 8.1 %back_even.1.refs_0_ = bf16[2,256,1024]{2,1,0:T(8,128)(2,1)S(1)} custom-call(s32[2]{0:T(128)S(1)} %pad_add_fusion.me_ref, bf16[256,512]{1,0:T(8,128)(2,1)S(1)} %get-tuple-element.18.to_token_ref, bf16[512,384]{1,0:T(8,128)(2,1)S(1)} %copy-done.8, bf16[8,4096,384]{2,1,0:T(8,128)(2,1)} %w_ref.3, bf16[256,1024]{1,0:T(8,128)(2,1)S(1)} %mix_1.1.refs_0_), custom_call_target="tpu_custom_call" | custom-call | flops 805306368 | bytes 26869768 | tf_op jit(solution)/shard_map/back_even/pallas_call | solution.py:360
  124.0 0.0 copy-start.6
  124.0 0.7 back_1.1.refs_4_
  124.7 0.5 collective-permute-start.9
  125.2 12.3 %d_w_out.1 = (bf16[3072,4096]{1,0:T(8,128)(2,1)}, f32[8,128]{1,0:T(8,128)S(1)}) custom-call(s32[2]{0:T(128)S(1)} %pad_add_fusion.me_ref, bf16[256,3072]{1,0:T(8,128)(2,1)S(1)} %copy-done.18, bf16[8,32,1024]{2,1,0:T(8,128)(2,1)S(1)} %all-to-all-done.1.refs_5_.refs_0_, bf16[8,32,1024]{2,1,0:T(8,128)(2,1)S(1)} %copy-done.12, ...), custom_call_target="tpu_custom_call" | custom-call | flops 6442450944 | bytes 28839944 | tf_op jit(solution)/shard_map/d_w_out/pallas_call | solution.py:360
  137.5 0.3 collective-permute-done.9.refs_2_
  137.8 1.5 back_sum.1.refs_4_
  139.4 0.0 all-to-all-done.2
  139.4 5.7 %all-to-all-start.3 = ((bf16[8,32,1024]{2,1,0:T(8,128)(2,1)}), bf16[8,32,1024]{2,1,0:T(8,128)(2,1)S(1)}, u32[]{:S(2)}, u32[]{:S(2)}) async-start(bf16[8,32,1024]{2,1,0:T(8,128)(2,1)} %bitcast.4), calls=%async_computation.3 | async-start | bytes 1048576 | tf_op jit(solution)/shard_map/all_to_all | solution.py:27
  145.1 15.4 %d_w_in.1 = bf16[8,4096,384]{2,1,0:T(8,128)(2,1)} custom-call(s32[2]{0:T(128)S(1)} %pad_add_fusion.me_ref, bf16[256,3072]{1,0:T(8,128)(2,1)S(1)} %copy-done.6, bf16[8,32,1152]{2,1,0:T(8,128)(2,1)} %copy-done, bf16[8,32,1152]{2,1,0:T(8,128)(2,1)} %copy-done.2, bf16[8,32,1152]{2,1,0:T(8,128)(2,1)} %copy-done.1, bf16[8,32,1152]{2,1,0:T(8,128)(2,1)} %copy-done.3, ...), custom_call_target="tpu_custom_call" | custom-call | flops 6442450944 | bytes 29097992 | tf_op jit(solution)/shard_map/d_w_in/pallas_call | solution.py:360
  160.5 1.8 %reduce_sum.24 = bf16[32,1024]{1,0:T(8,128)(2,1)} reduce(bf16[8,32,1024]{2,1,0:T(8,128)(2,1)} %all-to-all-done.2, bf16[]{:T(256)} %constant.14.clone.1), dimensions={0}, to_apply=%region_0.0 | reduce | flops 229376 | bytes 589826 | tf_op jit(solution)/shard_map/reduce_sum | solution.py:49
  162.2 0.7 reduce_sum.25
  (35 shorter events, 0.1 us)
Async XLA Ops:
  2.2 0.8 copy-start.15
  27.4 0.8 copy-start.16
  28.2 55.9 %copy-start = (bf16[8,32,1152]{2,1,0:T(8,128)(2,1)}, bf16[8,32,1152]{2,1,0:T(8,128)(2,1)S(1)}, u32[]{:S(2)}) copy-start(bf16[8,32,1152]{2,1,0:T(8,128)(2,1)S(1)} %all_to_all.20.packed_ref.refs_0_) | copy-start | bytes 1769476
  29.6 17.6 %all-to-all-start.1 = ((bf16[8,32,1024]{2,1,0:T(8,128)(2,1)}), bf16[8,32,1024]{2,1,0:T(8,128)(2,1)S(1)}, u32[]{:S(2)}, u32[]{:S(2)}) async-start(bf16[8,32,1024]{2,1,0:T(8,128)(2,1)} %repeat.1), calls=%async_computation.1 | async-start | bytes 1048576 | tf_op jit(solution)/shard_map/all_to_all | solution.py:27
  33.1 14.1 %collective-permute-start.1 = (bf16[8,32,1152]{2,1,0:T(8,128)(2,1)S(1)}, bf16[8,32,1152]{2,1,0:T(8,128)(2,1)S(1)}, u32[]{:S(2)}, u32[]{:S(2)}) collective-permute-start(bf16[8,32,1152]{2,1,0:T(8,128)(2,1)S(1)} %all_to_all.20.packed_ref.refs_0_), channel_id=1, source_target_pairs={{0,2},{1,3},{2,0},{3,1},{4,6},{5,7},{6,4},{7,5},{8,10},{9,11},{10,... | collective-permute-start | bytes 1769480 | tf_op jit(solution)/shard_map/ppermute | solution.py:23
  34.7 16.6 %collective-permute-start = (bf16[8,32,1152]{2,1,0:T(8,128)(2,1)S(1)}, bf16[8,32,1152]{2,1,0:T(8,128)(2,1)S(1)}, u32[]{:S(2)}, u32[]{:S(2)}) collective-permute-start(bf16[8,32,1152]{2,1,0:T(8,128)(2,1)S(1)} %all_to_all.20.packed_ref.refs_0_), channel_id=1, source_target_pairs={{0,1},{1,0},{2,3},{3,2},{4,5},{5,4},{6,7},{7,6},{8,9},{9,8},{10,11... | collective-permute-start | bytes 1769480 | tf_op jit(solution)/shard_map/ppermute | solution.py:23
  47.2 37.0 %copy-start.1 = (bf16[8,32,1152]{2,1,0:T(8,128)(2,1)}, bf16[8,32,1152]{2,1,0:T(8,128)(2,1)S(1)}, u32[]{:S(2)}) copy-start(bf16[8,32,1152]{2,1,0:T(8,128)(2,1)S(1)} %collective-permute-done.1.refs_2_) | copy-start | bytes 1769476
  47.2 4.1 %collective-permute-start.2 = (bf16[8,32,1152]{2,1,0:T(8,128)(2,1)S(1)}, bf16[8,32,1152]{2,1,0:T(8,128)(2,1)S(1)}, u32[]{:S(2)}, u32[]{:S(2)}) collective-permute-start(bf16[8,32,1152]{2,1,0:T(8,128)(2,1)S(1)} %collective-permute-done.1.refs_2_), channel_id=1, source_target_pairs={{0,1},{1,0},{2,3},{3,2},{4,5},{5,4},{6,7},{7,6},{8,9},{9,8},{10,11... | collective-permute-start | bytes 1769480 | tf_op jit(solution)/shard_map/ppermute | solution.py:23
  47.2 15.9 %collective-permute-start.3 = (bf16[8,32,1024]{2,1,0:T(8,128)(2,1)S(1)}, bf16[8,32,1024]{2,1,0:T(8,128)(2,1)S(1)}, u32[]{:S(2)}, u32[]{:S(2)}) collective-permute-start(bf16[8,32,1024]{2,1,0:T(8,128)(2,1)S(1)} %all-to-all-done.1.refs_5_.refs_0_), channel_id=1, source_target_pairs={{0,2},{1,3},{2,0},{3,1},{4,6},{5,7},{6,4},{7,5},{8,10},{9,11},{10,... | collective-permute-start | bytes 1572872 | tf_op jit(solution)/shard_map/ppermute | solution.py:23
  51.0 12.4 %collective-permute-start.4 = (bf16[8,32,1024]{2,1,0:T(8,128)(2,1)S(1)}, bf16[8,32,1024]{2,1,0:T(8,128)(2,1)S(1)}, u32[]{:S(2)}, u32[]{:S(2)}) collective-permute-start(bf16[8,32,1024]{2,1,0:T(8,128)(2,1)S(1)} %all-to-all-done.1.refs_5_.refs_0_), channel_id=1, source_target_pairs={{0,1},{1,0},{2,3},{3,2},{4,5},{5,4},{6,7},{7,6},{8,9},{9,8},{10,11... | collective-permute-start | bytes 1572872 | tf_op jit(solution)/shard_map/ppermute | solution.py:23
  51.3 32.9 %copy-start.2 = (bf16[8,32,1152]{2,1,0:T(8,128)(2,1)}, bf16[8,32,1152]{2,1,0:T(8,128)(2,1)S(1)}, u32[]{:S(2)}) copy-start(bf16[8,32,1152]{2,1,0:T(8,128)(2,1)S(1)} %collective-permute-done.refs_1_) | copy-start | bytes 1769476
  51.3 32.9 %copy-start.3 = (bf16[8,32,1152]{2,1,0:T(8,128)(2,1)}, bf16[8,32,1152]{2,1,0:T(8,128)(2,1)S(1)}, u32[]{:S(2)}) copy-start(bf16[8,32,1152]{2,1,0:T(8,128)(2,1)S(1)} %collective-permute-done.2.refs_3_) | copy-start | bytes 1769476
  61.9 1.1 copy-start.17
  63.1 29.3 %copy-start.9 = (bf16[8,32,1024]{2,1,0:T(8,128)(2,1)}, bf16[8,32,1024]{2,1,0:T(8,128)(2,1)S(1)}, u32[]{:S(2)}) copy-start(bf16[8,32,1024]{2,1,0:T(8,128)(2,1)S(1)} %collective-permute-done.3.refs_2_) | copy-start | bytes 1572868
  63.1 1.9 %collective-permute-start.5 = (bf16[8,32,1024]{2,1,0:T(8,128)(2,1)S(1)}, bf16[8,32,1024]{2,1,0:T(8,128)(2,1)S(1)}, u32[]{:S(2)}, u32[]{:S(2)}) collective-permute-start(bf16[8,32,1024]{2,1,0:T(8,128)(2,1)S(1)} %collective-permute-done.3.refs_2_), channel_id=1, source_target_pairs={{0,1},{1,0},{2,3},{3,2},{4,5},{5,4},{6,7},{7,6},{8,9},{9,8},{10,11... | collective-permute-start | bytes 1572872 | tf_op jit(solution)/shard_map/ppermute | solution.py:23
  63.4 29.0 %copy-start.11 = (bf16[8,32,1024]{2,1,0:T(8,128)(2,1)}, bf16[8,32,1024]{2,1,0:T(8,128)(2,1)S(1)}, u32[]{:S(2)}) copy-start(bf16[8,32,1024]{2,1,0:T(8,128)(2,1)S(1)} %collective-permute-done.4.refs_1_) | copy-start | bytes 1572868
  65.0 27.4 %copy-start.13 = (bf16[8,32,1024]{2,1,0:T(8,128)(2,1)}, bf16[8,32,1024]{2,1,0:T(8,128)(2,1)S(1)}, u32[]{:S(2)}) copy-start(bf16[8,32,1024]{2,1,0:T(8,128)(2,1)S(1)} %collective-permute-done.5.refs_3_) | copy-start | bytes 1572868
  84.2 24.1 %copy-start.7 = (bf16[512,384]{1,0:T(8,128)(2,1)}, bf16[512,384]{1,0:T(8,128)(2,1)S(1)}, u32[]{:S(2)}) copy-start(bf16[512,384]{1,0:T(8,128)(2,1)S(1)} %get-tuple-element.27.grad_ref) | copy-start | bytes 1179652
  84.2 8.5 %collective-permute-start.6 = (bf16[2,256,1024]{2,1,0:T(8,128)(2,1)S(1)}, bf16[2,256,1024]{2,1,0:T(8,128)(2,1)S(1)}, u32[]{:S(2)}, u32[]{:S(2)}) collective-permute-start(bf16[2,256,1024]{2,1,0:T(8,128)(2,1)S(1)} %get-tuple-element.26), channel_id=1, source_target_pairs={{0,1},{1,0},{2,3},{3,2},{4,5},{5,4},{6,7},{7,6},{8,9},{9,8},{10,11... | collective-permute-start | bytes 3145736 | tf_op jit(solution)/shard_map/ppermute | solution.py:23
  92.4 31.6 %collective-permute-start.8 = (bf16[2,256,1024]{2,1,0:T(8,128)(2,1)S(1)}, bf16[2,256,1024]{2,1,0:T(8,128)(2,1)S(1)}, u32[]{:S(2)}, u32[]{:S(2)}) collective-permute-start(bf16[2,256,1024]{2,1,0:T(8,128)(2,1)S(1)} %back_odd.1.refs_2_), channel_id=1, source_target_pairs={{0,1},{1,0},{2,3},{3,2},{4,5},{5,4},{6,7},{7,6},{8,9},{9,8},{10,11... | collective-permute-start | bytes 3145736 | tf_op jit(solution)/shard_map/ppermute | solution.py:23
  93.3 14.2 %collective-permute-start.7 = (bf16[256,1024]{1,0:T(8,128)(2,1)S(1)}, bf16[256,1024]{1,0:T(8,128)(2,1)S(1)}, u32[]{:S(2)}, u32[]{:S(2)}) collective-permute-start(bf16[256,1024]{1,0:T(8,128)(2,1)S(1)} %mix_1.1.refs_0_), channel_id=1, source_target_pairs={{0,2},{1,3},{2,0},{3,1},{4,6},{5,7},{6,4},{7,5},{8,10},{9,11},{10,... | collective-permute-start | bytes 1572872 | tf_op jit(solution)/shard_map/ppermute | solution.py:23
  108.3 0.8 copy-start.4
  109.1 30.3 %all-to-all-start.2 = ((bf16[8,32,1024]{2,1,0:T(8,128)(2,1)}), bf16[8,32,1024]{2,1,0:T(8,128)(2,1)}, u32[]{:S(2)}, u32[]{:S(2)}) async-start(bf16[8,32,1024]{2,1,0:T(8,128)(2,1)} %bitcast.6), calls=%async_computation.2 | async-start | bytes 1048576 | tf_op jit(solution)/shard_map/all_to_all | solution.py:27
  114.8 1.0 copy-start.8
  115.8 9.4 %copy-start.5 = (bf16[256,1024]{1,0:T(8,128)(2,1)S(1)}, bf16[256,1024]{1,0:T(8,128)(2,1)}, u32[]{:S(2)}) copy-start(bf16[256,1024]{1,0:T(8,128)(2,1)} %copy-done.4) | copy-start | bytes 1572868
  115.8 9.4 %copy-start.10 = (bf16[8,32,1024]{2,1,0:T(8,128)(2,1)S(1)}, bf16[8,32,1024]{2,1,0:T(8,128)(2,1)}, u32[]{:S(2)}) copy-start(bf16[8,32,1024]{2,1,0:T(8,128)(2,1)} %copy-done.9) | copy-start | bytes 1572868
  115.8 9.4 %copy-start.12 = (bf16[8,32,1024]{2,1,0:T(8,128)(2,1)S(1)}, bf16[8,32,1024]{2,1,0:T(8,128)(2,1)}, u32[]{:S(2)}) copy-start(bf16[8,32,1024]{2,1,0:T(8,128)(2,1)} %copy-done.11) | copy-start | bytes 1572868
  115.8 9.4 %copy-start.14 = (bf16[8,32,1024]{2,1,0:T(8,128)(2,1)S(1)}, bf16[8,32,1024]{2,1,0:T(8,128)(2,1)}, u32[]{:S(2)}) copy-start(bf16[8,32,1024]{2,1,0:T(8,128)(2,1)} %copy-done.13) | copy-start | bytes 1572868
  115.8 9.4 %copy-start.18 = (bf16[256,3072]{1,0:T(8,128)(2,1)S(1)}, bf16[256,3072]{1,0:T(8,128)(2,1)}, u32[]{:S(2)}) copy-start(bf16[256,3072]{1,0:T(8,128)(2,1)} %copy-done.17) | copy-start | bytes 4718596
  124.0 21.1 %copy-start.6 = (bf16[256,3072]{1,0:T(8,128)(2,1)S(1)}, bf16[256,3072]{1,0:T(8,128)(2,1)}, u32[]{:S(2)}) copy-start(bf16[256,3072]{1,0:T(8,128)(2,1)} %get-tuple-element.30.grad_ref) | copy-start | bytes 4718596
  124.7 13.2 %collective-permute-start.9 = (bf16[256,1024]{1,0:T(8,128)(2,1)S(1)}, bf16[256,1024]{1,0:T(8,128)(2,1)S(1)}, u32[]{:S(2)}, u32[]{:S(2)}) collective-permute-start(bf16[256,1024]{1,0:T(8,128)(2,1)S(1)} %back_1.1.refs_4_), channel_id=1, source_target_pairs={{0,2},{1,3},{2,0},{3,1},{4,6},{5,7},{6,4},{7,5},{8,10},{9,11},{10,... | collective-permute-start | bytes 1572872 | tf_op jit(solution)/shard_map/ppermute | solution.py:23
  139.4 22.9 %all-to-all-start.3 = ((bf16[8,32,1024]{2,1,0:T(8,128)(2,1)}), bf16[8,32,1024]{2,1,0:T(8,128)(2,1)S(1)}, u32[]{:S(2)}, u32[]{:S(2)}) async-start(bf16[8,32,1024]{2,1,0:T(8,128)(2,1)} %bitcast.4), calls=%async_computation.3 | async-start | bytes 1048576 | tf_op jit(solution)/shard_map/all_to_all | solution.py:27
